TPU v7x, 32 devices: a whole 2x2x4 slice. The times are simulated.
32 devices in a mesh: ctx: 16 (over z, y, x), dp: 2 (over core).
Axes of the slice: x: 2, y: 2, z: 4, core: 2. Of those that a mesh axis runs over, the one named last changes fastest.
Arguments:
- queries: bfloat16 [2048, 2048], P('ctx', 'dp'), may hold values from -192 to 192
- keys: bfloat16 [2048, 128], P('ctx'), may hold values from -32 to 32
- values: bfloat16 [2048, 128], P('ctx'), may hold values from -6 to 6
- out_grads: bfloat16 [2048, 2048], P('ctx', 'dp'), may hold values from -6 to 6
- doc_lengths: int32 [8], replicated, may hold values from 1 to 1152, 2048 in all
Outputs:
- query_grads: bfloat16 [2048, 2048], P('ctx', 'dp')
- key_grads: bfloat16 [2048, 128], P(('ctx', 'dp'))
- value_grads: bfloat16 [2048, 128], P(('ctx', 'dp'))
Inputs may be any that keep to these rules, and one draw needn't show every extreme that they name: `doc_lengths`: document lengths in order of position; they sum to 2048 and the longest document has exactly 1152 tokens.
All inputs are finite; a program needn't handle non-finite values.
Results may differ from a plain program's by a relative error of at most 0.023.
Values may be sent and summed in bfloat16 or wider, within the bound.
No kernel may reach another device: no remote copies, remote signals or barrier semaphores. Data moves between devices by JAX's collectives and lax.ppermute only.
A program may use at most 64 MiB of HBM per device.

v0:
```python
import functools
import math

import jax
import jax.numpy as jnp
from jax import lax
from jax.experimental import pallas as pl
from jax.experimental.pallas import tpu as pltpu
from jax.sharding import PartitionSpec as P

masked_value = -1e30

vmem = pl.BlockSpec(memory_space=pltpu.VMEM)
smem = pl.BlockSpec(memory_space=pltpu.SMEM)
hbm = pl.BlockSpec(memory_space=pltpu.HBM)


def row_position(ctx_index, start, ctx_count, rows, span_rows):
    low = ctx_index * span_rows + start
    high = (2 * ctx_count - 1 - ctx_index) * span_rows + start - span_rows
    return pl.multiple_of(jnp.where(start < span_rows, low, high), rows)


def span_first(half, ctx_count, span_rows):
    ctx_index = lax.axis_index("ctx")
    return (ctx_index if half == 0 else 2 * ctx_count - 1 - ctx_index) * span_rows


def prepare_kernel(
    ctx_count,
    tile,
    lengths_hbm,
    q_hbm,
    g_hbm,
    line_ref,
    stack_ref,
    flip_ref,
    starts_ref,
    tiles_ref,
    zero_ref,
    same_ref,
    raw_ref,
    lengths_ref,
    sems,
):
    tok_rows = q_hbm.shape[0]
    head_width = stack_ref.shape[3]
    cols = stack_ref.shape[2]
    span_rows = tok_rows // 2
    copies = [
        pltpu.make_async_copy(source, raw_ref.at[slot], sems.at[slot])
        for slot, source in enumerate((q_hbm, g_hbm))
    ]
    for copy in copies:
        copy.start()
    lengths_copy = pltpu.make_async_copy(lengths_hbm, lengths_ref, sems.at[2])
    lengths_copy.start()
    same_ref[...] = line_ref[...]
    zero_ref[...] = jnp.zeros_like(zero_ref)
    lane = lax.broadcasted_iota(jnp.int32, tiles_ref.shape, 1)
    tiles = jnp.zeros(tiles_ref.shape, jnp.int32)
    lengths_copy.wait()
    for half in range(2):
        first = span_first(half, ctx_count, span_rows)
        query_pos = first + lax.rem(
            lax.broadcasted_iota(jnp.int32, (1, cols), 1), jnp.int32(span_rows)
        )
        doc_start = jnp.zeros((1, cols), jnp.int32)
        first_key = jnp.int32(0)
        end = jnp.int32(0)
        for doc in range(lengths_ref.shape[0]):
            end = end + lengths_ref[doc]
            doc_start = jnp.where(query_pos >= end, end, doc_start)
            first_key = jnp.where(first >= end, end, first_key)
        starts_ref[half] = doc_start
        count = (first + span_rows - first_key + tile - 1) // tile
        tiles = jnp.where(lane == half, count, tiles)
    tiles_ref[...] = tiles
    for slot, copy in enumerate(copies):
        copy.wait()
        for half in range(2):
            for head in range(q_hbm.shape[1] // head_width):
                stack_ref[half, slot, pl.ds(head * span_rows, span_rows), :] = raw_ref[
                    slot,
                    pl.ds(half * span_rows, span_rows),
                    pl.ds(head * head_width, head_width),
                ]
            flip_ref[half, slot] = stack_ref[half, slot].T


def line_steps(outer):
    return (0, 1, 3, 2) if outer == 4 else tuple(range(outer))


def send_order(outer):
    return (3, 1, 2) if outer == 4 else tuple(reversed(range(1, outer)))


def attend_kernel(
    ctx_count, dp_count, inner, tile, tiles_ref, starts_ref, stack_ref, flip_ref, _, *refs
):
    outer = ctx_count // inner
    piece_count = dp_count * inner
    kv_refs = refs[:piece_count]
    refs = refs[piece_count:]
    keys_ref, dlogits_ref, acc_ref = refs[:3]
    dkv_refs = refs[3 : piece_count + 3]
    values_ref, terms_ref, dweights_ref, tops_ref, counts_ref, sem = refs[piece_count + 3 :]
    cols, head_width = stack_ref.shape[2:]
    tok_rows = (keys_ref.shape[0] - tile) // ctx_count
    part_rows = tok_rows // dp_count
    span_rows = tok_rows // 2
    scale = head_width ** (-0.5)
    ctx_index = lax.axis_index("ctx")
    dp_index = lax.axis_index("dp")
    count_copy = pltpu.make_async_copy(tiles_ref, counts_ref, sem)
    count_copy.start()

    def blocks(steps):
        for piece in range(piece_count):
            for block, step in enumerate(steps):
                owner = ctx_index ^ (piece % inner) ^ (step * inner)
                first = (dp_index ^ (piece // inner)) * part_rows
                position = row_position(owner, first, ctx_count, part_rows, span_rows)
                row = 2 * block * part_rows
                yield (
                    piece,
                    pl.ds(row, part_rows),
                    pl.ds(row + part_rows, part_rows),
                    pl.ds(tile + position, part_rows),
                )

    dead = jnp.zeros((tile, head_width), jnp.bfloat16)
    keys_ref[:tile, :] = dead
    values_ref[:tile, :] = dead
    for piece, key_rows, value_rows, ordered in blocks(line_steps(outer)):
        keys_ref[ordered, :] = kv_refs[piece][key_rows, :]
        values_ref[ordered, :] = kv_refs[piece][value_rows, :]
    count_copy.wait()
    group = min(256, cols)
    groups = [slice(start, start + group) for start in range(0, cols, group)]

    for half in range(2):
        first = span_first(half, ctx_count, span_rows)
        query_pos = first + lax.rem(
            lax.broadcasted_iota(jnp.int32, (1, group), 1), jnp.int32(span_rows)
        )
        doc_start = starts_ref[half]
        count = counts_ref[0, half]

        def tile_rows(index):
            position = first + span_rows - (index + 1) * tile
            rows = pl.ds(pl.multiple_of(tile + position, span_rows), tile)
            return position, rows, pl.ds(pl.multiple_of(index * tile, tile), tile)

        def sums_step(index, state):
            position, rows, slot = tile_rows(index)
            key_block, value_block = keys_ref[rows, :], values_ref[rows, :]
            all_logits = [
                jnp.dot(key_block, flip_ref[half, 0, :, lanes], preferred_element_type=jnp.float32)
                for lanes in groups
            ]
            all_dweights = [
                jnp.dot(
                    value_block, flip_ref[half, 1, :, lanes], preferred_element_type=jnp.float32
                )
                for lanes in groups
            ]
            following = []
            for lanes, logits, dweights, (top, total, mixed) in zip(
                groups, all_logits, all_dweights, state
            ):
                key_pos = lax.broadcasted_iota(jnp.int32, logits.shape, 0)
                live = (key_pos >= doc_start[:, lanes] - position) & (
                    key_pos <= query_pos - position
                )
                logits = jnp.where(live, logits * (scale * math.log2(math.e)), masked_value)
                new_top = jnp.maximum(top, jnp.max(logits, axis=0, keepdims=True))
                terms = jnp.exp2(logits - new_top)
                terms_ref[slot, lanes] = terms
                dweights_ref[slot, lanes] = dweights
                tops_ref[pl.ds(index, 1), lanes] = new_top
                decay = jnp.exp2(top - new_top)
                following.append(
                    (
                        new_top,
                        total * decay + jnp.sum(terms, axis=0, keepdims=True),
                        mixed * decay + jnp.sum(terms * dweights, axis=0, keepdims=True),
                    )
                )
            return tuple(following)

        zero = jnp.zeros((1, group), jnp.float32)
        empty = (jnp.full_like(zero, masked_value), zero, zero)
        sums = lax.fori_loop(0, count, sums_step, (empty,) * len(groups))
        top, total, mixed = (jnp.concatenate(part, axis=1) for part in zip(*sums))
        inverse = 1.0 / total
        delta = mixed * inverse

        def grads_step(index, carry):
            _, rows, slot = tile_rows(index)
            factor = jnp.exp2(tops_ref[pl.ds(index, 1), :] - top) * inverse
            weights = terms_ref[slot, :] * factor
            dlogits = (weights * (dweights_ref[slot, :] - delta)).astype(jnp.bfloat16)
            for lane_block in range(cols // head_width):
                dlogits_ref[half, lane_block, slot, :] = dlogits[
                    :, lane_block * head_width : (lane_block + 1) * head_width
                ]
            acc_ref[1, rows, :] += jnp.dot(
                weights.astype(jnp.bfloat16),
                stack_ref[half, 1],
                preferred_element_type=jnp.float32,
            )
            acc_ref[0, rows, :] += jnp.dot(
                dlogits, stack_ref[half, 0], preferred_element_type=jnp.float32
            )
            return carry

        lax.fori_loop(0, count, grads_step, 0)

    for piece, key_rows, value_rows, ordered in blocks(range(outer)):
        dkv_refs[piece][key_rows, :] = (scale * acc_ref[0, ordered, :]).astype(jnp.bfloat16)
        dkv_refs[piece][value_rows, :] = acc_ref[1, ordered, :].astype(jnp.bfloat16)


def query_kernel(
    ctx_count,
    tile,
    tiles_ref,
    keys_ref,
    dlogits_ref,
    passed_ref,
    dq_ref,
    same_ref,
    sum_ref,
    counts_ref,
    sem,
):
    tok_rows = dq_ref.shape[0]
    head_width = keys_ref.shape[1]
    span_rows = tok_rows // 2
    scale = head_width ** (-0.5)
    count_copy = pltpu.make_async_copy(tiles_ref, counts_ref, sem)
    count_copy.start()
    same_ref[...] = passed_ref[...]
    count_copy.wait()
    for half in range(2):
        end = span_first(half, ctx_count, span_rows) + span_rows
        sum_ref[...] = jnp.zeros_like(sum_ref)

        def query_step(index, carry):
            rows = pl.ds(pl.multiple_of(end - index * tile, span_rows), tile)
            slot = pl.ds(pl.multiple_of(index * tile, tile), tile)
            dlogits = jnp.concatenate(
                [dlogits_ref[half, block, slot, :] for block in range(dlogits_ref.shape[1])], axis=1
            )
            sum_ref[...] += jnp.dot(
                keys_ref[rows, :].T, dlogits, preferred_element_type=jnp.float32
            )
            return carry

        lax.fori_loop(0, counts_ref[0, half], query_step, 0)
        grads = (scale * sum_ref[...]).T.astype(jnp.bfloat16)
        for head in range(dq_ref.shape[1] // head_width):
            dq_ref[
                pl.ds(half * span_rows, span_rows), pl.ds(head * head_width, head_width)
            ] = grads[head * span_rows : (head + 1) * span_rows]


def prepare(ctx_count, tile, doc_lengths, queries, out_grads, head_width, line):
    tok_rows, width = queries.shape
    cols = width // head_width * (tok_rows // 2)
    unmoved = [
        pltpu.with_memory_space_constraint(argument, pltpu.HBM)
        for argument in (doc_lengths, queries, out_grads)
    ]
    return pl.pallas_call(
        functools.partial(prepare_kernel, ctx_count, tile),
        out_shape=(
            jax.ShapeDtypeStruct((2, 2, cols, head_width), jnp.bfloat16),
            jax.ShapeDtypeStruct((2, 2, head_width, cols), jnp.bfloat16),
            jax.ShapeDtypeStruct((2, 1, cols), jnp.int32),
            jax.ShapeDtypeStruct((8, 128), jnp.int32),
            jax.ShapeDtypeStruct((2, tile + ctx_count * tok_rows, head_width), jnp.float32),
            jax.ShapeDtypeStruct(line.shape, line.dtype),
        ),
        in_specs=[hbm, hbm, hbm, vmem],
        out_specs=[vmem] * 6,
        scratch_shapes=[
            pltpu.VMEM((2, tok_rows, width), jnp.bfloat16),
            pltpu.SMEM(doc_lengths.shape, jnp.int32),
            pltpu.SemaphoreType.DMA((3,)),
        ],
        compiler_params=pltpu.CompilerParams(vmem_limit_bytes=4 * 1024 * 1024),
    )(*unmoved, line)


def attend(ctx_count, dp_count, inner, tile, tiles, starts, stacked, flipped, zeros, pieces):
    cols, head_width = stacked.shape[2:]
    seq = dp_count * inner * pieces[0].shape[0] // 2
    slots = -(-seq // tile)
    results = pl.pallas_call(
        functools.partial(attend_kernel, ctx_count, dp_count, inner, tile),
        out_shape=[
            jax.ShapeDtypeStruct((tile + seq, head_width), jnp.bfloat16),
            jax.ShapeDtypeStruct(
                (2, cols // head_width, slots * tile, head_width), jnp.bfloat16
            ),
            jax.ShapeDtypeStruct(zeros.shape, zeros.dtype),
        ]
        + [jax.ShapeDtypeStruct(piece.shape, jnp.bfloat16) for piece in pieces],
        in_specs=[vmem] * (5 + len(pieces)),
        out_specs=[vmem] * (3 + len(pieces)),
        scratch_shapes=[
            pltpu.VMEM((tile + seq, head_width), jnp.bfloat16),
            pltpu.VMEM((slots * tile, cols), jnp.float32),
            pltpu.VMEM((slots * tile, cols), jnp.float32),
            pltpu.VMEM((slots, cols), jnp.float32),
            pltpu.SMEM((8, 128), jnp.int32),
            pltpu.SemaphoreType.DMA,
        ],
        input_output_aliases={4: 2},
        compiler_params=pltpu.CompilerParams(vmem_limit_bytes=32 * 1024 * 1024),
    )(tiles, starts, stacked, flipped, zeros, *pieces)
    return results[0], results[1], results[3:]


def query_side(ctx_count, tile, tiles, keys_ordered, dlogits, passed, tok_rows):
    head_width = keys_ordered.shape[1]
    cols = dlogits.shape[1] * head_width
    return pl.pallas_call(
        functools.partial(query_kernel, ctx_count, tile),
        out_shape=(
            jax.ShapeDtypeStruct(
                (tok_rows, cols // (tok_rows // 2) * head_width), jnp.bfloat16
            ),
            jax.ShapeDtypeStruct(passed.shape, passed.dtype),
        ),
        in_specs=[vmem] * 4,
        out_specs=(vmem, vmem),
        scratch_shapes=[
            pltpu.VMEM((head_width, cols), jnp.float32),
            pltpu.SMEM((8, 128), jnp.int32),
            pltpu.SemaphoreType.DMA,
        ],
        compiler_params=pltpu.CompilerParams(vmem_limit_bytes=8 * 1024 * 1024),
    )(tiles, keys_ordered, dlogits, passed)


def swap(value, axis, offset):
    pairs = [(index, index ^ offset) for index in range(lax.axis_size(axis))]
    return lax.ppermute(value, axis, pairs)


def total_of(terms):
    return sum(term.astype(jnp.float32) for term in terms).astype(jnp.bfloat16)


def body(queries, keys, values, out_grads, doc_lengths):
    ctx_count = lax.axis_size("ctx")
    dp_count = lax.axis_size("dp")
    inner = math.gcd(4, ctx_count)
    outer = ctx_count // inner
    tok_rows, head_width = keys.shape
    part_rows = tok_rows // dp_count
    tile = math.gcd(512, ctx_count * tok_rows)
    start = lax.axis_index("dp") * part_rows
    own_keys = lax.dynamic_slice_in_dim(keys, start, part_rows, 0)
    own_values = lax.dynamic_slice_in_dim(values, start, part_rows, 0)
    zero = jnp.zeros((), keys.dtype)
    own = jnp.where(
        lax.broadcasted_iota(jnp.int32, (2 * part_rows, head_width), 0) < part_rows,
        lax.pad(own_keys, zero, ((0, part_rows, 0), (0, 0, 0))),
        lax.pad(own_values, zero, ((part_rows, 0, 0), (0, 0, 0))),
    )
    line = jnp.concatenate(
        [own] + [swap(own, "ctx", step * inner) for step in line_steps(outer)[1:]], axis=0
    )
    plane = [line] + [swap(line, "ctx", offset) for offset in range(1, inner)]
    stacked, flipped, starts, tiles, zeros, plane[0] = prepare(
        ctx_count, tile, doc_lengths, queries, out_grads, head_width, line
    )
    pieces = plane + [
        swap(piece, "dp", offset) for offset in range(1, dp_count) for piece in plane
    ]
    keys_ordered, dlogits, parts = attend(
        ctx_count, dp_count, inner, tile, tiles, starts, stacked, flipped, zeros, pieces
    )
    plane_sums = [
        total_of(
            [parts[offset]]
            + [swap(parts[far * inner + offset], "dp", far) for far in range(1, dp_count)]
        )
        for offset in range(inner)
    ]
    query_grads, plane_sums[0] = query_side(
        ctx_count, tile, tiles, keys_ordered, dlogits, plane_sums[0], tok_rows
    )
    line_sum = total_of(
        [plane_sums[0]] + [swap(plane_sums[offset], "ctx", offset) for offset in reversed(range(1, inner))]
    )
    blocks = jnp.split(line_sum, outer, axis=0)
    kv_grads = total_of(
        [blocks[0]] + [swap(blocks[block], "ctx", block * inner) for block in send_order(outer)]
    )
    return (query_grads, kv_grads[:part_rows], kv_grads[part_rows:])


def solution(mesh):
    return jax.shard_map(
        body,
        mesh=mesh,
        in_specs=(P("ctx", "dp"), P("ctx", None), P("ctx", None), P("ctx", "dp"), P()),
        out_specs=(P("ctx", "dp"), P(("ctx", "dp"), None), P(("ctx", "dp"), None)),
        check_vma=False,
    )
```

profile of v0, /device:TPU:0, one launch (start us, length us, event | category | flops | bytes accessed | tf_op | source)
XLA Modules:
  0.0 44.9 jit_solution(1739792216308415146)
XLA Ops:
  0.6 0.7 %constant_dynamic-slice_fusion = (bf16[64,128]{1,0:T(8,128)(2,1)S(1)}, bf16[64,128]{1,0:T(8,128)(2,1)S(1)}) fusion(bf16[128,128]{1,0:T(8,128)(2,1)} %param.7, s32[]{:T(128)S(6)} %select_n.8, bf16[128,128]{1,0:T(8,128)(2,1)} %param.6), kind=kLoop, calls=%fused_computation.8 | loop fusion | bytes 65540 | tf_op jit(solution)/shard_map/dynamic_slice | solution.py:369
  1.5 4.1 %collective-permute-start.2 = (bf16[128,128]{1,0:T(8,128)(2,1)S(1)}, bf16[128,128]{1,0:T(8,128)(2,1)S(1)}, u32[]{:S(2)}, u32[]{:S(2)}) collective-permute-start(bf16[128,128]{1,0:T(8,128)(2,1)S(1)} %pad_select_fusion), channel_id=1, source_target_pairs={{0,16},{2,18},{4,20},{6,22},{8,24},{10,26},{12,28},{14,30},{16,0},... | collective-permute-start | bytes 98312 | tf_op jit(solution)/shard_map/ppermute | solution.py:352
  5.6 1.3 %collective-permute-start.1 = (bf16[128,128]{1,0:T(8,128)(2,1)S(1)}, bf16[128,128]{1,0:T(8,128)(2,1)S(1)}, u32[]{:S(2)}, u32[]{:S(2)}) collective-permute-start(bf16[128,128]{1,0:T(8,128)(2,1)S(1)} %pad_select_fusion), channel_id=1, source_target_pairs={{0,24},{2,26},{4,28},{6,30},{8,16},{10,18},{12,20},{14,22},{16,8},... | collective-permute-start | bytes 98312 | tf_op jit(solution)/shard_map/ppermute | solution.py:352
  7.2 0.7 %collective-permute-done.2 = bf16[128,128]{1,0:T(8,128)(2,1)S(1)} collective-permute-done((bf16[128,128]{1,0:T(8,128)(2,1)S(1)}, bf16[128,128]{1,0:T(8,128)(2,1)S(1)}, u32[]{:S(2)}, u32[]{:S(2)}) %collective-permute-start.2) | collective-permute-done | bytes 32800 | tf_op jit(solution)/shard_map/ppermute | solution.py:352
  7.8 3.5 %collective-permute-done.1 = bf16[128,128]{1,0:T(8,128)(2,1)S(1)} collective-permute-done((bf16[128,128]{1,0:T(8,128)(2,1)S(1)}, bf16[128,128]{1,0:T(8,128)(2,1)S(1)}, u32[]{:S(2)}, u32[]{:S(2)}) %collective-permute-start.1) | collective-permute-done | bytes 32800 | tf_op jit(solution)/shard_map/ppermute | solution.py:352
  11.3 2.5 %collective-permute-start.5 = (bf16[512,128]{1,0:T(8,128)(2,1)S(1)}, bf16[512,128]{1,0:T(8,128)(2,1)S(1)}, u32[]{:S(2)}, u32[]{:S(2)}) collective-permute-start(bf16[512,128]{1,0:T(8,128)(2,1)S(1)} %pad_maximum_fusion.line_ref), channel_id=1, source_target_pairs={{0,6},{2,4},{4,2},{6,0},{8,14},{10,12},{12,10},{14,8},{16,22},{18,... | collective-permute-start | bytes 393224 | tf_op jit(solution)/shard_map/ppermute | solution.py:352
  14.3 0.5 %collective-permute-start.3 = (bf16[512,128]{1,0:T(8,128)(2,1)S(1)}, bf16[512,128]{1,0:T(8,128)(2,1)S(1)}, u32[]{:S(2)}, u32[]{:S(2)}) collective-permute-start(bf16[512,128]{1,0:T(8,128)(2,1)S(1)} %pad_maximum_fusion.line_ref), channel_id=1, source_target_pairs={{0,2},{2,0},{4,6},{6,4},{8,10},{10,8},{12,14},{14,12},{16,18},{18,... | collective-permute-start | bytes 393224 | tf_op jit(solution)/shard_map/ppermute | solution.py:352
  14.9 1.3 %shard_map.76 = (bf16[2,2,512,128]{3,2,1,0:T(8,128)(2,1)S(1)}, bf16[2,2,128,512]{3,2,1,0:T(8,128)(2,1)S(1)}, s32[2,1,512]{2,1,0:T(1,128)S(1)}, s32[8,128]{1,0:T(...) custom-call(s32[8]{0:T(128)} %lengths_hbm.1, bf16[128,1024]{1,0:T(8,128)(2,1)} %q_hbm.1, ...), custom_call_target="tpu_custom_call" | custom-call | tf_op jit(solution)/shard_map/pallas_call | solution.py:277
  16.2 2.4 %collective-permute-done.5.refs_3_ = bf16[512,128]{1,0:T(8,128)(2,1)S(1)} collective-permute-done((bf16[512,128]{1,0:T(8,128)(2,1)S(1)}, bf16[512,128]{1,0:T(8,128)(2,1)S(1)}, u32[]{:S(2)}, u32[]{:S(2)}) %collective-permute-start.5) | collective-permute-done | bytes 131104 | tf_op jit(solution)/shard_map/ppermute | solution.py:352
  18.7 0.8 %collective-permute-done.4.refs_2_ = bf16[512,128]{1,0:T(8,128)(2,1)S(1)} collective-permute-done((bf16[512,128]{1,0:T(8,128)(2,1)S(1)}, bf16[512,128]{1,0:T(8,128)(2,1)S(1)}, u32[]{:S(2)}, u32[]{:S(2)}) %collective-permute-start.4) | collective-permute-done | bytes 131104 | tf_op jit(solution)/shard_map/ppermute | solution.py:352
  19.4 0.5 %collective-permute-start.7 = (bf16[512,128]{1,0:T(8,128)(2,1)S(1)}, bf16[512,128]{1,0:T(8,128)(2,1)S(1)}, u32[]{:S(2)}, u32[]{:S(2)}) collective-permute-start(bf16[512,128]{1,0:T(8,128)(2,1)S(1)} %collective-permute-done.3.refs_1_), channel_id=1, source_target_pairs={{0,1},{1,0},{2,3},{3,2},{4,5},{5,4},{6,7},{7,6},{8,9},{9,8},{10,11... | collective-permute-start | bytes 393224 | tf_op jit(solution)/shard_map/ppermute | solution.py:352
  20.0 0.8 %collective-permute-done.8.refs_6_ = bf16[512,128]{1,0:T(8,128)(2,1)S(1)} collective-permute-done((bf16[512,128]{1,0:T(8,128)(2,1)S(1)}, bf16[512,128]{1,0:T(8,128)(2,1)S(1)}, u32[]{:S(2)}, u32[]{:S(2)}) %collective-permute-start.8) | collective-permute-done | bytes 131104 | tf_op jit(solution)/shard_map/ppermute | solution.py:352
  21.0 3.1 %shard_map.77 = (bf16[2560,128]{1,0:T(8,128)(2,1)S(1)}, bf16[2,4,2048,128]{3,2,1,0:T(8,128)(2,1)S(1)}, f32[2,2560,128]{2,1,0:T(8,128)S(1)}, bf16[512,128]{1,0:T(...) custom-call(s32[8,128]{1,0:T(8,128)S(1)} %get-tuple-element.21.tiles, ...), custom_call_target="tpu_custom_call", output_to_operand_aliasing={{2}: (4, {})} | custom-call | tf_op jit(solution)/shard_map/pallas_call | solution.py:302
  25.5 1.3 %collective-permute-start.12 = (bf16[512,128]{1,0:T(8,128)(2,1)S(1)}, bf16[512,128]{1,0:T(8,128)(2,1)S(1)}, u32[]{:S(2)}, u32[]{:S(2)}) collective-permute-start(bf16[512,128]{1,0:T(8,128)(2,1)S(1)} %add_convert_fusion.3), channel_id=1, source_target_pairs={{0,6},{2,4},{4,2},{6,0},{8,14},{10,12},{12,10},{14,8},{16,22},{18,... | collective-permute-start | bytes 393224 | tf_op jit(solution)/shard_map/ppermute | solution.py:352
  26.9 1.3 %collective-permute-start.14 = (bf16[512,128]{1,0:T(8,128)(2,1)S(1)}, bf16[512,128]{1,0:T(8,128)(2,1)S(1)}, u32[]{:S(2)}, u32[]{:S(2)}) collective-permute-start(bf16[512,128]{1,0:T(8,128)(2,1)S(1)} %add_convert_fusion.2), channel_id=1, source_target_pairs={{0,4},{2,6},{4,0},{6,2},{8,12},{10,14},{12,8},{14,10},{16,20},{18,... | collective-permute-start | bytes 393224 | tf_op jit(solution)/shard_map/ppermute | solution.py:352
  28.2 1.1 %collective-permute-start.16 = (bf16[512,128]{1,0:T(8,128)(2,1)S(1)}, bf16[512,128]{1,0:T(8,128)(2,1)S(1)}, u32[]{:S(2)}, u32[]{:S(2)}) collective-permute-start(bf16[512,128]{1,0:T(8,128)(2,1)S(1)} %add_convert_fusion.1), channel_id=1, source_target_pairs={{0,2},{2,0},{4,6},{6,4},{8,10},{10,8},{12,14},{14,12},{16,18},{18,... | collective-permute-start | bytes 393224 | tf_op jit(solution)/shard_map/ppermute | solution.py:352
  29.3 2.1 %shard_map.78 = (bf16[128,1024]{1,0:T(8,128)(2,1)}, bf16[512,128]{1,0:T(8,128)(2,1)S(1)}) custom-call(s32[8,128]{1,0:T(8,128)S(1)} %get-tuple-element.21.tiles_ref, bf16[2560,128]{1,0:T(8,128)(2,1)S(1)} %get-tuple-element.27.keys_ref, bf16[2,4,2048,128]{3,2,1,0:T(8,128)(2,1)S(1)} %get-tuple-element.28.dlogits_ref, ...), custom_call_target="tpu_custom_call" | custom-call | tf_op jit(solution)/shard_map/pallas_call | solution.py:331
  31.4 1.4 %collective-permute-done.12 = bf16[512,128]{1,0:T(8,128)(2,1)S(1)} collective-permute-done((bf16[512,128]{1,0:T(8,128)(2,1)S(1)}, bf16[512,128]{1,0:T(8,128)(2,1)S(1)}, u32[]{:S(2)}, u32[]{:S(2)}) %collective-permute-start.12) | collective-permute-done | bytes 131104 | tf_op jit(solution)/shard_map/ppermute | solution.py:352
  32.8 2.2 %collective-permute-done.14 = bf16[512,128]{1,0:T(8,128)(2,1)S(1)} collective-permute-done((bf16[512,128]{1,0:T(8,128)(2,1)S(1)}, bf16[512,128]{1,0:T(8,128)(2,1)S(1)}, u32[]{:S(2)}, u32[]{:S(2)}) %collective-permute-start.14) | collective-permute-done | bytes 131104 | tf_op jit(solution)/shard_map/ppermute | solution.py:352
  35.1 4.3 %collective-permute-start.17 = (bf16[128,128]{1,0:T(8,128)(2,1)S(1)}, bf16[128,128]{1,0:T(8,128)(2,1)S(1)}, u32[]{:S(2)}, u32[]{:S(2)}) collective-permute-start(bf16[128,128]{1,0:T(8,128)(2,1)S(1)} %get-tuple-element.39), channel_id=1, source_target_pairs={{0,24},{2,26},{4,28},{6,30},{8,16},{10,18},{12,20},{14,22},{16,8},... | collective-permute-start | bytes 98312 | tf_op jit(solution)/shard_map/ppermute | solution.py:352
  39.4 0.6 %collective-permute-start.18 = (bf16[128,128]{1,0:T(8,128)(2,1)S(1)}, bf16[128,128]{1,0:T(8,128)(2,1)S(1)}, u32[]{:S(2)}, u32[]{:S(2)}) collective-permute-start(bf16[128,128]{1,0:T(8,128)(2,1)S(1)} %get-tuple-element.41), channel_id=1, source_target_pairs={{0,8},{2,10},{4,12},{6,14},{8,0},{10,2},{12,4},{14,6},{16,24},{18,... | collective-permute-start | bytes 98312 | tf_op jit(solution)/shard_map/ppermute | solution.py:352
  40.0 1.5 %collective-permute-done.17 = bf16[128,128]{1,0:T(8,128)(2,1)S(1)} collective-permute-done((bf16[128,128]{1,0:T(8,128)(2,1)S(1)}, bf16[128,128]{1,0:T(8,128)(2,1)S(1)}, u32[]{:S(2)}, u32[]{:S(2)}) %collective-permute-start.17) | collective-permute-done | bytes 32800 | tf_op jit(solution)/shard_map/ppermute | solution.py:352
  41.5 2.7 %collective-permute-done.19 = bf16[128,128]{1,0:T(8,128)(2,1)S(1)} collective-permute-done((bf16[128,128]{1,0:T(8,128)(2,1)S(1)}, bf16[128,128]{1,0:T(8,128)(2,1)S(1)}, u32[]{:S(2)}, u32[]{:S(2)}) %collective-permute-start.19) | collective-permute-done | bytes 32800 | tf_op jit(solution)/shard_map/ppermute | solution.py:352
  44.3 0.6 %fusion.1 = (bf16[64,128]{1,0:T(8,128)(2,1)}, bf16[64,128]{1,0:T(8,128)(2,1)}) fusion(bf16[128,128]{1,0:T(8,128)(2,1)S(1)} %add_convert_fusion.5), kind=kLoop, calls=%fused_computation.12 | loop fusion | bytes 65536 | tf_op jit(solution)/shard_map/slice | solution.py:406
  (31 shorter events, 2.8 us)
Async XLA Ops:
  1.5 6.3 %collective-permute-start.2 = (bf16[128,128]{1,0:T(8,128)(2,1)S(1)}, bf16[128,128]{1,0:T(8,128)(2,1)S(1)}, u32[]{:S(2)}, u32[]{:S(2)}) collective-permute-start(bf16[128,128]{1,0:T(8,128)(2,1)S(1)} %pad_select_fusion), channel_id=1, source_target_pairs={{0,16},{2,18},{4,20},{6,22},{8,24},{10,26},{12,28},{14,30},{16,0},... | collective-permute-start | bytes 98312 | tf_op jit(solution)/shard_map/ppermute | solution.py:352
  5.6 5.7 %collective-permute-start.1 = (bf16[128,128]{1,0:T(8,128)(2,1)S(1)}, bf16[128,128]{1,0:T(8,128)(2,1)S(1)}, u32[]{:S(2)}, u32[]{:S(2)}) collective-permute-start(bf16[128,128]{1,0:T(8,128)(2,1)S(1)} %pad_select_fusion), channel_id=1, source_target_pairs={{0,24},{2,26},{4,28},{6,30},{8,16},{10,18},{12,20},{14,22},{16,8},... | collective-permute-start | bytes 98312 | tf_op jit(solution)/shard_map/ppermute | solution.py:352
  6.9 4.4 %collective-permute-start = (bf16[128,128]{1,0:T(8,128)(2,1)S(1)}, bf16[128,128]{1,0:T(8,128)(2,1)S(1)}, u32[]{:S(2)}, u32[]{:S(2)}) collective-permute-start(bf16[128,128]{1,0:T(8,128)(2,1)S(1)} %pad_select_fusion), channel_id=1, source_target_pairs={{0,8},{2,10},{4,12},{6,14},{8,0},{10,2},{12,4},{14,6},{16,24},{18,... | collective-permute-start | bytes 98312 | tf_op jit(solution)/shard_map/ppermute | solution.py:352
  11.3 7.3 %collective-permute-start.5 = (bf16[512,128]{1,0:T(8,128)(2,1)S(1)}, bf16[512,128]{1,0:T(8,128)(2,1)S(1)}, u32[]{:S(2)}, u32[]{:S(2)}) collective-permute-start(bf16[512,128]{1,0:T(8,128)(2,1)S(1)} %pad_maximum_fusion.line_ref), channel_id=1, source_target_pairs={{0,6},{2,4},{4,2},{6,0},{8,14},{10,12},{12,10},{14,8},{16,22},{18,... | collective-permute-start | bytes 393224 | tf_op jit(solution)/shard_map/ppermute | solution.py:352
  13.8 5.6 %collective-permute-start.4 = (bf16[512,128]{1,0:T(8,128)(2,1)S(1)}, bf16[512,128]{1,0:T(8,128)(2,1)S(1)}, u32[]{:S(2)}, u32[]{:S(2)}) collective-permute-start(bf16[512,128]{1,0:T(8,128)(2,1)S(1)} %pad_maximum_fusion.line_ref), channel_id=1, source_target_pairs={{0,4},{2,6},{4,0},{6,2},{8,12},{10,14},{12,8},{14,10},{16,20},{18,... | collective-permute-start | bytes 393224 | tf_op jit(solution)/shard_map/ppermute | solution.py:352
  14.3 5.1 %collective-permute-start.3 = (bf16[512,128]{1,0:T(8,128)(2,1)S(1)}, bf16[512,128]{1,0:T(8,128)(2,1)S(1)}, u32[]{:S(2)}, u32[]{:S(2)}) collective-permute-start(bf16[512,128]{1,0:T(8,128)(2,1)S(1)} %pad_maximum_fusion.line_ref), channel_id=1, source_target_pairs={{0,2},{2,0},{4,6},{6,4},{8,10},{10,8},{12,14},{14,12},{16,18},{18,... | collective-permute-start | bytes 393224 | tf_op jit(solution)/shard_map/ppermute | solution.py:352
  16.1 3.8 %collective-permute-start.6 = (bf16[512,128]{1,0:T(8,128)(2,1)S(1)}, bf16[512,128]{1,0:T(8,128)(2,1)S(1)}, u32[]{:S(2)}, u32[]{:S(2)}) collective-permute-start(bf16[512,128]{1,0:T(8,128)(2,1)S(1)} %get-tuple-element.26.refs_0_), channel_id=1, source_target_pairs={{0,1},{1,0},{2,3},{3,2},{4,5},{5,4},{6,7},{7,6},{8,9},{9,8},{10,11... | collective-permute-start | bytes 393224 | tf_op jit(solution)/shard_map/ppermute | solution.py:352
  18.7 1.3 %collective-permute-start.9 = (bf16[512,128]{1,0:T(8,128)(2,1)S(1)}, bf16[512,128]{1,0:T(8,128)(2,1)S(1)}, u32[]{:S(2)}, u32[]{:S(2)}) collective-permute-start(bf16[512,128]{1,0:T(8,128)(2,1)S(1)} %collective-permute-done.5.refs_3_), channel_id=1, source_target_pairs={{0,1},{1,0},{2,3},{3,2},{4,5},{5,4},{6,7},{7,6},{8,9},{9,8},{10,11... | collective-permute-start | bytes 393224 | tf_op jit(solution)/shard_map/ppermute | solution.py:352
  19.4 1.3 %collective-permute-start.8 = (bf16[512,128]{1,0:T(8,128)(2,1)S(1)}, bf16[512,128]{1,0:T(8,128)(2,1)S(1)}, u32[]{:S(2)}, u32[]{:S(2)}) collective-permute-start(bf16[512,128]{1,0:T(8,128)(2,1)S(1)} %collective-permute-done.4.refs_2_), channel_id=1, source_target_pairs={{0,1},{1,0},{2,3},{3,2},{4,5},{5,4},{6,7},{7,6},{8,9},{9,8},{10,11... | collective-permute-start | bytes 393224 | tf_op jit(solution)/shard_map/ppermute | solution.py:352
  19.4 1.5 %collective-permute-start.7 = (bf16[512,128]{1,0:T(8,128)(2,1)S(1)}, bf16[512,128]{1,0:T(8,128)(2,1)S(1)}, u32[]{:S(2)}, u32[]{:S(2)}) collective-permute-start(bf16[512,128]{1,0:T(8,128)(2,1)S(1)} %collective-permute-done.3.refs_1_), channel_id=1, source_target_pairs={{0,1},{1,0},{2,3},{3,2},{4,5},{5,4},{6,7},{7,6},{8,9},{9,8},{10,11... | collective-permute-start | bytes 393224 | tf_op jit(solution)/shard_map/ppermute | solution.py:352
  24.0 1.4 %collective-permute-start.11 = (bf16[512,128]{1,0:T(8,128)(2,1)S(1)}, bf16[512,128]{1,0:T(8,128)(2,1)S(1)}, u32[]{:S(2)}, u32[]{:S(2)}) collective-permute-start(bf16[512,128]{1,0:T(8,128)(2,1)S(1)} %get-tuple-element.34), channel_id=1, source_target_pairs={{0,1},{1,0},{2,3},{3,2},{4,5},{5,4},{6,7},{7,6},{8,9},{9,8},{10,11... | collective-permute-start | bytes 393224 | tf_op jit(solution)/shard_map/ppermute | solution.py:352
  24.4 4.8 %collective-permute-start.10 = (bf16[512,128]{1,0:T(8,128)(2,1)S(1)}, bf16[512,128]{1,0:T(8,128)(2,1)S(1)}, u32[]{:S(2)}, u32[]{:S(2)}) collective-permute-start(bf16[512,128]{1,0:T(8,128)(2,1)S(1)} %get-tuple-element.30), channel_id=1, source_target_pairs={{0,1},{1,0},{2,3},{3,2},{4,5},{5,4},{6,7},{7,6},{8,9},{9,8},{10,11... | collective-permute-start | bytes 393224 | tf_op jit(solution)/shard_map/ppermute | solution.py:352
  24.6 2.2 %collective-permute-start.13 = (bf16[512,128]{1,0:T(8,128)(2,1)S(1)}, bf16[512,128]{1,0:T(8,128)(2,1)S(1)}, u32[]{:S(2)}, u32[]{:S(2)}) collective-permute-start(bf16[512,128]{1,0:T(8,128)(2,1)S(1)} %get-tuple-element.36), channel_id=1, source_target_pairs={{0,1},{1,0},{2,3},{3,2},{4,5},{5,4},{6,7},{7,6},{8,9},{9,8},{10,11... | collective-permute-start | bytes 393224 | tf_op jit(solution)/shard_map/ppermute | solution.py:352
  24.9 3.2 %collective-permute-start.15 = (bf16[512,128]{1,0:T(8,128)(2,1)S(1)}, bf16[512,128]{1,0:T(8,128)(2,1)S(1)}, u32[]{:S(2)}, u32[]{:S(2)}) collective-permute-start(bf16[512,128]{1,0:T(8,128)(2,1)S(1)} %get-tuple-element.38), channel_id=1, source_target_pairs={{0,1},{1,0},{2,3},{3,2},{4,5},{5,4},{6,7},{7,6},{8,9},{9,8},{10,11... | collective-permute-start | bytes 393224 | tf_op jit(solution)/shard_map/ppermute | solution.py:352
  25.5 7.3 %collective-permute-start.12 = (bf16[512,128]{1,0:T(8,128)(2,1)S(1)}, bf16[512,128]{1,0:T(8,128)(2,1)S(1)}, u32[]{:S(2)}, u32[]{:S(2)}) collective-permute-start(bf16[512,128]{1,0:T(8,128)(2,1)S(1)} %add_convert_fusion.3), channel_id=1, source_target_pairs={{0,6},{2,4},{4,2},{6,0},{8,14},{10,12},{12,10},{14,8},{16,22},{18,... | collective-permute-start | bytes 393224 | tf_op jit(solution)/shard_map/ppermute | solution.py:352
  26.9 8.1 %collective-permute-start.14 = (bf16[512,128]{1,0:T(8,128)(2,1)S(1)}, bf16[512,128]{1,0:T(8,128)(2,1)S(1)}, u32[]{:S(2)}, u32[]{:S(2)}) collective-permute-start(bf16[512,128]{1,0:T(8,128)(2,1)S(1)} %add_convert_fusion.2), channel_id=1, source_target_pairs={{0,4},{2,6},{4,0},{6,2},{8,12},{10,14},{12,8},{14,10},{16,20},{18,... | collective-permute-start | bytes 393224 | tf_op jit(solution)/shard_map/ppermute | solution.py:352
  28.2 6.8 %collective-permute-start.16 = (bf16[512,128]{1,0:T(8,128)(2,1)S(1)}, bf16[512,128]{1,0:T(8,128)(2,1)S(1)}, u32[]{:S(2)}, u32[]{:S(2)}) collective-permute-start(bf16[512,128]{1,0:T(8,128)(2,1)S(1)} %add_convert_fusion.1), channel_id=1, source_target_pairs={{0,2},{2,0},{4,6},{6,4},{8,10},{10,8},{12,14},{14,12},{16,18},{18,... | collective-permute-start | bytes 393224 | tf_op jit(solution)/shard_map/ppermute | solution.py:352
  35.1 6.4 %collective-permute-start.17 = (bf16[128,128]{1,0:T(8,128)(2,1)S(1)}, bf16[128,128]{1,0:T(8,128)(2,1)S(1)}, u32[]{:S(2)}, u32[]{:S(2)}) collective-permute-start(bf16[128,128]{1,0:T(8,128)(2,1)S(1)} %get-tuple-element.39), channel_id=1, source_target_pairs={{0,24},{2,26},{4,28},{6,30},{8,16},{10,18},{12,20},{14,22},{16,8},... | collective-permute-start | bytes 98312 | tf_op jit(solution)/shard_map/ppermute | solution.py:352
  39.4 4.8 %collective-permute-start.19 = (bf16[128,128]{1,0:T(8,128)(2,1)S(1)}, bf16[128,128]{1,0:T(8,128)(2,1)S(1)}, u32[]{:S(2)}, u32[]{:S(2)}) collective-permute-start(bf16[128,128]{1,0:T(8,128)(2,1)S(1)} %get-tuple-element.40), channel_id=1, source_target_pairs={{0,16},{2,18},{4,20},{6,22},{8,24},{10,26},{12,28},{14,30},{16,0},... | collective-permute-start | bytes 98312 | tf_op jit(solution)/shard_map/ppermute | solution.py:352
  39.4 4.8 %collective-permute-start.18 = (bf16[128,128]{1,0:T(8,128)(2,1)S(1)}, bf16[128,128]{1,0:T(8,128)(2,1)S(1)}, u32[]{:S(2)}, u32[]{:S(2)}) collective-permute-start(bf16[128,128]{1,0:T(8,128)(2,1)S(1)} %get-tuple-element.41), channel_id=1, source_target_pairs={{0,8},{2,10},{4,12},{6,14},{8,0},{10,2},{12,4},{14,6},{16,24},{18,... | collective-permute-start | bytes 98312 | tf_op jit(solution)/shard_map/ppermute | solution.py:352
where the time goes:
time: 45.2 us; the launch traced here: 44.9 us
  starting transfers between devices  19.5 us (43%)
  waiting for transfers between devices  16.5 us (37%)
  Pallas kernels  6.37 us (14%)
  local copies, waits for them, and re-layouts  1.37 us (3%)
  between operations  0.74 us (2%)
    ppermute x20, starting transfers between devices, swap(): return lax.ppermute(value, axis, pairs)  19.5 us
    ppermute x20, waiting for transfers between devices, swap(): return lax.ppermute(value, axis, pairs)  16.5 us
    pallas_call x1, Pallas kernels, attend(): pl.pallas_call(functools.partial(attend_kernel, ctx_count, dp_count, inne...  3.06 us
    pallas_call x1, Pallas kernels, query_side(): pl.pallas_call(functools.partial(query_kernel, ctx_count, tile), out_shap...  2.05 us
    pallas_call x1, Pallas kernels, prepare(): pl.pallas_call(functools.partial(prepare_kernel, ctx_count, tile), out_sh...  1.26 us
  transfers between devices with their start and end apart: 20, of which 12 were waited for; matrix products, arithmetic and copies ran while one was open for 0% of the time, Pallas kernels for 7%

commit v1 on v0

--- a/solution.py
+++ b/solution.py
@@ -88,8 +88,24 @@
             flip_ref[half, slot] = stack_ref[half, slot].T
 
 
-def line_steps(outer):
-    return (0, 1, 3, 2) if outer == 4 else tuple(range(outer))
+def staged_moves(ctx_count, dp_count, inner, part_rows, ctx_index, dp_index):
+    for piece in range(dp_count * inner):
+        for block in range(ctx_count // inner):
+            owner = ctx_index ^ (piece % inner) ^ (block * inner)
+            start = (dp_index ^ (piece // inner)) * part_rows
+            yield piece, 2 * block * part_rows, owner, start
+
+
+def paired_moves(inner, part_rows, ctx_index, dp_index):
+    for side in range(2):
+        holder = dp_index ^ side
+        for offset in range(inner):
+            piece, near = side * inner + offset, ctx_index ^ offset
+            whole = near ^ jnp.where(holder == 1, 3 * inner, inner)
+            yield piece, 0, near, holder * part_rows
+            yield piece, 2 * part_rows, near ^ (2 * inner), holder * part_rows
+            yield piece, 4 * part_rows, whole, 0
+            yield piece, 6 * part_rows, whole, part_rows
 
 
 def send_order(outer):
@@ -97,9 +113,8 @@
 
 
 def attend_kernel(
-    ctx_count, dp_count, inner, tile, tiles_ref, starts_ref, stack_ref, flip_ref, _, *refs
+    ctx_count, dp_count, inner, tile, moves, tiles_ref, starts_ref, stack_ref, flip_ref, _, *refs
 ):
-    outer = ctx_count // inner
     piece_count = dp_count * inner
     kv_refs = refs[:piece_count]
     refs = refs[piece_count:]
@@ -116,24 +131,19 @@
     count_copy = pltpu.make_async_copy(tiles_ref, counts_ref, sem)
     count_copy.start()
 
-    def blocks(steps):
-        for piece in range(piece_count):
-            for block, step in enumerate(steps):
-                owner = ctx_index ^ (piece % inner) ^ (step * inner)
-                first = (dp_index ^ (piece // inner)) * part_rows
-                position = row_position(owner, first, ctx_count, part_rows, span_rows)
-                row = 2 * block * part_rows
-                yield (
-                    piece,
-                    pl.ds(row, part_rows),
-                    pl.ds(row + part_rows, part_rows),
-                    pl.ds(tile + position, part_rows),
-                )
+    def rows_of(row, owner, start):
+        position = row_position(owner, start, ctx_count, part_rows, span_rows)
+        return (
+            pl.ds(row, part_rows),
+            pl.ds(row + part_rows, part_rows),
+            pl.ds(tile + position, part_rows),
+        )
 
     dead = jnp.zeros((tile, head_width), jnp.bfloat16)
     keys_ref[:tile, :] = dead
     values_ref[:tile, :] = dead
-    for piece, key_rows, value_rows, ordered in blocks(line_steps(outer)):
+    for piece, *place in moves(ctx_index, dp_index):
+        key_rows, value_rows, ordered = rows_of(*place)
         keys_ref[ordered, :] = kv_refs[piece][key_rows, :]
         values_ref[ordered, :] = kv_refs[piece][value_rows, :]
     count_copy.wait()
@@ -153,7 +163,7 @@
             rows = pl.ds(pl.multiple_of(tile + position, span_rows), tile)
             return position, rows, pl.ds(pl.multiple_of(index * tile, tile), tile)
 
-        def sums_step(index, state):
+        def sums_step(index, state, diagonal=False):
             position, rows, slot = tile_rows(index)
             key_block, value_block = keys_ref[rows, :], values_ref[rows, :]
             all_logits = [
@@ -171,9 +181,9 @@
                 groups, all_logits, all_dweights, state
             ):
                 key_pos = lax.broadcasted_iota(jnp.int32, logits.shape, 0)
-                live = (key_pos >= doc_start[:, lanes] - position) & (
-                    key_pos <= query_pos - position
-                )
+                live = key_pos >= doc_start[:, lanes] - position
+                if diagonal:
+                    live = live & (key_pos <= query_pos - position)
                 logits = jnp.where(live, logits * (scale * math.log2(math.e)), masked_value)
                 new_top = jnp.maximum(top, jnp.max(logits, axis=0, keepdims=True))
                 terms = jnp.exp2(logits - new_top)
@@ -192,7 +202,8 @@
 
         zero = jnp.zeros((1, group), jnp.float32)
         empty = (jnp.full_like(zero, masked_value), zero, zero)
-        sums = lax.fori_loop(0, count, sums_step, (empty,) * len(groups))
+        sums = sums_step(0, (empty,) * len(groups), diagonal=True)
+        sums = lax.fori_loop(1, count, sums_step, sums)
         top, total, mixed = (jnp.concatenate(part, axis=1) for part in zip(*sums))
         inverse = 1.0 / total
         delta = mixed * inverse
@@ -218,7 +229,10 @@
 
         lax.fori_loop(0, count, grads_step, 0)
 
-    for piece, key_rows, value_rows, ordered in blocks(range(outer)):
+    for piece, *place in staged_moves(
+        ctx_count, dp_count, inner, part_rows, ctx_index, dp_index
+    ):
+        key_rows, value_rows, ordered = rows_of(*place)
         dkv_refs[piece][key_rows, :] = (scale * acc_ref[0, ordered, :]).astype(jnp.bfloat16)
         dkv_refs[piece][value_rows, :] = acc_ref[1, ordered, :].astype(jnp.bfloat16)
 
@@ -295,12 +309,12 @@
     )(*unmoved, line)
 
 
-def attend(ctx_count, dp_count, inner, tile, tiles, starts, stacked, flipped, zeros, pieces):
+def attend(ctx_count, dp_count, inner, tile, moves, tiles, starts, stacked, flipped, zeros, pieces):
     cols, head_width = stacked.shape[2:]
     seq = dp_count * inner * pieces[0].shape[0] // 2
     slots = -(-seq // tile)
     results = pl.pallas_call(
-        functools.partial(attend_kernel, ctx_count, dp_count, inner, tile),
+        functools.partial(attend_kernel, ctx_count, dp_count, inner, tile, moves),
         out_shape=[
             jax.ShapeDtypeStruct((tile + seq, head_width), jnp.bfloat16),
             jax.ShapeDtypeStruct(
@@ -356,14 +370,9 @@
     return sum(term.astype(jnp.float32) for term in terms).astype(jnp.bfloat16)
 
 
-def body(queries, keys, values, out_grads, doc_lengths):
-    ctx_count = lax.axis_size("ctx")
-    dp_count = lax.axis_size("dp")
-    inner = math.gcd(4, ctx_count)
-    outer = ctx_count // inner
-    tok_rows, head_width = keys.shape
-    part_rows = tok_rows // dp_count
-    tile = math.gcd(512, ctx_count * tok_rows)
+def staged_line(keys, values, inner, part_rows):
+    head_width = keys.shape[1]
+    outer = lax.axis_size("ctx") // inner
     start = lax.axis_index("dp") * part_rows
     own_keys = lax.dynamic_slice_in_dim(keys, start, part_rows, 0)
     own_values = lax.dynamic_slice_in_dim(values, start, part_rows, 0)
@@ -373,9 +382,43 @@
         lax.pad(own_keys, zero, ((0, part_rows, 0), (0, 0, 0))),
         lax.pad(own_values, zero, ((part_rows, 0, 0), (0, 0, 0))),
     )
-    line = jnp.concatenate(
-        [own] + [swap(own, "ctx", step * inner) for step in line_steps(outer)[1:]], axis=0
-    )
+    others = [swap(own, "ctx", step * inner) for step in range(1, outer)]
+    return jnp.concatenate([own] + others, axis=0)
+
+
+def paired_line(keys, values, inner, part_rows):
+    head_width = keys.shape[1]
+    halves = (2, 1, part_rows, head_width)
+    own = jnp.where(
+        lax.broadcasted_iota(jnp.int32, (2, 2, part_rows, head_width), 1) == 0,
+        keys.reshape(halves),
+        values.reshape(halves),
+    ).reshape(4 * part_rows, head_width)
+    rows = 2 * part_rows
+    own_half = lax.dynamic_slice_in_dim(own, lax.axis_index("dp") * rows, rows, 0)
+    pairs = [
+        (2 * ctx + dp, 2 * (ctx ^ ((3 if dp else 1) * inner)) + dp)
+        for ctx in range(lax.axis_size("ctx"))
+        for dp in range(2)
+    ]
+    whole = lax.ppermute(own, ("ctx", "dp"), pairs)
+    return jnp.concatenate([own_half, swap(own_half, "ctx", 2 * inner), whole], axis=0)
+
+
+def body(queries, keys, values, out_grads, doc_lengths):
+    ctx_count = lax.axis_size("ctx")
+    dp_count = lax.axis_size("dp")
+    inner = math.gcd(4, ctx_count)
+    outer = ctx_count // inner
+    tok_rows, head_width = keys.shape
+    part_rows = tok_rows // dp_count
+    tile = math.gcd(256, ctx_count * tok_rows)
+    if outer == 4 and dp_count == 2:
+        line = paired_line(keys, values, inner, part_rows)
+        moves = functools.partial(paired_moves, inner, part_rows)
+    else:
+        line = staged_line(keys, values, inner, part_rows)
+        moves = functools.partial(staged_moves, ctx_count, dp_count, inner, part_rows)
     plane = [line] + [swap(line, "ctx", offset) for offset in range(1, inner)]
     stacked, flipped, starts, tiles, zeros, plane[0] = prepare(
         ctx_count, tile, doc_lengths, queries, out_grads, head_width, line
@@ -384,7 +427,7 @@
         swap(piece, "dp", offset) for offset in range(1, dp_count) for piece in plane
     ]
     keys_ordered, dlogits, parts = attend(
-        ctx_count, dp_count, inner, tile, tiles, starts, stacked, flipped, zeros, pieces
+        ctx_count, dp_count, inner, tile, moves, tiles, starts, stacked, flipped, zeros, pieces
     )
     plane_sums = [
         total_of(

time: 45.2 us -> 44.5 us (0.985)
  Pallas kernels: 6.37 us -> 5.48 us
  other arithmetic: 0.35 us -> 1.14 us
  local copies, waits for them, and re-layouts: 1.37 us -> 0.79 us
    ppermute x0 -> x1, starting transfers between devices: none -> 3.09 us  [paired_line(): whole = lax.ppermute(own, ('ctx', 'dp'), pairs)]
    ppermute x20 -> x18, starting transfers between devices: 19.5 us -> 16.7 us  [swap(): return lax.ppermute(value, axis, pairs)]
    pallas_call x1, Pallas kernels: 3.06 us -> 2.26 us  [attend(): pl.pallas_call(functools.partial(attend_kernel, ctx_count, dp_count, inne...]
    select_n x1, other arithmetic: 0.09 us -> 0.87 us  [paired_line(): jnp.where(lax.broadcasted_iota(jnp.int32, (2, 2, part_rows, head_width),...]
    dynamic_slice x1, local copies, waits for them, and re-layouts: 0.74 us -> 0.01 us  [paired_line(): lax.dynamic_slice_in_dim(own, lax.axis_index('dp') * rows, rows, 0)]
    ppermute x20 -> x18, waiting for transfers between devices: 16.5 us -> 16.7 us  [swap(): return lax.ppermute(value, axis, pairs)]
  transfers between devices with their start and end apart: 20 -> 19, of which waited for: 12 -> 11; matrix products, arithmetic and copies ran while one was open for 0% -> 0% of each run, Pallas kernels for 7% -> 7%
where the time goes in v1:
time: 44.5 us
  starting transfers between devices  19.7 us (44%)
  waiting for transfers between devices  16.7 us (38%)
  Pallas kernels  5.48 us (12%)
  other arithmetic  1.14 us (3%)
  local copies, waits for them, and re-layouts  0.79 us (2%)
  between operations  0.73 us (2%)
    ppermute x18, starting transfers between devices, swap(): return lax.ppermute(value, axis, pairs)  16.7 us
    ppermute x18, waiting for transfers between devices, swap(): return lax.ppermute(value, axis, pairs)  16.7 us
    ppermute x1, starting transfers between devices, paired_line(): whole = lax.ppermute(own, ('ctx', 'dp'), pairs)  3.09 us
    pallas_call x1, Pallas kernels, attend(): pl.pallas_call(functools.partial(attend_kernel, ctx_count, dp_count, inne...  2.26 us
    pallas_call x1, Pallas kernels, query_side(): pl.pallas_call(functools.partial(query_kernel, ctx_count, tile), out_shap...  1.97 us
    pallas_call x1, Pallas kernels, prepare(): pl.pallas_call(functools.partial(prepare_kernel, ctx_count, tile), out_sh...  1.26 us
  transfers between devices with their start and end apart: 19, of which 11 were waited for; matrix products, arithmetic and copies ran while one was open for 0% of the time, Pallas kernels for 7%

profile of v1, /device:TPU:0, one launch (start us, length us, event | category | flops | bytes accessed | tf_op | source)
XLA Modules:
  0.0 44.5 jit_solution(7004324415566675679)
XLA Ops:
  0.8 0.9 %bitcast_select_fusion = bf16[256,128]{1,0:T(8,128)(2,1)S(1)} fusion(pred[256]{0:T(512)(128)(4,1)S(1)} %iota.12, bf16[2,64,128]{2,1,0:T(8,128)(2,1)} %bitcast.6, bf16[2,64,128]{2,1,0:T(8,128)(2,1)} %bitcast.7), kind=kLoop, calls=%fused_computation.6 | loop fusion | flops 32768 | bytes 131328 | tf_op jit(solution)/shard_map/jit(_where)/select_n | solution.py:392
  1.7 3.1 %collective-permute-start.1 = (bf16[256,128]{1,0:T(8,128)(2,1)S(1)}, bf16[256,128]{1,0:T(8,128)(2,1)S(1)}, u32[]{:S(2)}, u32[]{:S(2)}) collective-permute-start(bf16[256,128]{1,0:T(8,128)(2,1)S(1)} %bitcast_select_fusion), channel_id=1, source_target_pairs={{0,8},{1,25},{2,10},{3,27},{4,12},{5,29},{6,14},{7,31},{8,0},{9,17... | collective-permute-start | bytes 196616 | tf_op jit(solution)/shard_map/ppermute | solution.py:404
  4.8 2.6 %collective-permute-start = (bf16[128,128]{1,0:T(8,128)(2,1)S(1)}, bf16[128,128]{1,0:T(8,128)(2,1)S(1)}, u32[]{:S(2)}, u32[]{:S(2)}) collective-permute-start(bf16[128,128]{1,0:T(8,128)(2,1)S(1)} %constant_dynamic-slice_fusion), channel_id=1, source_target_pairs={{0,16},{2,18},{4,20},{6,22},{8,24},{10,26},{12,28},{14,30},{16,0},... | collective-permute-start | bytes 98312 | tf_op jit(solution)/shard_map/ppermute | solution.py:366
  7.4 2.4 %collective-permute-done = bf16[128,128]{1,0:T(8,128)(2,1)S(1)} collective-permute-done((bf16[128,128]{1,0:T(8,128)(2,1)S(1)}, bf16[128,128]{1,0:T(8,128)(2,1)S(1)}, u32[]{:S(2)}, u32[]{:S(2)}) %collective-permute-start) | collective-permute-done | bytes 32800 | tf_op jit(solution)/shard_map/ppermute | solution.py:366
  9.8 2.5 %collective-permute-start.4 = (bf16[512,128]{1,0:T(8,128)(2,1)S(1)}, bf16[512,128]{1,0:T(8,128)(2,1)S(1)}, u32[]{:S(2)}, u32[]{:S(2)}) collective-permute-start(bf16[512,128]{1,0:T(8,128)(2,1)S(1)} %pad_maximum_fusion.line_ref), channel_id=1, source_target_pairs={{0,6},{2,4},{4,2},{6,0},{8,14},{10,12},{12,10},{14,8},{16,22},{18,... | collective-permute-start | bytes 393224 | tf_op jit(solution)/shard_map/ppermute | solution.py:366
  12.3 0.5 %collective-permute-start.3 = (bf16[512,128]{1,0:T(8,128)(2,1)S(1)}, bf16[512,128]{1,0:T(8,128)(2,1)S(1)}, u32[]{:S(2)}, u32[]{:S(2)}) collective-permute-start(bf16[512,128]{1,0:T(8,128)(2,1)S(1)} %pad_maximum_fusion.line_ref), channel_id=1, source_target_pairs={{0,4},{2,6},{4,0},{6,2},{8,12},{10,14},{12,8},{14,10},{16,20},{18,... | collective-permute-start | bytes 393224 | tf_op jit(solution)/shard_map/ppermute | solution.py:366
  12.8 0.5 %collective-permute-start.2 = (bf16[512,128]{1,0:T(8,128)(2,1)S(1)}, bf16[512,128]{1,0:T(8,128)(2,1)S(1)}, u32[]{:S(2)}, u32[]{:S(2)}) collective-permute-start(bf16[512,128]{1,0:T(8,128)(2,1)S(1)} %pad_maximum_fusion.line_ref), channel_id=1, source_target_pairs={{0,2},{2,0},{4,6},{6,4},{8,10},{10,8},{12,14},{14,12},{16,18},{18,... | collective-permute-start | bytes 393224 | tf_op jit(solution)/shard_map/ppermute | solution.py:366
  13.3 1.3 %shard_map.76 = (bf16[2,2,512,128]{3,2,1,0:T(8,128)(2,1)S(1)}, bf16[2,2,128,512]{3,2,1,0:T(8,128)(2,1)S(1)}, s32[2,1,512]{2,1,0:T(1,128)S(1)}, s32[8,128]{1,0:T(...) custom-call(s32[8]{0:T(128)} %lengths_hbm.1, bf16[128,1024]{1,0:T(8,128)(2,1)} %q_hbm.1, ...), custom_call_target="tpu_custom_call" | custom-call | tf_op jit(solution)/shard_map/pallas_call | solution.py:291
  14.7 2.3 %collective-permute-done.4.refs_3_ = bf16[512,128]{1,0:T(8,128)(2,1)S(1)} collective-permute-done((bf16[512,128]{1,0:T(8,128)(2,1)S(1)}, bf16[512,128]{1,0:T(8,128)(2,1)S(1)}, u32[]{:S(2)}, u32[]{:S(2)}) %collective-permute-start.4) | collective-permute-done | bytes 131104 | tf_op jit(solution)/shard_map/ppermute | solution.py:366
  17.0 2.6 %collective-permute-done.3.refs_2_ = bf16[512,128]{1,0:T(8,128)(2,1)S(1)} collective-permute-done((bf16[512,128]{1,0:T(8,128)(2,1)S(1)}, bf16[512,128]{1,0:T(8,128)(2,1)S(1)}, u32[]{:S(2)}, u32[]{:S(2)}) %collective-permute-start.3) | collective-permute-done | bytes 131104 | tf_op jit(solution)/shard_map/ppermute | solution.py:366
  19.7 0.4 collective-permute-start.6
  20.1 0.8 %collective-permute-done.7.refs_6_ = bf16[512,128]{1,0:T(8,128)(2,1)S(1)} collective-permute-done((bf16[512,128]{1,0:T(8,128)(2,1)S(1)}, bf16[512,128]{1,0:T(8,128)(2,1)S(1)}, u32[]{:S(2)}, u32[]{:S(2)}) %collective-permute-start.7) | collective-permute-done | bytes 131104 | tf_op jit(solution)/shard_map/ppermute | solution.py:366
  21.1 2.3 %shard_map.77 = (bf16[2304,128]{1,0:T(8,128)(2,1)S(1)}, bf16[2,4,2048,128]{3,2,1,0:T(8,128)(2,1)S(1)}, f32[2,2304,128]{2,1,0:T(8,128)S(1)}, bf16[512,128]{1,0:T(...) custom-call(s32[8,128]{1,0:T(8,128)S(1)} %get-tuple-element.21.tiles, ...), custom_call_target="tpu_custom_call", output_to_operand_aliasing={{2}: (4, {})} | custom-call | tf_op jit(solution)/shard_map/pallas_call | solution.py:316
  24.8 1.8 %collective-permute-start.11 = (bf16[512,128]{1,0:T(8,128)(2,1)S(1)}, bf16[512,128]{1,0:T(8,128)(2,1)S(1)}, u32[]{:S(2)}, u32[]{:S(2)}) collective-permute-start(bf16[512,128]{1,0:T(8,128)(2,1)S(1)} %add_convert_fusion.3), channel_id=1, source_target_pairs={{0,6},{2,4},{4,2},{6,0},{8,14},{10,12},{12,10},{14,8},{16,22},{18,... | collective-permute-start | bytes 393224 | tf_op jit(solution)/shard_map/ppermute | solution.py:366
  26.7 1.3 %collective-permute-start.13 = (bf16[512,128]{1,0:T(8,128)(2,1)S(1)}, bf16[512,128]{1,0:T(8,128)(2,1)S(1)}, u32[]{:S(2)}, u32[]{:S(2)}) collective-permute-start(bf16[512,128]{1,0:T(8,128)(2,1)S(1)} %add_convert_fusion.2), channel_id=1, source_target_pairs={{0,4},{2,6},{4,0},{6,2},{8,12},{10,14},{12,8},{14,10},{16,20},{18,... | collective-permute-start | bytes 393224 | tf_op jit(solution)/shard_map/ppermute | solution.py:366
  28.0 0.6 %collective-permute-start.15 = (bf16[512,128]{1,0:T(8,128)(2,1)S(1)}, bf16[512,128]{1,0:T(8,128)(2,1)S(1)}, u32[]{:S(2)}, u32[]{:S(2)}) collective-permute-start(bf16[512,128]{1,0:T(8,128)(2,1)S(1)} %add_convert_fusion.1), channel_id=1, source_target_pairs={{0,2},{2,0},{4,6},{6,4},{8,10},{10,8},{12,14},{14,12},{16,18},{18,... | collective-permute-start | bytes 393224 | tf_op jit(solution)/shard_map/ppermute | solution.py:366
  28.6 2.0 %shard_map.78 = (bf16[128,1024]{1,0:T(8,128)(2,1)}, bf16[512,128]{1,0:T(8,128)(2,1)S(1)}) custom-call(s32[8,128]{1,0:T(8,128)S(1)} %get-tuple-element.21.tiles_ref, bf16[2304,128]{1,0:T(8,128)(2,1)S(1)} %get-tuple-element.27.keys_ref, bf16[2,4,2048,128]{3,2,1,0:T(8,128)(2,1)S(1)} %get-tuple-element.28.dlogits_ref, ...), custom_call_target="tpu_custom_call" | custom-call | tf_op jit(solution)/shard_map/pallas_call | solution.py:345
  30.6 1.5 %collective-permute-done.11 = bf16[512,128]{1,0:T(8,128)(2,1)S(1)} collective-permute-done((bf16[512,128]{1,0:T(8,128)(2,1)S(1)}, bf16[512,128]{1,0:T(8,128)(2,1)S(1)}, u32[]{:S(2)}, u32[]{:S(2)}) %collective-permute-start.11) | collective-permute-done | bytes 131104 | tf_op jit(solution)/shard_map/ppermute | solution.py:366
  32.1 2.2 %collective-permute-done.13 = bf16[512,128]{1,0:T(8,128)(2,1)S(1)} collective-permute-done((bf16[512,128]{1,0:T(8,128)(2,1)S(1)}, bf16[512,128]{1,0:T(8,128)(2,1)S(1)}, u32[]{:S(2)}, u32[]{:S(2)}) %collective-permute-start.13) | collective-permute-done | bytes 131104 | tf_op jit(solution)/shard_map/ppermute | solution.py:366
  34.5 4.6 %collective-permute-start.16 = (bf16[128,128]{1,0:T(8,128)(2,1)S(1)}, bf16[128,128]{1,0:T(8,128)(2,1)S(1)}, u32[]{:S(2)}, u32[]{:S(2)}) collective-permute-start(bf16[128,128]{1,0:T(8,128)(2,1)S(1)} %get-tuple-element.39), channel_id=1, source_target_pairs={{0,24},{2,26},{4,28},{6,30},{8,16},{10,18},{12,20},{14,22},{16,8},... | collective-permute-start | bytes 98312 | tf_op jit(solution)/shard_map/ppermute | solution.py:366
  39.1 0.6 %collective-permute-start.17 = (bf16[128,128]{1,0:T(8,128)(2,1)S(1)}, bf16[128,128]{1,0:T(8,128)(2,1)S(1)}, u32[]{:S(2)}, u32[]{:S(2)}) collective-permute-start(bf16[128,128]{1,0:T(8,128)(2,1)S(1)} %get-tuple-element.41), channel_id=1, source_target_pairs={{0,8},{2,10},{4,12},{6,14},{8,0},{10,2},{12,4},{14,6},{16,24},{18,... | collective-permute-start | bytes 98312 | tf_op jit(solution)/shard_map/ppermute | solution.py:366
  39.7 1.3 %collective-permute-done.16 = bf16[128,128]{1,0:T(8,128)(2,1)S(1)} collective-permute-done((bf16[128,128]{1,0:T(8,128)(2,1)S(1)}, bf16[128,128]{1,0:T(8,128)(2,1)S(1)}, u32[]{:S(2)}, u32[]{:S(2)}) %collective-permute-start.16) | collective-permute-done | bytes 32800 | tf_op jit(solution)/shard_map/ppermute | solution.py:366
  41.0 2.9 %collective-permute-done.18 = bf16[128,128]{1,0:T(8,128)(2,1)S(1)} collective-permute-done((bf16[128,128]{1,0:T(8,128)(2,1)S(1)}, bf16[128,128]{1,0:T(8,128)(2,1)S(1)}, u32[]{:S(2)}, u32[]{:S(2)}) %collective-permute-start.18) | collective-permute-done | bytes 32800 | tf_op jit(solution)/shard_map/ppermute | solution.py:366
  43.9 0.6 %fusion.1 = (bf16[64,128]{1,0:T(8,128)(2,1)}, bf16[64,128]{1,0:T(8,128)(2,1)}) fusion(bf16[128,128]{1,0:T(8,128)(2,1)S(1)} %add_convert_fusion.5), kind=kLoop, calls=%fused_computation.11 | loop fusion | bytes 65536 | tf_op jit(solution)/shard_map/slice | solution.py:449
  (31 shorter events, 2.3 us)
Async XLA Ops:
  1.7 8.1 %collective-permute-start.1 = (bf16[256,128]{1,0:T(8,128)(2,1)S(1)}, bf16[256,128]{1,0:T(8,128)(2,1)S(1)}, u32[]{:S(2)}, u32[]{:S(2)}) collective-permute-start(bf16[256,128]{1,0:T(8,128)(2,1)S(1)} %bitcast_select_fusion), channel_id=1, source_target_pairs={{0,8},{1,25},{2,10},{3,27},{4,12},{5,29},{6,14},{7,31},{8,0},{9,17... | collective-permute-start | bytes 196616 | tf_op jit(solution)/shard_map/ppermute | solution.py:404
  4.8 5.0 %collective-permute-start = (bf16[128,128]{1,0:T(8,128)(2,1)S(1)}, bf16[128,128]{1,0:T(8,128)(2,1)S(1)}, u32[]{:S(2)}, u32[]{:S(2)}) collective-permute-start(bf16[128,128]{1,0:T(8,128)(2,1)S(1)} %constant_dynamic-slice_fusion), channel_id=1, source_target_pairs={{0,16},{2,18},{4,20},{6,22},{8,24},{10,26},{12,28},{14,30},{16,0},... | collective-permute-start | bytes 98312 | tf_op jit(solution)/shard_map/ppermute | solution.py:366
  9.8 7.2 %collective-permute-start.4 = (bf16[512,128]{1,0:T(8,128)(2,1)S(1)}, bf16[512,128]{1,0:T(8,128)(2,1)S(1)}, u32[]{:S(2)}, u32[]{:S(2)}) collective-permute-start(bf16[512,128]{1,0:T(8,128)(2,1)S(1)} %pad_maximum_fusion.line_ref), channel_id=1, source_target_pairs={{0,6},{2,4},{4,2},{6,0},{8,14},{10,12},{12,10},{14,8},{16,22},{18,... | collective-permute-start | bytes 393224 | tf_op jit(solution)/shard_map/ppermute | solution.py:366
  12.3 7.3 %collective-permute-start.3 = (bf16[512,128]{1,0:T(8,128)(2,1)S(1)}, bf16[512,128]{1,0:T(8,128)(2,1)S(1)}, u32[]{:S(2)}, u32[]{:S(2)}) collective-permute-start(bf16[512,128]{1,0:T(8,128)(2,1)S(1)} %pad_maximum_fusion.line_ref), channel_id=1, source_target_pairs={{0,4},{2,6},{4,0},{6,2},{8,12},{10,14},{12,8},{14,10},{16,20},{18,... | collective-permute-start | bytes 393224 | tf_op jit(solution)/shard_map/ppermute | solution.py:366
  12.8 6.9 %collective-permute-start.2 = (bf16[512,128]{1,0:T(8,128)(2,1)S(1)}, bf16[512,128]{1,0:T(8,128)(2,1)S(1)}, u32[]{:S(2)}, u32[]{:S(2)}) collective-permute-start(bf16[512,128]{1,0:T(8,128)(2,1)S(1)} %pad_maximum_fusion.line_ref), channel_id=1, source_target_pairs={{0,2},{2,0},{4,6},{6,4},{8,10},{10,8},{12,14},{14,12},{16,18},{18,... | collective-permute-start | bytes 393224 | tf_op jit(solution)/shard_map/ppermute | solution.py:366
  14.6 5.5 %collective-permute-start.5 = (bf16[512,128]{1,0:T(8,128)(2,1)S(1)}, bf16[512,128]{1,0:T(8,128)(2,1)S(1)}, u32[]{:S(2)}, u32[]{:S(2)}) collective-permute-start(bf16[512,128]{1,0:T(8,128)(2,1)S(1)} %get-tuple-element.26.refs_0_), channel_id=1, source_target_pairs={{0,1},{1,0},{2,3},{3,2},{4,5},{5,4},{6,7},{7,6},{8,9},{9,8},{10,11... | collective-permute-start | bytes 393224 | tf_op jit(solution)/shard_map/ppermute | solution.py:366
  17.0 3.1 %collective-permute-start.8 = (bf16[512,128]{1,0:T(8,128)(2,1)S(1)}, bf16[512,128]{1,0:T(8,128)(2,1)S(1)}, u32[]{:S(2)}, u32[]{:S(2)}) collective-permute-start(bf16[512,128]{1,0:T(8,128)(2,1)S(1)} %collective-permute-done.4.refs_3_), channel_id=1, source_target_pairs={{0,1},{1,0},{2,3},{3,2},{4,5},{5,4},{6,7},{7,6},{8,9},{9,8},{10,11... | collective-permute-start | bytes 393224 | tf_op jit(solution)/shard_map/ppermute | solution.py:366
  19.6 1.3 %collective-permute-start.7 = (bf16[512,128]{1,0:T(8,128)(2,1)S(1)}, bf16[512,128]{1,0:T(8,128)(2,1)S(1)}, u32[]{:S(2)}, u32[]{:S(2)}) collective-permute-start(bf16[512,128]{1,0:T(8,128)(2,1)S(1)} %collective-permute-done.3.refs_2_), channel_id=1, source_target_pairs={{0,1},{1,0},{2,3},{3,2},{4,5},{5,4},{6,7},{7,6},{8,9},{9,8},{10,11... | collective-permute-start | bytes 393224 | tf_op jit(solution)/shard_map/ppermute | solution.py:366
  19.7 1.4 %collective-permute-start.6 = (bf16[512,128]{1,0:T(8,128)(2,1)S(1)}, bf16[512,128]{1,0:T(8,128)(2,1)S(1)}, u32[]{:S(2)}, u32[]{:S(2)}) collective-permute-start(bf16[512,128]{1,0:T(8,128)(2,1)S(1)} %collective-permute-done.2.refs_1_), channel_id=1, source_target_pairs={{0,1},{1,0},{2,3},{3,2},{4,5},{5,4},{6,7},{7,6},{8,9},{9,8},{10,11... | collective-permute-start | bytes 393224 | tf_op jit(solution)/shard_map/ppermute | solution.py:366
  23.4 1.4 %collective-permute-start.10 = (bf16[512,128]{1,0:T(8,128)(2,1)S(1)}, bf16[512,128]{1,0:T(8,128)(2,1)S(1)}, u32[]{:S(2)}, u32[]{:S(2)}) collective-permute-start(bf16[512,128]{1,0:T(8,128)(2,1)S(1)} %get-tuple-element.34), channel_id=1, source_target_pairs={{0,1},{1,0},{2,3},{3,2},{4,5},{5,4},{6,7},{7,6},{8,9},{9,8},{10,11... | collective-permute-start | bytes 393224 | tf_op jit(solution)/shard_map/ppermute | solution.py:366
  23.8 4.8 %collective-permute-start.9 = (bf16[512,128]{1,0:T(8,128)(2,1)S(1)}, bf16[512,128]{1,0:T(8,128)(2,1)S(1)}, u32[]{:S(2)}, u32[]{:S(2)}) collective-permute-start(bf16[512,128]{1,0:T(8,128)(2,1)S(1)} %get-tuple-element.30), channel_id=1, source_target_pairs={{0,1},{1,0},{2,3},{3,2},{4,5},{5,4},{6,7},{7,6},{8,9},{9,8},{10,11... | collective-permute-start | bytes 393224 | tf_op jit(solution)/shard_map/ppermute | solution.py:366
  23.9 2.7 %collective-permute-start.12 = (bf16[512,128]{1,0:T(8,128)(2,1)S(1)}, bf16[512,128]{1,0:T(8,128)(2,1)S(1)}, u32[]{:S(2)}, u32[]{:S(2)}) collective-permute-start(bf16[512,128]{1,0:T(8,128)(2,1)S(1)} %get-tuple-element.36), channel_id=1, source_target_pairs={{0,1},{1,0},{2,3},{3,2},{4,5},{5,4},{6,7},{7,6},{8,9},{9,8},{10,11... | collective-permute-start | bytes 393224 | tf_op jit(solution)/shard_map/ppermute | solution.py:366
  24.3 3.7 %collective-permute-start.14 = (bf16[512,128]{1,0:T(8,128)(2,1)S(1)}, bf16[512,128]{1,0:T(8,128)(2,1)S(1)}, u32[]{:S(2)}, u32[]{:S(2)}) collective-permute-start(bf16[512,128]{1,0:T(8,128)(2,1)S(1)} %get-tuple-element.38), channel_id=1, source_target_pairs={{0,1},{1,0},{2,3},{3,2},{4,5},{5,4},{6,7},{7,6},{8,9},{9,8},{10,11... | collective-permute-start | bytes 393224 | tf_op jit(solution)/shard_map/ppermute | solution.py:366
  24.8 7.3 %collective-permute-start.11 = (bf16[512,128]{1,0:T(8,128)(2,1)S(1)}, bf16[512,128]{1,0:T(8,128)(2,1)S(1)}, u32[]{:S(2)}, u32[]{:S(2)}) collective-permute-start(bf16[512,128]{1,0:T(8,128)(2,1)S(1)} %add_convert_fusion.3), channel_id=1, source_target_pairs={{0,6},{2,4},{4,2},{6,0},{8,14},{10,12},{12,10},{14,8},{16,22},{18,... | collective-permute-start | bytes 393224 | tf_op jit(solution)/shard_map/ppermute | solution.py:366
  26.7 7.6 %collective-permute-start.13 = (bf16[512,128]{1,0:T(8,128)(2,1)S(1)}, bf16[512,128]{1,0:T(8,128)(2,1)S(1)}, u32[]{:S(2)}, u32[]{:S(2)}) collective-permute-start(bf16[512,128]{1,0:T(8,128)(2,1)S(1)} %add_convert_fusion.2), channel_id=1, source_target_pairs={{0,4},{2,6},{4,0},{6,2},{8,12},{10,14},{12,8},{14,10},{16,20},{18,... | collective-permute-start | bytes 393224 | tf_op jit(solution)/shard_map/ppermute | solution.py:366
  28.0 6.4 %collective-permute-start.15 = (bf16[512,128]{1,0:T(8,128)(2,1)S(1)}, bf16[512,128]{1,0:T(8,128)(2,1)S(1)}, u32[]{:S(2)}, u32[]{:S(2)}) collective-permute-start(bf16[512,128]{1,0:T(8,128)(2,1)S(1)} %add_convert_fusion.1), channel_id=1, source_target_pairs={{0,2},{2,0},{4,6},{6,4},{8,10},{10,8},{12,14},{14,12},{16,18},{18,... | collective-permute-start | bytes 393224 | tf_op jit(solution)/shard_map/ppermute | solution.py:366
  34.5 6.5 %collective-permute-start.16 = (bf16[128,128]{1,0:T(8,128)(2,1)S(1)}, bf16[128,128]{1,0:T(8,128)(2,1)S(1)}, u32[]{:S(2)}, u32[]{:S(2)}) collective-permute-start(bf16[128,128]{1,0:T(8,128)(2,1)S(1)} %get-tuple-element.39), channel_id=1, source_target_pairs={{0,24},{2,26},{4,28},{6,30},{8,16},{10,18},{12,20},{14,22},{16,8},... | collective-permute-start | bytes 98312 | tf_op jit(solution)/shard_map/ppermute | solution.py:366
  39.1 4.8 %collective-permute-start.18 = (bf16[128,128]{1,0:T(8,128)(2,1)S(1)}, bf16[128,128]{1,0:T(8,128)(2,1)S(1)}, u32[]{:S(2)}, u32[]{:S(2)}) collective-permute-start(bf16[128,128]{1,0:T(8,128)(2,1)S(1)} %get-tuple-element.40), channel_id=1, source_target_pairs={{0,16},{2,18},{4,20},{6,22},{8,24},{10,26},{12,28},{14,30},{16,0},... | collective-permute-start | bytes 98312 | tf_op jit(solution)/shard_map/ppermute | solution.py:366
  39.1 4.8 %collective-permute-start.17 = (bf16[128,128]{1,0:T(8,128)(2,1)S(1)}, bf16[128,128]{1,0:T(8,128)(2,1)S(1)}, u32[]{:S(2)}, u32[]{:S(2)}) collective-permute-start(bf16[128,128]{1,0:T(8,128)(2,1)S(1)} %get-tuple-element.41), channel_id=1, source_target_pairs={{0,8},{2,10},{4,12},{6,14},{8,0},{10,2},{12,4},{14,6},{16,24},{18,... | collective-permute-start | bytes 98312 | tf_op jit(solution)/shard_map/ppermute | solution.py:366

commit v2 on v1

v2 whole, which is shorter than its diff:
```python
import functools
import math

import jax
import jax.numpy as jnp
from jax import lax
from jax.experimental import pallas as pl
from jax.experimental.pallas import tpu as pltpu
from jax.sharding import PartitionSpec as P

masked_value = -1e30

vmem = pl.BlockSpec(memory_space=pltpu.VMEM)
smem = pl.BlockSpec(memory_space=pltpu.SMEM)
hbm = pl.BlockSpec(memory_space=pltpu.HBM)


def span_first(half, ctx_count, span_rows):
    ctx_index = lax.axis_index("ctx")
    return (ctx_index if half == 0 else 2 * ctx_count - 1 - ctx_index) * span_rows


def prepare_kernel(
    ctx_count,
    lengths_hbm,
    q_hbm,
    g_hbm,
    line_ref,
    stack_ref,
    flip_ref,
    starts_ref,
    bounds_ref,
    same_ref,
    raw_ref,
    lengths_ref,
    sems,
):
    tok_rows = q_hbm.shape[0]
    head_width = stack_ref.shape[3]
    cols = stack_ref.shape[2]
    span_rows = tok_rows // 2
    copies = [
        pltpu.make_async_copy(source, raw_ref.at[slot], sems.at[slot])
        for slot, source in enumerate((q_hbm, g_hbm))
    ]
    for copy in copies:
        copy.start()
    lengths_copy = pltpu.make_async_copy(lengths_hbm, lengths_ref, sems.at[2])
    lengths_copy.start()
    same_ref[...] = line_ref[...]
    lane = lax.broadcasted_iota(jnp.int32, bounds_ref.shape, 1)
    bounds = jnp.zeros(bounds_ref.shape, jnp.int32)
    lengths_copy.wait()
    for half in range(2):
        first = span_first(half, ctx_count, span_rows)
        query_pos = first + lax.rem(
            lax.broadcasted_iota(jnp.int32, (1, cols), 1), jnp.int32(span_rows)
        )
        doc_start = jnp.zeros((1, cols), jnp.int32)
        first_key = jnp.int32(0)
        end = jnp.int32(0)
        for doc in range(lengths_ref.shape[0]):
            end = end + lengths_ref[doc]
            doc_start = jnp.where(query_pos >= end, end, doc_start)
            first_key = jnp.where(first >= end, end, first_key)
        starts_ref[half] = doc_start
        bounds = jnp.where(lane == half, first_key, bounds)
    bounds_ref[...] = bounds
    for slot, copy in enumerate(copies):
        copy.wait()
        for half in range(2):
            for head in range(q_hbm.shape[1] // head_width):
                stack_ref[half, slot, pl.ds(head * span_rows, span_rows), :] = raw_ref[
                    slot,
                    pl.ds(half * span_rows, span_rows),
                    pl.ds(head * head_width, head_width),
                ]
            flip_ref[half, slot] = stack_ref[half, slot].T


def staged_moves(ctx_count, dp_count, inner, part_rows, ctx_index, dp_index):
    for piece in range(dp_count * inner):
        for block in range(ctx_count // inner):
            owner = ctx_index ^ (piece % inner) ^ (block * inner)
            start = (dp_index ^ (piece // inner)) * part_rows
            yield piece, 2 * block * part_rows, owner, start


def paired_moves(inner, part_rows, ctx_index, dp_index):
    for side in range(2):
        holder = dp_index ^ side
        for offset in range(inner):
            piece, near = side * inner + offset, ctx_index ^ offset
            whole = near ^ jnp.where(holder == 1, 3 * inner, inner)
            yield piece, 0, near, holder * part_rows
            yield piece, 2 * part_rows, near ^ (2 * inner), holder * part_rows
            yield piece, 4 * part_rows, whole, 0
            yield piece, 6 * part_rows, whole, part_rows


def send_order(outer):
    return (3, 1, 2) if outer == 4 else tuple(reversed(range(1, outer)))


def tile_spans(ctx_count, inner, offset):
    lane = lax.axis_index("ctx") ^ offset
    lane = lane & (inner - 1)
    low = lane
    high = ctx_count + inner - 1 - lane
    return low, low, high


tile_halves = (0, 1, 1)


def tile_live(ctx_count, inner, offset, span_rows, bounds_ref):
    outer = ctx_count // inner
    ctx_index = lax.axis_index("ctx")
    alive = []
    for half, first in zip(tile_halves, tile_spans(ctx_count, inner, offset)):
        span = ctx_index if half == 0 else 2 * ctx_count - 1 - ctx_index
        steps = jnp.minimum(lax.div(span - first, jnp.int32(inner)), outer - 1)
        last = first + inner * steps
        alive.append((first <= span) & ((last + 1) * span_rows > bounds_ref[0, half]))
    return alive


def tile_row(ctx_count, inner, part_rows, span_rows, owner, start):
    outer = ctx_count // inner
    step = lax.div(owner, jnp.int32(inner))
    low = step * span_rows + start
    high = (2 * outer - 1 - step) * span_rows + start - span_rows
    return pl.ds(pl.multiple_of(jnp.where(start < span_rows, low, high), part_rows), part_rows)


def scores_kernel(
    ctx_count, dp_count, inner, offset, moves, bounds_vmem, starts_ref, flip_ref, *refs
):
    kv_refs = refs[:dp_count]
    passed_ref, keys_ref, terms_ref, dweights_ref, stats_ref, same_ref = refs[
        dp_count : dp_count + 6
    ]
    values_ref, bounds_ref, sem = refs[dp_count + 6 :]
    same_ref[...] = passed_ref[...]
    outer = ctx_count // inner
    cols = flip_ref.shape[3]
    head_width = keys_ref.shape[1]
    tile = keys_ref.shape[0] // 2
    span_rows = tile // outer
    part_rows = 2 * span_rows // dp_count
    scale = head_width ** (-0.5)
    bounds_copy = pltpu.make_async_copy(bounds_vmem, bounds_ref, sem)
    bounds_copy.start()
    for piece, row, owner, start in moves(lax.axis_index("ctx"), lax.axis_index("dp")):
        if piece % inner == offset:
            rows = tile_row(ctx_count, inner, part_rows, span_rows, owner, start)
            source = kv_refs[piece // inner]
            keys_ref[rows, :] = source[pl.ds(row, part_rows), :]
            values_ref[rows, :] = source[pl.ds(row + part_rows, part_rows), :]
    lane_groups = [
        slice(start, start + min(256, cols)) for start in range(0, cols, min(256, cols))
    ]
    stat_row = lax.broadcasted_iota(jnp.int32, stats_ref.shape, 0)
    stats_ref[...] = jnp.where(lax.rem(stat_row, 3) == 0, masked_value, 0.0)
    bounds_copy.wait()
    alive = tile_live(ctx_count, inner, offset, span_rows, bounds_ref)
    for kind, first in enumerate(tile_spans(ctx_count, inner, offset)):
        half = tile_halves[kind]
        rows = slice(tile, 2 * tile) if kind == 2 else slice(0, tile)

        @pl.when(alive[kind])
        def _():
            for lanes in lane_groups:
                logits = jnp.dot(
                    keys_ref[rows, :], flip_ref[half, 0, :, lanes],
                    preferred_element_type=jnp.float32,
                )
                dweights = jnp.dot(
                    values_ref[rows, :], flip_ref[half, 1, :, lanes],
                    preferred_element_type=jnp.float32,
                )
                group = logits.shape[1]
                query_pos = span_first(half, ctx_count, span_rows) + lax.rem(
                    lax.broadcasted_iota(jnp.int32, (1, group), 1), jnp.int32(span_rows)
                )
                key_row = lax.broadcasted_iota(jnp.int32, (span_rows, group), 0)
                masked = []
                for step in range(outer):
                    position = (first + inner * step) * span_rows
                    live = key_row >= starts_ref[half, :, lanes] - position
                    if kind != 1:
                        live = live & (key_row <= query_pos - position)
                    part = logits[step * span_rows : (step + 1) * span_rows]
                    masked.append(
                        jnp.where(live, part * (scale * math.log2(math.e)), masked_value)
                    )
                top = jnp.max(functools.reduce(jnp.maximum, masked), axis=0, keepdims=True)
                total, mixed = 0.0, 0.0
                for step in range(outer):
                    part_rows_here = slice(step * span_rows, (step + 1) * span_rows)
                    terms = jnp.exp2(masked[step] - top)
                    part = dweights[part_rows_here]
                    terms_ref[kind, part_rows_here, lanes] = terms
                    dweights_ref[kind, part_rows_here, lanes] = part
                    total = total + terms
                    mixed = mixed + terms * part
                stats_ref[3 * kind : 3 * kind + 1, lanes] = top
                stats_ref[3 * kind + 1 : 3 * kind + 2, lanes] = jnp.sum(
                    total, axis=0, keepdims=True
                )
                stats_ref[3 * kind + 2 : 3 * kind + 3, lanes] = jnp.sum(
                    mixed, axis=0, keepdims=True
                )


def grads_kernel(ctx_count, dp_count, inner, offset, bounds_vmem, stack_ref, _, *refs):
    stats_refs = refs[:inner]
    terms_ref, dweights_ref = refs[inner : inner + 2]
    dlogits_ref = refs[inner + 2]
    dkv_refs = refs[inner + 3 : inner + 3 + dp_count]
    acc_ref, bounds_ref, sem = refs[inner + 3 + dp_count :]
    outer = ctx_count // inner
    cols, head_width = stack_ref.shape[2:]
    tile = terms_ref.shape[1]
    span_rows = tile // outer
    part_rows = 2 * span_rows // dp_count
    scale = head_width ** (-0.5)
    bounds_copy = pltpu.make_async_copy(bounds_vmem, bounds_ref, sem)
    bounds_copy.start()
    acc_ref[...] = jnp.zeros_like(acc_ref)
    sums = []
    for half in range(2):
        tiles = [
            [ref[3 * kind + which : 3 * kind + which + 1, :] for which in range(3)]
            for ref in stats_refs
            for kind in range(3)
            if tile_halves[kind] == half
        ]
        top = functools.reduce(jnp.maximum, [tops for tops, _, _ in tiles])
        decays = [jnp.exp2(tops - top) for tops, _, _ in tiles]
        total = sum(decay * part for decay, (_, part, _) in zip(decays, tiles))
        mixed = sum(decay * part for decay, (_, _, part) in zip(decays, tiles))
        inverse = 1.0 / total
        sums.append((top, inverse, mixed * inverse))
    bounds_copy.wait()
    alive = tile_live(ctx_count, inner, offset, span_rows, bounds_ref)
    for kind, half in enumerate(tile_halves):
        rows = slice(tile, 2 * tile) if kind == 2 else slice(0, tile)
        top, inverse, delta = sums[half]

        @pl.when(alive[kind])
        def _():
            factor = jnp.exp2(stats_refs[offset][3 * kind : 3 * kind + 1, :] - top) * inverse
            weights = terms_ref[kind] * factor
            dlogits = (weights * (dweights_ref[kind] - delta)).astype(jnp.bfloat16)
            for lane_block in range(cols // head_width):
                dlogits_ref[kind, lane_block] = dlogits[
                    :, lane_block * head_width : (lane_block + 1) * head_width
                ]
            acc_ref[1, rows, :] += jnp.dot(
                weights.astype(jnp.bfloat16),
                stack_ref[half, 1],
                preferred_element_type=jnp.float32,
            )
            acc_ref[0, rows, :] += jnp.dot(
                dlogits, stack_ref[half, 0], preferred_element_type=jnp.float32
            )

    for piece, row, owner, start in staged_moves(
        ctx_count, dp_count, inner, part_rows, lax.axis_index("ctx"), lax.axis_index("dp")
    ):
        if piece % inner == offset:
            rows = tile_row(ctx_count, inner, part_rows, span_rows, owner, start)
            target = dkv_refs[piece // inner]
            target[pl.ds(row, part_rows), :] = (scale * acc_ref[0, rows, :]).astype(jnp.bfloat16)
            target[pl.ds(row + part_rows, part_rows), :] = acc_ref[1, rows, :].astype(jnp.bfloat16)


def query_kernel(ctx_count, inner, bounds_vmem, *refs):
    keys_refs = refs[:inner]
    dlogits_refs = refs[inner : 2 * inner]
    passed_ref, dq_ref, same_ref, sum_ref, bounds_ref, sem = refs[2 * inner :]
    head_width = keys_refs[0].shape[1]
    tile = keys_refs[0].shape[0] // 2
    span_rows = dq_ref.shape[0] // 2
    scale = head_width ** (-0.5)
    bounds_copy = pltpu.make_async_copy(bounds_vmem, bounds_ref, sem)
    bounds_copy.start()
    same_ref[...] = passed_ref[...]
    sum_ref[...] = jnp.zeros_like(sum_ref)
    bounds_copy.wait()
    for offset in range(inner):
        alive = tile_live(ctx_count, inner, offset, span_rows, bounds_ref)
        for kind, half in enumerate(tile_halves):

            @pl.when(alive[kind])
            def _():
                rows = slice(tile, 2 * tile) if kind == 2 else slice(0, tile)
                dlogits = jnp.concatenate(
                    [
                        dlogits_refs[offset][kind, lane_block]
                        for lane_block in range(dlogits_refs[offset].shape[1])
                    ],
                    axis=1,
                )
                sum_ref[half] += jnp.dot(
                    keys_refs[offset][rows, :].T, dlogits, preferred_element_type=jnp.float32
                )

    for half in range(2):
        grads = (scale * sum_ref[half]).T.astype(jnp.bfloat16)
        for head in range(dq_ref.shape[1] // head_width):
            dq_ref[
                pl.ds(half * span_rows, span_rows), pl.ds(head * head_width, head_width)
            ] = grads[head * span_rows : (head + 1) * span_rows]


def prepare(ctx_count, doc_lengths, queries, out_grads, head_width, line):
    tok_rows, width = queries.shape
    cols = width // head_width * (tok_rows // 2)
    unmoved = [
        pltpu.with_memory_space_constraint(argument, pltpu.HBM)
        for argument in (doc_lengths, queries, out_grads)
    ]
    return pl.pallas_call(
        functools.partial(prepare_kernel, ctx_count),
        out_shape=(
            jax.ShapeDtypeStruct((2, 2, cols, head_width), jnp.bfloat16),
            jax.ShapeDtypeStruct((2, 2, head_width, cols), jnp.bfloat16),
            jax.ShapeDtypeStruct((2, 1, cols), jnp.int32),
            jax.ShapeDtypeStruct((8, 128), jnp.int32),
            jax.ShapeDtypeStruct(line.shape, line.dtype),
        ),
        in_specs=[hbm, hbm, hbm, vmem],
        out_specs=[vmem] * 5,
        scratch_shapes=[
            pltpu.VMEM((2, tok_rows, width), jnp.bfloat16),
            pltpu.SMEM(doc_lengths.shape, jnp.int32),
            pltpu.SemaphoreType.DMA((3,)),
        ],
        compiler_params=pltpu.CompilerParams(vmem_limit_bytes=4 * 1024 * 1024),
    )(*unmoved, line)


def bounds_scratch():
    return [pltpu.SMEM((8, 128), jnp.int32), pltpu.SemaphoreType.DMA]


def scores(ctx_count, dp_count, inner, offset, moves, bounds, starts, flipped, pieces, passed):
    head_width, cols = flipped.shape[2:]
    tile = dp_count * pieces[0].shape[0] // 4
    return pl.pallas_call(
        functools.partial(scores_kernel, ctx_count, dp_count, inner, offset, moves),
        out_shape=(
            jax.ShapeDtypeStruct((2 * tile, head_width), jnp.bfloat16),
            jax.ShapeDtypeStruct((3, tile, cols), jnp.float32),
            jax.ShapeDtypeStruct((3, tile, cols), jnp.float32),
            jax.ShapeDtypeStruct((16, cols), jnp.float32),
            jax.ShapeDtypeStruct(passed.shape, passed.dtype),
        ),
        in_specs=[vmem] * (4 + dp_count),
        out_specs=[vmem] * 5,
        scratch_shapes=[pltpu.VMEM((2 * tile, head_width), jnp.bfloat16)] + bounds_scratch(),
        compiler_params=pltpu.CompilerParams(vmem_limit_bytes=12 * 1024 * 1024),
    )(bounds, starts, flipped, *pieces, passed)


def piece_grads(
    ctx_count, dp_count, inner, offset, bounds, stacked, after, stats, terms, dweights
):
    cols, head_width = stacked.shape[2:]
    tile = terms.shape[1]
    part = jax.ShapeDtypeStruct((4 * tile // dp_count, head_width), jnp.bfloat16)
    dlogits, *parts = pl.pallas_call(
        functools.partial(grads_kernel, ctx_count, dp_count, inner, offset),
        out_shape=[
            jax.ShapeDtypeStruct((3, cols // head_width, tile, head_width), jnp.bfloat16)
        ]
        + [part] * dp_count,
        in_specs=[vmem] * 2 + [pl.BlockSpec(memory_space=pl.ANY)] + [vmem] * (2 + inner),
        out_specs=[vmem] * (1 + dp_count),
        scratch_shapes=[pltpu.VMEM((2, 2 * tile, head_width), jnp.float32)] + bounds_scratch(),
        compiler_params=pltpu.CompilerParams(vmem_limit_bytes=12 * 1024 * 1024),
    )(bounds, stacked, after, *stats, terms, dweights)
    return dlogits, parts


def query_side(ctx_count, inner, bounds, keys_ordered, dlogits, passed, tok_rows):
    head_width = keys_ordered[0].shape[1]
    cols = dlogits[0].shape[1] * head_width
    return pl.pallas_call(
        functools.partial(query_kernel, ctx_count, inner),
        out_shape=(
            jax.ShapeDtypeStruct(
                (tok_rows, cols // (tok_rows // 2) * head_width), jnp.bfloat16
            ),
            jax.ShapeDtypeStruct(passed.shape, passed.dtype),
        ),
        in_specs=[vmem] * (2 + 2 * inner),
        out_specs=(vmem, vmem),
        scratch_shapes=[pltpu.VMEM((2, head_width, cols), jnp.float32)] + bounds_scratch(),
        compiler_params=pltpu.CompilerParams(vmem_limit_bytes=8 * 1024 * 1024),
    )(bounds, *keys_ordered, *dlogits, passed)


def swap(value, axis, offset):
    pairs = [(index, index ^ offset) for index in range(lax.axis_size(axis))]
    return lax.ppermute(value, axis, pairs)


def total_of(terms):
    return sum(term.astype(jnp.float32) for term in terms).astype(jnp.bfloat16)


def staged_line(keys, values, inner, part_rows, run_prepare):
    head_width = keys.shape[1]
    outer = lax.axis_size("ctx") // inner
    start = lax.axis_index("dp") * part_rows
    own_keys = lax.dynamic_slice_in_dim(keys, start, part_rows, 0)
    own_values = lax.dynamic_slice_in_dim(values, start, part_rows, 0)
    zero = jnp.zeros((), keys.dtype)
    own = jnp.where(
        lax.broadcasted_iota(jnp.int32, (2 * part_rows, head_width), 0) < part_rows,
        lax.pad(own_keys, zero, ((0, part_rows, 0), (0, 0, 0))),
        lax.pad(own_values, zero, ((part_rows, 0, 0), (0, 0, 0))),
    )
    others = [swap(own, "ctx", step * inner) for step in range(1, outer)]
    prepared, others[-1] = run_prepare(others[-1])
    return prepared, jnp.concatenate([own] + others, axis=0)


def paired_line(keys, values, inner, part_rows, run_prepare):
    head_width = keys.shape[1]
    halves = (2, 1, part_rows, head_width)
    own = jnp.where(
        lax.broadcasted_iota(jnp.int32, (2, 2, part_rows, head_width), 1) == 0,
        keys.reshape(halves),
        values.reshape(halves),
    ).reshape(4 * part_rows, head_width)
    rows = 2 * part_rows
    own_half = lax.dynamic_slice_in_dim(own, lax.axis_index("dp") * rows, rows, 0)
    pairs = [
        (2 * ctx + dp, 2 * (ctx ^ ((3 if dp else 1) * inner)) + dp)
        for ctx in range(lax.axis_size("ctx"))
        for dp in range(2)
    ]
    whole = lax.ppermute(own, ("ctx", "dp"), pairs)
    prepared, whole = run_prepare(whole)
    line = jnp.concatenate([own_half, swap(own_half, "ctx", 2 * inner), whole], axis=0)
    return prepared, line


def body(queries, keys, values, out_grads, doc_lengths):
    ctx_count = lax.axis_size("ctx")
    dp_count = lax.axis_size("dp")
    inner = math.gcd(4, ctx_count)
    outer = ctx_count // inner
    tok_rows, head_width = keys.shape
    part_rows = tok_rows // dp_count

    def run_prepare(held):
        *prepared, held = prepare(ctx_count, doc_lengths, queries, out_grads, head_width, held)
        return prepared, held

    if outer == 4 and dp_count == 2:
        make_line, moves = paired_line, functools.partial(paired_moves, inner, part_rows)
    else:
        make_line = staged_line
        moves = functools.partial(staged_moves, ctx_count, dp_count, inner, part_rows)
    (stacked, flipped, starts, bounds), line = make_line(
        keys, values, inner, part_rows, run_prepare
    )
    plane = [line] + [swap(line, "ctx", offset) for offset in range(1, inner)]
    scored = {}
    for offset in [0] + list(reversed(range(1, inner))):
        pieces = [plane[offset]] + [swap(plane[offset], "dp", far) for far in range(1, dp_count)]
        passed = plane[-1] if offset == 0 else bounds
        *scored[offset], passed = scores(
            ctx_count, dp_count, inner, offset, moves, bounds, starts, flipped, pieces, passed
        )
        if offset == 0:
            plane[-1] = passed
    stats = [scored[offset][3] for offset in range(inner)]
    dlogits, plane_sums = [None] * inner, [None] * inner
    for offset in reversed(range(inner)):
        after = plane_sums[offset + 2] if offset + 2 < inner else bounds
        dlogits[offset], parts = piece_grads(
            ctx_count, dp_count, inner, offset, bounds, stacked, after, stats, *scored[offset][1:3]
        )
        plane_sums[offset] = total_of(
            [parts[0]] + [swap(parts[far], "dp", far) for far in range(1, dp_count)]
        )
    query_grads, plane_sums[0] = query_side(
        ctx_count,
        inner,
        bounds,
        [scored[offset][0] for offset in range(inner)],
        dlogits,
        plane_sums[0],
        tok_rows,
    )
    line_sum = total_of(
        [plane_sums[0]] + [swap(plane_sums[offset], "ctx", offset) for offset in reversed(range(1, inner))]
    )
    blocks = jnp.split(line_sum, outer, axis=0)
    kv_grads = total_of(
        [blocks[0]] + [swap(blocks[block], "ctx", block * inner) for block in send_order(outer)]
    )
    return (query_grads, kv_grads[:part_rows], kv_grads[part_rows:])


def solution(mesh):
    return jax.shard_map(
        body,
        mesh=mesh,
        in_specs=(P("ctx", "dp"), P("ctx", None), P("ctx", None), P("ctx", "dp"), P()),
        out_specs=(P("ctx", "dp"), P(("ctx", "dp"), None), P(("ctx", "dp"), None)),
        check_vma=False,
    )
```

time: 44.5 us -> 51.8 us (1.16); the launches traced: 44.5 us -> 50.9 us
  Pallas kernels: 5.48 us -> 16.3 us
  waiting for transfers between devices: 16.7 us -> 11.3 us
  starting transfers between devices: 19.7 us -> 20.4 us
    pallas_call x3 -> x10, Pallas kernels: 5.48 us -> 16.3 us  [the longest x4 7.15 us: scores(): pl.pallas_call(functools.partial(scores_kernel, ctx_count, dp_count, inne...]
    ppermute x18, waiting for transfers between devices: 16.7 us -> 11.3 us  [swap(): return lax.ppermute(value, axis, pairs)]
    ppermute x18, starting transfers between devices: 16.7 us -> 17.3 us  [swap(): return lax.ppermute(value, axis, pairs)]
  transfers between devices with their start and end apart: 19 -> 19, of which waited for: 11 -> 7; matrix products, arithmetic and copies ran while one was open for 0% -> 0% of each run, Pallas kernels for 7% -> 26%
where the time goes in v2:
time: 51.8 us; the launch traced here: 50.9 us
  starting transfers between devices  20.4 us (39%)
  Pallas kernels  16.3 us (31%)
  waiting for transfers between devices  11.3 us (22%)
  other arithmetic  1.14 us (2%)
  between operations  0.83 us (2%)
  local copies, waits for them, and re-layouts  0.79 us (2%)
    ppermute x18, starting transfers between devices, swap(): return lax.ppermute(value, axis, pairs)  17.3 us
    ppermute x18, waiting for transfers between devices, swap(): return lax.ppermute(value, axis, pairs)  11.3 us
    pallas_call x4, Pallas kernels, scores(): pl.pallas_call(functools.partial(scores_kernel, ctx_count, dp_count, inne...  7.15 us
    pallas_call x4, Pallas kernels, piece_grads(): pl.pallas_call(functools.partial(grads_kernel, ctx_count, dp_count, inner...  4.91 us
    ppermute x1, starting transfers between devices, paired_line(): whole = lax.ppermute(own, ('ctx', 'dp'), pairs)  3.09 us
    pallas_call x1, Pallas kernels, query_side(): pl.pallas_call(functools.partial(query_kernel, ctx_count, inner), out_sha...  3 us
    pallas_call x1, Pallas kernels, prepare(): pl.pallas_call(functools.partial(prepare_kernel, ctx_count), out_shape=(j...  1.27 us
  transfers between devices with their start and end apart: 19, of which 7 were waited for; matrix products, arithmetic and copies ran while one was open for 0% of the time, Pallas kernels for 26%

profile of v2, /device:TPU:0, one launch (start us, length us, event | category | flops | bytes accessed | tf_op | source)
XLA Modules:
  0.0 50.9 jit_solution(4934370795512201608)
XLA Ops:
  0.8 0.9 %bitcast_select_fusion = bf16[256,128]{1,0:T(8,128)(2,1)S(1)} fusion(pred[256]{0:T(512)(128)(4,1)S(1)} %iota.12, bf16[2,64,128]{2,1,0:T(8,128)(2,1)} %bitcast.6, bf16[2,64,128]{2,1,0:T(8,128)(2,1)} %bitcast.7), kind=kLoop, calls=%fused_computation.6 | loop fusion | flops 32768 | bytes 131328 | tf_op jit(solution)/shard_map/jit(_where)/select_n | solution.py:435
  1.7 3.1 %collective-permute-start = (bf16[256,128]{1,0:T(8,128)(2,1)S(1)}, bf16[256,128]{1,0:T(8,128)(2,1)S(1)}, u32[]{:S(2)}, u32[]{:S(2)}) collective-permute-start(bf16[256,128]{1,0:T(8,128)(2,1)S(1)} %bitcast_select_fusion), channel_id=1, source_target_pairs={{0,8},{1,25},{2,10},{3,27},{4,12},{5,29},{6,14},{7,31},{8,0},{9,17... | collective-permute-start | bytes 196616 | tf_op jit(solution)/shard_map/ppermute | solution.py:447
  4.8 2.6 %collective-permute-start.1 = (bf16[128,128]{1,0:T(8,128)(2,1)S(1)}, bf16[128,128]{1,0:T(8,128)(2,1)S(1)}, u32[]{:S(2)}, u32[]{:S(2)}) collective-permute-start(bf16[128,128]{1,0:T(8,128)(2,1)S(1)} %constant_dynamic-slice_fusion), channel_id=1, source_target_pairs={{0,16},{2,18},{4,20},{6,22},{8,24},{10,26},{12,28},{14,30},{16,0},... | collective-permute-start | bytes 98312 | tf_op jit(solution)/shard_map/ppermute | solution.py:408
  7.4 1.3 %shard_map.76 = (bf16[2,2,512,128]{3,2,1,0:T(8,128)(2,1)S(1)}, bf16[2,2,128,512]{3,2,1,0:T(8,128)(2,1)S(1)}, s32[2,1,512]{2,1,0:T(1,128)S(1)}, s32[8,128]{1,0:T(8,128)S(1)}, bf16[256,128]{1,0:T(8,128)(2,1)S(1)}) custom-call(s32[8]{0:T(128)} %lengths_hbm.1, bf16[128,1024]{1,0:T(8,128)(2,1)} %q_hbm.1, bf16[128,1024]{1,0:T(8,128)(2,1)} %g_hbm.1, ...), custom_call_target="tpu_custom_call" | custom-call | tf_op jit(solution)/shard_map/pallas_call | solution.py:325
  8.6 1.1 %collective-permute-done.1 = bf16[128,128]{1,0:T(8,128)(2,1)S(1)} collective-permute-done((bf16[128,128]{1,0:T(8,128)(2,1)S(1)}, bf16[128,128]{1,0:T(8,128)(2,1)S(1)}, u32[]{:S(2)}, u32[]{:S(2)}) %collective-permute-start.1) | collective-permute-done | bytes 32800 | tf_op jit(solution)/shard_map/ppermute | solution.py:408
  9.8 2.5 %collective-permute-start.3 = (bf16[512,128]{1,0:T(8,128)(2,1)S(1)}, bf16[512,128]{1,0:T(8,128)(2,1)S(1)}, u32[]{:S(2)}, u32[]{:S(2)}) collective-permute-start(bf16[512,128]{1,0:T(8,128)(2,1)S(1)} %pad_maximum_fusion.refs_0_), channel_id=1, source_target_pairs={{0,6},{2,4},{4,2},{6,0},{8,14},{10,12},{12,10},{14,8},{16,22},{18,... | collective-permute-start | bytes 393224 | tf_op jit(solution)/shard_map/ppermute | solution.py:408
  13.7 3.3 %collective-permute-done.3.refs_2_ = bf16[512,128]{1,0:T(8,128)(2,1)S(1)} collective-permute-done((bf16[512,128]{1,0:T(8,128)(2,1)S(1)}, bf16[512,128]{1,0:T(8,128)(2,1)S(1)}, u32[]{:S(2)}, u32[]{:S(2)}) %collective-permute-start.3) | collective-permute-done | bytes 131104 | tf_op jit(solution)/shard_map/ppermute | solution.py:408
  17.0 1.5 %shard_map.77 = (bf16[512,128]{1,0:T(8,128)(2,1)S(1)}, f32[3,256,512]{2,1,0:T(8,128)S(1)}, f32[3,256,512]{2,1,0:T(8,128)S(1)}, f32[16,512]{1,0:T(8,128)S(1)}, bf16[512,128]{1,0:T(8,128)(2,1)S(1)}) custom-call(s32[8,128]{1,0:T(8,128)S(1)} %get-tuple-element.39.bounds_vmem.refs_2_._, s32[2,1,512]{2,1,0:T(1,128)S(1)} %get-tuple-element.40.starts_ref, ...), custom_call_target="tpu_custom_call" | custom-call | tf_op jit(solution)/shard_map/pallas_call | solution.py:352
  18.5 1.1 %collective-permute-done.4.refs_0_ = bf16[512,128]{1,0:T(8,128)(2,1)S(1)} collective-permute-done((bf16[512,128]{1,0:T(8,128)(2,1)S(1)}, bf16[512,128]{1,0:T(8,128)(2,1)S(1)}, u32[]{:S(2)}, u32[]{:S(2)}) %collective-permute-start.4) | collective-permute-done | bytes 131104 | tf_op jit(solution)/shard_map/ppermute | solution.py:408
  20.2 2.0 %shard_map.80 = (bf16[512,128]{1,0:T(8,128)(2,1)S(1)}, f32[3,256,512]{2,1,0:T(8,128)S(1)}, f32[3,256,512]{2,1,0:T(8,128)S(1)}, f32[16,512]{1,0:T(8,128)S(1)}, s32[8,128]{1,0:T(8,128)}) custom-call(s32[8,128]{1,0:T(8,128)S(1)} %get-tuple-element.39.bounds_vmem.refs_2_._, s32[2,1,512]{2,1,0:T(1,128)S(1)} %get-tuple-element.40.starts_ref, ...), custom_call_target="tpu_custom_call" | custom-call | tf_op jit(solution)/shard_map/pallas_call | solution.py:352
  22.2 1.6 %shard_map.78 = (bf16[512,128]{1,0:T(8,128)(2,1)S(1)}, f32[3,256,512]{2,1,0:T(8,128)S(1)}, f32[3,256,512]{2,1,0:T(8,128)S(1)}, f32[16,512]{1,0:T(8,128)S(1)}, s32[8,128]{1,0:T(8,128)}) custom-call(s32[8,128]{1,0:T(8,128)S(1)} %get-tuple-element.39.bounds_vmem.refs_2_._, s32[2,1,512]{2,1,0:T(1,128)S(1)} %get-tuple-element.40.starts_ref, ...), custom_call_target="tpu_custom_call" | custom-call | tf_op jit(solution)/shard_map/pallas_call | solution.py:352
  23.9 2.0 %shard_map.79 = (bf16[512,128]{1,0:T(8,128)(2,1)S(1)}, f32[3,256,512]{2,1,0:T(8,128)S(1)}, f32[3,256,512]{2,1,0:T(8,128)S(1)}, f32[16,512]{1,0:T(8,128)S(1)}, s32[8,128]{1,0:T(8,128)}) custom-call(s32[8,128]{1,0:T(8,128)S(1)} %get-tuple-element.39.bounds_vmem.refs_2_._, s32[2,1,512]{2,1,0:T(1,128)S(1)} %get-tuple-element.40.starts_ref, ...), custom_call_target="tpu_custom_call" | custom-call | tf_op jit(solution)/shard_map/pallas_call | solution.py:352
  25.9 1.3 %shard_map.83 = (bf16[3,4,256,128]{3,2,1,0:T(8,128)(2,1)S(1)}, bf16[512,128]{1,0:T(8,128)(2,1)S(1)}, bf16[512,128]{1,0:T(8,128)(2,1)S(1)}) custom-call(s32[8,128]{1,0:T(8,128)S(1)} %get-tuple-element.39.bounds_vmem.refs_2_._, bf16[2,2,512,128]{3,2,1,0:T(8,128)(2,1)S(1)} %get-tuple-element.48.stack_ref, s32[8,128]{1,0:T(8,128)S(1)} %get-tuple-element.39.bounds_vmem.refs_2_._, ...), custom_call_target="tpu_custom_call" | custom-call | tf_op jit(solution)/shard_map/pallas_call | solution.py:374
  27.3 1.3 %shard_map.81 = (bf16[3,4,256,128]{3,2,1,0:T(8,128)(2,1)S(1)}, bf16[512,128]{1,0:T(8,128)(2,1)S(1)}, bf16[512,128]{1,0:T(8,128)(2,1)S(1)}) custom-call(s32[8,128]{1,0:T(8,128)S(1)} %get-tuple-element.39.bounds_vmem.refs_2_._, bf16[2,2,512,128]{3,2,1,0:T(8,128)(2,1)S(1)} %get-tuple-element.48.stack_ref, s32[8,128]{1,0:T(8,128)S(1)} %get-tuple-element.39.bounds_vmem.refs_2_._, ...), custom_call_target="tpu_custom_call" | custom-call | tf_op jit(solution)/shard_map/pallas_call | solution.py:374
  29.2 3.5 %collective-permute-start.12 = (bf16[512,128]{1,0:T(8,128)(2,1)S(1)}, bf16[512,128]{1,0:T(8,128)(2,1)S(1)}, u32[]{:S(2)}, u32[]{:S(2)}) collective-permute-start(bf16[512,128]{1,0:T(8,128)(2,1)S(1)} %add_convert_fusion.3._), channel_id=1, source_target_pairs={{0,6},{2,4},{4,2},{6,0},{8,14},{10,12},{12,10},{14,8},{16,22},{18,... | collective-permute-start | bytes 393224 | tf_op jit(solution)/shard_map/ppermute | solution.py:408
  32.7 1.0 %shard_map.84 = (bf16[3,4,256,128]{3,2,1,0:T(8,128)(2,1)S(1)}, bf16[512,128]{1,0:T(8,128)(2,1)S(1)}, bf16[512,128]{1,0:T(8,128)(2,1)S(1)}) custom-call(s32[8,128]{1,0:T(8,128)S(1)} %get-tuple-element.39.bounds_vmem.refs_2_._, bf16[2,2,512,128]{3,2,1,0:T(8,128)(2,1)S(1)} %get-tuple-element.48.stack_ref, bf16[512,128]{1,0:T(8,128)(2,1)S(1)} %add_convert_fusion.3._, ...), custom_call_target="tpu_custom_call" | custom-call | tf_op jit(solution)/shard_map/pallas_call | solution.py:374
  34.2 1.3 %shard_map.82 = (bf16[3,4,256,128]{3,2,1,0:T(8,128)(2,1)S(1)}, bf16[512,128]{1,0:T(8,128)(2,1)S(1)}, bf16[512,128]{1,0:T(8,128)(2,1)S(1)}) custom-call(s32[8,128]{1,0:T(8,128)S(1)} %get-tuple-element.39.bounds_vmem.refs_2_._, bf16[2,2,512,128]{3,2,1,0:T(8,128)(2,1)S(1)} %get-tuple-element.48.stack_ref, bf16[512,128]{1,0:T(8,128)(2,1)S(1)} %add_convert_fusion.4._, ...), custom_call_target="tpu_custom_call" | custom-call | tf_op jit(solution)/shard_map/pallas_call | solution.py:374
  35.9 1.0 %collective-permute-start.15 = (bf16[512,128]{1,0:T(8,128)(2,1)S(1)}, bf16[512,128]{1,0:T(8,128)(2,1)S(1)}, u32[]{:S(2)}, u32[]{:S(2)}) collective-permute-start(bf16[512,128]{1,0:T(8,128)(2,1)S(1)} %add_convert_fusion.1), channel_id=1, source_target_pairs={{0,2},{2,0},{4,6},{6,4},{8,10},{10,8},{12,14},{14,12},{16,18},{18,... | collective-permute-start | bytes 393224 | tf_op jit(solution)/shard_map/ppermute | solution.py:408
  36.9 3.0 %shard_map.85 = (bf16[128,1024]{1,0:T(8,128)(2,1)}, bf16[512,128]{1,0:T(8,128)(2,1)S(1)}) custom-call(s32[8,128]{1,0:T(8,128)S(1)} %get-tuple-element.39.bounds_vmem.refs_2_._, bf16[512,128]{1,0:T(8,128)(2,1)S(1)} %get-tuple-element.43.refs_0_, bf16[512,128]{1,0:T(8,128)(2,1)S(1)} %get-tuple-element.44.refs_1_, ...), custom_call_target="tpu_custom_call" | custom-call | tf_op jit(solution)/shard_map/pallas_call | solution.py:391
  40.0 1.6 %collective-permute-done.15 = bf16[512,128]{1,0:T(8,128)(2,1)S(1)} collective-permute-done((bf16[512,128]{1,0:T(8,128)(2,1)S(1)}, bf16[512,128]{1,0:T(8,128)(2,1)S(1)}, u32[]{:S(2)}, u32[]{:S(2)}) %collective-permute-start.15) | collective-permute-done | bytes 131104 | tf_op jit(solution)/shard_map/ppermute | solution.py:408
  41.7 3.7 %collective-permute-start.16 = (bf16[128,128]{1,0:T(8,128)(2,1)S(1)}, bf16[128,128]{1,0:T(8,128)(2,1)S(1)}, u32[]{:S(2)}, u32[]{:S(2)}) collective-permute-start(bf16[128,128]{1,0:T(8,128)(2,1)S(1)} %get-tuple-element.75), channel_id=1, source_target_pairs={{0,24},{2,26},{4,28},{6,30},{8,16},{10,18},{12,20},{14,22},{16,8},... | collective-permute-start | bytes 98312 | tf_op jit(solution)/shard_map/ppermute | solution.py:408
  45.4 0.7 %collective-permute-start.17 = (bf16[128,128]{1,0:T(8,128)(2,1)S(1)}, bf16[128,128]{1,0:T(8,128)(2,1)S(1)}, u32[]{:S(2)}, u32[]{:S(2)}) collective-permute-start(bf16[128,128]{1,0:T(8,128)(2,1)S(1)} %get-tuple-element.77), channel_id=1, source_target_pairs={{0,8},{2,10},{4,12},{6,14},{8,0},{10,2},{12,4},{14,6},{16,24},{18,... | collective-permute-start | bytes 98312 | tf_op jit(solution)/shard_map/ppermute | solution.py:408
  46.1 1.3 %collective-permute-done.16 = bf16[128,128]{1,0:T(8,128)(2,1)S(1)} collective-permute-done((bf16[128,128]{1,0:T(8,128)(2,1)S(1)}, bf16[128,128]{1,0:T(8,128)(2,1)S(1)}, u32[]{:S(2)}, u32[]{:S(2)}) %collective-permute-start.16) | collective-permute-done | bytes 32800 | tf_op jit(solution)/shard_map/ppermute | solution.py:408
  47.5 2.7 %collective-permute-done.18 = bf16[128,128]{1,0:T(8,128)(2,1)S(1)} collective-permute-done((bf16[128,128]{1,0:T(8,128)(2,1)S(1)}, bf16[128,128]{1,0:T(8,128)(2,1)S(1)}, u32[]{:S(2)}, u32[]{:S(2)}) %collective-permute-start.18) | collective-permute-done | bytes 32800 | tf_op jit(solution)/shard_map/ppermute | solution.py:408
  (38 shorter events, 4.5 us)
Async XLA Ops:
  1.7 5.7 %collective-permute-start = (bf16[256,128]{1,0:T(8,128)(2,1)S(1)}, bf16[256,128]{1,0:T(8,128)(2,1)S(1)}, u32[]{:S(2)}, u32[]{:S(2)}) collective-permute-start(bf16[256,128]{1,0:T(8,128)(2,1)S(1)} %bitcast_select_fusion), channel_id=1, source_target_pairs={{0,8},{1,25},{2,10},{3,27},{4,12},{5,29},{6,14},{7,31},{8,0},{9,17... | collective-permute-start | bytes 196616 | tf_op jit(solution)/shard_map/ppermute | solution.py:447
  4.8 5.0 %collective-permute-start.1 = (bf16[128,128]{1,0:T(8,128)(2,1)S(1)}, bf16[128,128]{1,0:T(8,128)(2,1)S(1)}, u32[]{:S(2)}, u32[]{:S(2)}) collective-permute-start(bf16[128,128]{1,0:T(8,128)(2,1)S(1)} %constant_dynamic-slice_fusion), channel_id=1, source_target_pairs={{0,16},{2,18},{4,20},{6,22},{8,24},{10,26},{12,28},{14,30},{16,0},... | collective-permute-start | bytes 98312 | tf_op jit(solution)/shard_map/ppermute | solution.py:408
  9.8 7.2 %collective-permute-start.3 = (bf16[512,128]{1,0:T(8,128)(2,1)S(1)}, bf16[512,128]{1,0:T(8,128)(2,1)S(1)}, u32[]{:S(2)}, u32[]{:S(2)}) collective-permute-start(bf16[512,128]{1,0:T(8,128)(2,1)S(1)} %pad_maximum_fusion.refs_0_), channel_id=1, source_target_pairs={{0,6},{2,4},{4,2},{6,0},{8,14},{10,12},{12,10},{14,8},{16,22},{18,... | collective-permute-start | bytes 393224 | tf_op jit(solution)/shard_map/ppermute | solution.py:408
  12.3 4.7 %collective-permute-start.2 = (bf16[512,128]{1,0:T(8,128)(2,1)S(1)}, bf16[512,128]{1,0:T(8,128)(2,1)S(1)}, u32[]{:S(2)}, u32[]{:S(2)}) collective-permute-start(bf16[512,128]{1,0:T(8,128)(2,1)S(1)} %pad_maximum_fusion.refs_0_), channel_id=1, source_target_pairs={{0,1},{1,0},{2,3},{3,2},{4,5},{5,4},{6,7},{7,6},{8,9},{9,8},{10,11... | collective-permute-start | bytes 393224 | tf_op jit(solution)/shard_map/ppermute | solution.py:408
  12.6 7.0 %collective-permute-start.4 = (bf16[512,128]{1,0:T(8,128)(2,1)S(1)}, bf16[512,128]{1,0:T(8,128)(2,1)S(1)}, u32[]{:S(2)}, u32[]{:S(2)}) collective-permute-start(bf16[512,128]{1,0:T(8,128)(2,1)S(1)} %pad_maximum_fusion.refs_0_), channel_id=1, source_target_pairs={{0,2},{2,0},{4,6},{6,4},{8,10},{10,8},{12,14},{14,12},{16,18},{18,... | collective-permute-start | bytes 393224 | tf_op jit(solution)/shard_map/ppermute | solution.py:408
  13.1 6.5 %collective-permute-start.6 = (bf16[512,128]{1,0:T(8,128)(2,1)S(1)}, bf16[512,128]{1,0:T(8,128)(2,1)S(1)}, u32[]{:S(2)}, u32[]{:S(2)}) collective-permute-start(bf16[512,128]{1,0:T(8,128)(2,1)S(1)} %pad_maximum_fusion.refs_0_), channel_id=1, source_target_pairs={{0,4},{2,6},{4,0},{6,2},{8,12},{10,14},{12,8},{14,10},{16,20},{18,... | collective-permute-start | bytes 393224 | tf_op jit(solution)/shard_map/ppermute | solution.py:408
  18.5 1.7 %collective-permute-start.8 = (bf16[512,128]{1,0:T(8,128)(2,1)S(1)}, bf16[512,128]{1,0:T(8,128)(2,1)S(1)}, u32[]{:S(2)}, u32[]{:S(2)}) collective-permute-start(bf16[512,128]{1,0:T(8,128)(2,1)S(1)} %get-tuple-element.46.refs_0_), channel_id=1, source_target_pairs={{0,1},{1,0},{2,3},{3,2},{4,5},{5,4},{6,7},{7,6},{8,9},{9,8},{10,11... | collective-permute-start | bytes 393224 | tf_op jit(solution)/shard_map/ppermute | solution.py:408
  19.7 2.5 %collective-permute-start.5 = (bf16[512,128]{1,0:T(8,128)(2,1)S(1)}, bf16[512,128]{1,0:T(8,128)(2,1)S(1)}, u32[]{:S(2)}, u32[]{:S(2)}) collective-permute-start(bf16[512,128]{1,0:T(8,128)(2,1)S(1)} %collective-permute-done.4.refs_0_), channel_id=1, source_target_pairs={{0,1},{1,0},{2,3},{3,2},{4,5},{5,4},{6,7},{7,6},{8,9},{9,8},{10,11... | collective-permute-start | bytes 393224 | tf_op jit(solution)/shard_map/ppermute | solution.py:408
  19.7 4.2 %collective-permute-start.7 = (bf16[512,128]{1,0:T(8,128)(2,1)S(1)}, bf16[512,128]{1,0:T(8,128)(2,1)S(1)}, u32[]{:S(2)}, u32[]{:S(2)}) collective-permute-start(bf16[512,128]{1,0:T(8,128)(2,1)S(1)} %collective-permute-done.6.refs_0_), channel_id=1, source_target_pairs={{0,1},{1,0},{2,3},{3,2},{4,5},{5,4},{6,7},{7,6},{8,9},{9,8},{10,11... | collective-permute-start | bytes 393224 | tf_op jit(solution)/shard_map/ppermute | solution.py:408
  27.2 2.0 %collective-permute-start.10 = (bf16[512,128]{1,0:T(8,128)(2,1)S(1)}, bf16[512,128]{1,0:T(8,128)(2,1)S(1)}, u32[]{:S(2)}, u32[]{:S(2)}) collective-permute-start(bf16[512,128]{1,0:T(8,128)(2,1)S(1)} %get-tuple-element.63), channel_id=1, source_target_pairs={{0,1},{1,0},{2,3},{3,2},{4,5},{5,4},{6,7},{7,6},{8,9},{9,8},{10,11... | collective-permute-start | bytes 393224 | tf_op jit(solution)/shard_map/ppermute | solution.py:408
  28.6 5.2 %collective-permute-start.9 = (bf16[512,128]{1,0:T(8,128)(2,1)S(1)}, bf16[512,128]{1,0:T(8,128)(2,1)S(1)}, u32[]{:S(2)}, u32[]{:S(2)}) collective-permute-start(bf16[512,128]{1,0:T(8,128)(2,1)S(1)} %get-tuple-element.56), channel_id=1, source_target_pairs={{0,1},{1,0},{2,3},{3,2},{4,5},{5,4},{6,7},{7,6},{8,9},{9,8},{10,11... | collective-permute-start | bytes 393224 | tf_op jit(solution)/shard_map/ppermute | solution.py:408
  29.2 10.7 %collective-permute-start.12 = (bf16[512,128]{1,0:T(8,128)(2,1)S(1)}, bf16[512,128]{1,0:T(8,128)(2,1)S(1)}, u32[]{:S(2)}, u32[]{:S(2)}) collective-permute-start(bf16[512,128]{1,0:T(8,128)(2,1)S(1)} %add_convert_fusion.3._), channel_id=1, source_target_pairs={{0,6},{2,4},{4,2},{6,0},{8,14},{10,12},{12,10},{14,8},{16,22},{18,... | collective-permute-start | bytes 393224 | tf_op jit(solution)/shard_map/ppermute | solution.py:408
  33.7 2.1 %collective-permute-start.14 = (bf16[512,128]{1,0:T(8,128)(2,1)S(1)}, bf16[512,128]{1,0:T(8,128)(2,1)S(1)}, u32[]{:S(2)}, u32[]{:S(2)}) collective-permute-start(bf16[512,128]{1,0:T(8,128)(2,1)S(1)} %get-tuple-element.74), channel_id=1, source_target_pairs={{0,1},{1,0},{2,3},{3,2},{4,5},{5,4},{6,7},{7,6},{8,9},{9,8},{10,11... | collective-permute-start | bytes 393224 | tf_op jit(solution)/shard_map/ppermute | solution.py:408
  33.9 6.1 %collective-permute-start.13 = (bf16[512,128]{1,0:T(8,128)(2,1)S(1)}, bf16[512,128]{1,0:T(8,128)(2,1)S(1)}, u32[]{:S(2)}, u32[]{:S(2)}) collective-permute-start(bf16[512,128]{1,0:T(8,128)(2,1)S(1)} %add_convert_fusion.4._), channel_id=1, source_target_pairs={{0,4},{2,6},{4,0},{6,2},{8,12},{10,14},{12,8},{14,10},{16,20},{18,... | collective-permute-start | bytes 393224 | tf_op jit(solution)/shard_map/ppermute | solution.py:408
  35.5 1.4 %collective-permute-start.11 = (bf16[512,128]{1,0:T(8,128)(2,1)S(1)}, bf16[512,128]{1,0:T(8,128)(2,1)S(1)}, u32[]{:S(2)}, u32[]{:S(2)}) collective-permute-start(bf16[512,128]{1,0:T(8,128)(2,1)S(1)} %get-tuple-element.70), channel_id=1, source_target_pairs={{0,1},{1,0},{2,3},{3,2},{4,5},{5,4},{6,7},{7,6},{8,9},{9,8},{10,11... | collective-permute-start | bytes 393224 | tf_op jit(solution)/shard_map/ppermute | solution.py:408
  35.9 5.7 %collective-permute-start.15 = (bf16[512,128]{1,0:T(8,128)(2,1)S(1)}, bf16[512,128]{1,0:T(8,128)(2,1)S(1)}, u32[]{:S(2)}, u32[]{:S(2)}) collective-permute-start(bf16[512,128]{1,0:T(8,128)(2,1)S(1)} %add_convert_fusion.1), channel_id=1, source_target_pairs={{0,2},{2,0},{4,6},{6,4},{8,10},{10,8},{12,14},{14,12},{16,18},{18,... | collective-permute-start | bytes 393224 | tf_op jit(solution)/shard_map/ppermute | solution.py:408
  41.7 5.8 %collective-permute-start.16 = (bf16[128,128]{1,0:T(8,128)(2,1)S(1)}, bf16[128,128]{1,0:T(8,128)(2,1)S(1)}, u32[]{:S(2)}, u32[]{:S(2)}) collective-permute-start(bf16[128,128]{1,0:T(8,128)(2,1)S(1)} %get-tuple-element.75), channel_id=1, source_target_pairs={{0,24},{2,26},{4,28},{6,30},{8,16},{10,18},{12,20},{14,22},{16,8},... | collective-permute-start | bytes 98312 | tf_op jit(solution)/shard_map/ppermute | solution.py:408
  45.4 4.8 %collective-permute-start.18 = (bf16[128,128]{1,0:T(8,128)(2,1)S(1)}, bf16[128,128]{1,0:T(8,128)(2,1)S(1)}, u32[]{:S(2)}, u32[]{:S(2)}) collective-permute-start(bf16[128,128]{1,0:T(8,128)(2,1)S(1)} %get-tuple-element.76), channel_id=1, source_target_pairs={{0,16},{2,18},{4,20},{6,22},{8,24},{10,26},{12,28},{14,30},{16,0},... | collective-permute-start | bytes 98312 | tf_op jit(solution)/shard_map/ppermute | solution.py:408
  45.4 4.8 %collective-permute-start.17 = (bf16[128,128]{1,0:T(8,128)(2,1)S(1)}, bf16[128,128]{1,0:T(8,128)(2,1)S(1)}, u32[]{:S(2)}, u32[]{:S(2)}) collective-permute-start(bf16[128,128]{1,0:T(8,128)(2,1)S(1)} %get-tuple-element.77), channel_id=1, source_target_pairs={{0,8},{2,10},{4,12},{6,14},{8,0},{10,2},{12,4},{14,6},{16,24},{18,... | collective-permute-start | bytes 98312 | tf_op jit(solution)/shard_map/ppermute | solution.py:408

commit v3 on v1

--- a/solution.py
+++ b/solution.py
@@ -97,15 +97,31 @@
 
 
 def paired_moves(inner, part_rows, ctx_index, dp_index):
+    yield 0, 0, ctx_index, 0
+    yield 0, 2 * part_rows, ctx_index, part_rows
     for side in range(2):
         holder = dp_index ^ side
+        pieces = 1 + side * (inner + 1)
+        for offset in range(1, inner):
+            near = ctx_index ^ offset
+            yield pieces, 2 * (offset - 1) * part_rows, near, holder * part_rows
         for offset in range(inner):
-            piece, near = side * inner + offset, ctx_index ^ offset
+            piece, near = pieces + 1 + offset, ctx_index ^ offset
             whole = near ^ jnp.where(holder == 1, 3 * inner, inner)
-            yield piece, 0, near, holder * part_rows
-            yield piece, 2 * part_rows, near ^ (2 * inner), holder * part_rows
-            yield piece, 4 * part_rows, whole, 0
-            yield piece, 6 * part_rows, whole, part_rows
+            yield piece, 0, whole, 0
+            yield piece, 2 * part_rows, whole, part_rows
+            yield piece, 4 * part_rows, near ^ (2 * inner), holder * part_rows
+
+
+def part_moves(ctx_count, dp_count, inner, part_rows, ctx_index, dp_index):
+    for far in range(dp_count):
+        start = (dp_index ^ far) * part_rows
+        for offset in range(inner):
+            near = ctx_index ^ offset
+            yield far * (inner + 1), 2 * offset * part_rows, near, start
+            for block in range(1, ctx_count // inner):
+                piece = far * (inner + 1) + 1 + offset
+                yield piece, 2 * (block - 1) * part_rows, near ^ (block * inner), start
 
 
 def send_order(outer):
@@ -113,14 +129,25 @@
 
 
 def attend_kernel(
-    ctx_count, dp_count, inner, tile, moves, tiles_ref, starts_ref, stack_ref, flip_ref, _, *refs
+    ctx_count,
+    dp_count,
+    inner,
+    tile,
+    moves,
+    piece_count,
+    part_count,
+    tiles_ref,
+    starts_ref,
+    stack_ref,
+    flip_ref,
+    _,
+    *refs,
 ):
-    piece_count = dp_count * inner
     kv_refs = refs[:piece_count]
     refs = refs[piece_count:]
     keys_ref, dlogits_ref, acc_ref = refs[:3]
-    dkv_refs = refs[3 : piece_count + 3]
-    values_ref, terms_ref, dweights_ref, tops_ref, counts_ref, sem = refs[piece_count + 3 :]
+    dkv_refs = refs[3 : part_count + 3]
+    values_ref, terms_ref, dweights_ref, tops_ref, counts_ref, sem = refs[part_count + 3 :]
     cols, head_width = stack_ref.shape[2:]
     tok_rows = (keys_ref.shape[0] - tile) // ctx_count
     part_rows = tok_rows // dp_count
@@ -229,7 +256,7 @@
 
         lax.fori_loop(0, count, grads_step, 0)
 
-    for piece, *place in staged_moves(
+    for piece, *place in part_moves(
         ctx_count, dp_count, inner, part_rows, ctx_index, dp_index
     ):
         key_rows, value_rows, ordered = rows_of(*place)
@@ -309,12 +336,21 @@
     )(*unmoved, line)
 
 
-def attend(ctx_count, dp_count, inner, tile, moves, tiles, starts, stacked, flipped, zeros, pieces):
+def attend(
+    ctx_count, dp_count, inner, tile, moves, tiles, starts, stacked, flipped, zeros, pieces, seq
+):
     cols, head_width = stacked.shape[2:]
-    seq = dp_count * inner * pieces[0].shape[0] // 2
     slots = -(-seq // tile)
+    block_rows = 2 * seq // (ctx_count * dp_count)
+    away_rows = (ctx_count // inner - 1) * block_rows
+    parts = [
+        jax.ShapeDtypeStruct((rows, head_width), jnp.bfloat16)
+        for rows in ([inner * block_rows] + [away_rows] * inner) * dp_count
+    ]
     results = pl.pallas_call(
-        functools.partial(attend_kernel, ctx_count, dp_count, inner, tile, moves),
+        functools.partial(
+            attend_kernel, ctx_count, dp_count, inner, tile, moves, len(pieces), len(parts)
+        ),
         out_shape=[
             jax.ShapeDtypeStruct((tile + seq, head_width), jnp.bfloat16),
             jax.ShapeDtypeStruct(
@@ -322,9 +358,9 @@
             ),
             jax.ShapeDtypeStruct(zeros.shape, zeros.dtype),
         ]
-        + [jax.ShapeDtypeStruct(piece.shape, jnp.bfloat16) for piece in pieces],
+        + parts,
         in_specs=[vmem] * (5 + len(pieces)),
-        out_specs=[vmem] * (3 + len(pieces)),
+        out_specs=[vmem] * (3 + len(parts)),
         scratch_shapes=[
             pltpu.VMEM((tile + seq, head_width), jnp.bfloat16),
             pltpu.VMEM((slots * tile, cols), jnp.float32),
@@ -370,29 +406,35 @@
     return sum(term.astype(jnp.float32) for term in terms).astype(jnp.bfloat16)
 
 
-def staged_line(keys, values, inner, part_rows):
+def gather_staged(keys, values, inner, part_rows, run_prepare):
     head_width = keys.shape[1]
     outer = lax.axis_size("ctx") // inner
     start = lax.axis_index("dp") * part_rows
-    own_keys = lax.dynamic_slice_in_dim(keys, start, part_rows, 0)
-    own_values = lax.dynamic_slice_in_dim(values, start, part_rows, 0)
-    zero = jnp.zeros((), keys.dtype)
-    own = jnp.where(
-        lax.broadcasted_iota(jnp.int32, (2 * part_rows, head_width), 0) < part_rows,
-        lax.pad(own_keys, zero, ((0, part_rows, 0), (0, 0, 0))),
-        lax.pad(own_values, zero, ((part_rows, 0, 0), (0, 0, 0))),
-    )
-    others = [swap(own, "ctx", step * inner) for step in range(1, outer)]
-    return jnp.concatenate([own] + others, axis=0)
-
-
-def paired_line(keys, values, inner, part_rows):
+    own = jnp.concatenate(
+        [
+            lax.dynamic_slice_in_dim(keys, start, part_rows, 0),
+            lax.dynamic_slice_in_dim(values, start, part_rows, 0),
+        ],
+        axis=0,
+    )
+    line = jnp.concatenate(
+        [own] + [swap(own, "ctx", step * inner) for step in range(1, outer)], axis=0
+    )
+    plane = [line] + [swap(line, "ctx", offset) for offset in range(1, inner)]
+    prepared, plane[0] = run_prepare(line)
+    pieces = plane + [
+        swap(piece, "dp", far) for far in range(1, lax.axis_size("dp")) for piece in plane
+    ]
+    return prepared, pieces
+
+
+def gather_paired(keys, values, inner, part_rows, run_prepare):
     head_width = keys.shape[1]
+    lowest = jnp.array(-jnp.inf, keys.dtype)
     halves = (2, 1, part_rows, head_width)
-    own = jnp.where(
-        lax.broadcasted_iota(jnp.int32, (2, 2, part_rows, head_width), 1) == 0,
-        keys.reshape(halves),
-        values.reshape(halves),
+    own = jnp.maximum(
+        lax.pad(keys.reshape(halves), lowest, ((0, 0, 0), (0, 1, 0), (0, 0, 0), (0, 0, 0))),
+        lax.pad(values.reshape(halves), lowest, ((0, 0, 0), (1, 0, 0), (0, 0, 0), (0, 0, 0))),
     ).reshape(4 * part_rows, head_width)
     rows = 2 * part_rows
     own_half = lax.dynamic_slice_in_dim(own, lax.axis_index("dp") * rows, rows, 0)
@@ -402,7 +444,14 @@
         for dp in range(2)
     ]
     whole = lax.ppermute(own, ("ctx", "dp"), pairs)
-    return jnp.concatenate([own_half, swap(own_half, "ctx", 2 * inner), whole], axis=0)
+    away = jnp.concatenate([whole, swap(own_half, "ctx", 2 * inner)], axis=0)
+    nears = [swap(own_half, "ctx", offset) for offset in range(1, inner)]
+    nears, away = lax.optimization_barrier((nears, away))
+    aways = [swap(away, "ctx", offset) for offset in range(1, inner)]
+    nears, aways[-1] = lax.optimization_barrier((nears, aways[-1]))
+    held = [jnp.concatenate(nears, axis=0), away] + aways
+    prepared, held[1] = run_prepare(away)
+    return prepared, [own] + held + [swap(piece, "dp", 1) for piece in held]
 
 
 def body(queries, keys, values, out_grads, doc_lengths):
@@ -412,39 +461,47 @@
     outer = ctx_count // inner
     tok_rows, head_width = keys.shape
     part_rows = tok_rows // dp_count
-    tile = math.gcd(256, ctx_count * tok_rows)
+    seq = ctx_count * tok_rows
+    tile = math.gcd(256, seq)
+
+    def run_prepare(held):
+        *prepared, held = prepare(
+            ctx_count, tile, doc_lengths, queries, out_grads, head_width, held
+        )
+        return prepared, held
+
     if outer == 4 and dp_count == 2:
-        line = paired_line(keys, values, inner, part_rows)
-        moves = functools.partial(paired_moves, inner, part_rows)
+        gather, moves = gather_paired, functools.partial(paired_moves, inner, part_rows)
     else:
-        line = staged_line(keys, values, inner, part_rows)
+        gather = gather_staged
         moves = functools.partial(staged_moves, ctx_count, dp_count, inner, part_rows)
-    plane = [line] + [swap(line, "ctx", offset) for offset in range(1, inner)]
-    stacked, flipped, starts, tiles, zeros, plane[0] = prepare(
-        ctx_count, tile, doc_lengths, queries, out_grads, head_width, line
-    )
-    pieces = plane + [
-        swap(piece, "dp", offset) for offset in range(1, dp_count) for piece in plane
-    ]
+    (stacked, flipped, starts, tiles, zeros), pieces = gather(
+        keys, values, inner, part_rows, run_prepare
+    )
     keys_ordered, dlogits, parts = attend(
-        ctx_count, dp_count, inner, tile, moves, tiles, starts, stacked, flipped, zeros, pieces
-    )
-    plane_sums = [
+        ctx_count, dp_count, inner, tile, moves, tiles, starts, stacked, flipped, zeros, pieces, seq
+    )
+    kinds = inner + 1
+    home, *plane_sums = [
         total_of(
-            [parts[offset]]
-            + [swap(parts[far * inner + offset], "dp", far) for far in range(1, dp_count)]
+            [parts[kind]] + [swap(parts[far * kinds + kind], "dp", far) for far in range(1, dp_count)]
         )
-        for offset in range(inner)
+        for kind in range(kinds)
     ]
     query_grads, plane_sums[0] = query_side(
         ctx_count, tile, tiles, keys_ordered, dlogits, plane_sums[0], tok_rows
     )
     line_sum = total_of(
-        [plane_sums[0]] + [swap(plane_sums[offset], "ctx", offset) for offset in reversed(range(1, inner))]
-    )
-    blocks = jnp.split(line_sum, outer, axis=0)
+        [plane_sums[0]]
+        + [swap(plane_sums[offset], "ctx", offset) for offset in reversed(range(1, inner))]
+    )
+    line_sum, home = lax.optimization_barrier((line_sum, home))
+    blocks = jnp.split(line_sum, outer - 1, axis=0)
+    home = jnp.split(home, inner, axis=0)
     kv_grads = total_of(
-        [blocks[0]] + [swap(blocks[block], "ctx", block * inner) for block in send_order(outer)]
+        [home[0]]
+        + [swap(home[offset], "ctx", offset) for offset in range(1, inner)]
+        + [swap(blocks[step - 1], "ctx", step * inner) for step in send_order(outer)]
     )
     return (query_grads, kv_grads[:part_rows], kv_grads[part_rows:])
 

time: 44.5 us -> 47.3 us (1.063)
  starting transfers between devices: 19.7 us -> 27 us
  waiting for transfers between devices: 16.7 us -> 12.1 us
    ppermute x18 -> x26, starting transfers between devices: 16.7 us -> 23.9 us  [swap(): return lax.ppermute(value, axis, pairs)]
    ppermute x18 -> x26, waiting for transfers between devices: 16.7 us -> 12.1 us  [swap(): return lax.ppermute(value, axis, pairs)]
    select_n x1 -> x0, other arithmetic: 0.87 us -> none  [paired_line(): jnp.where(lax.broadcasted_iota(jnp.int32, (2, 2, part_rows, head_width),...]
    max x0 -> x1, other arithmetic: none -> 0.79 us  [gather_paired(): jnp.maximum(lax.pad(keys.reshape(halves), lowest, ((0, 0, 0), (0, 1, 0),...]
  transfers between devices with their start and end apart: 19 -> 27, of which waited for: 11 -> 15; matrix products, arithmetic and copies ran while one was open for 0% -> 0% of each run, Pallas kernels for 7% -> 7%
where the time goes in v3:
time: 47.3 us; the launch traced here: 47 us
  starting transfers between devices  27 us (57%)
  waiting for transfers between devices  12.1 us (26%)
  Pallas kernels  5.49 us (12%)
  other arithmetic  1.05 us (2%)
  between operations  0.77 us (2%)
  local copies, waits for them, and re-layouts  0.66 us (1%)
    ppermute x26, starting transfers between devices, swap(): return lax.ppermute(value, axis, pairs)  23.9 us
    ppermute x26, waiting for transfers between devices, swap(): return lax.ppermute(value, axis, pairs)  12.1 us
    ppermute x1, starting transfers between devices, gather_paired(): whole = lax.ppermute(own, ('ctx', 'dp'), pairs)  3.08 us
    pallas_call x1, Pallas kernels, attend(): pl.pallas_call(functools.partial(attend_kernel, ctx_count, dp_count, inne...  2.27 us
    pallas_call x1, Pallas kernels, query_side(): pl.pallas_call(functools.partial(query_kernel, ctx_count, tile), out_shap...  1.97 us
    pallas_call x1, Pallas kernels, prepare(): pl.pallas_call(functools.partial(prepare_kernel, ctx_count, tile), out_sh...  1.26 us
  transfers between devices with their start and end apart: 27, of which 15 were waited for; matrix products, arithmetic and copies ran while one was open for 0% of the time, Pallas kernels for 7%

profile of v3, /device:TPU:0, one launch (start us, length us, event | category | flops | bytes accessed | tf_op | source)
XLA Modules:
  0.0 47.0 jit_solution(15219610789827881484)
XLA Ops:
  0.6 0.8 %pad_maximum_fusion.1 = bf16[2,2,64,128]{3,2,1,0:T(8,128)(2,1)S(1)} fusion(bf16[2,1,64,128]{3,2,1,0:T(8,128)(2,1)} %bitcast.10, bf16[2,1,64,128]{3,2,1,0:T(8,128)(2,1)} %bitcast.11), kind=kLoop, calls=%fused_computation.8 | loop fusion | flops 32768 | bytes 131072 | tf_op jit(solution)/shard_map/max | solution.py:435
  1.4 3.1 %collective-permute-start.3 = (bf16[256,128]{1,0:T(8,128)(2,1)S(1)}, bf16[256,128]{1,0:T(8,128)(2,1)S(1)}, u32[]{:S(2)}, u32[]{:S(2)}) collective-permute-start(bf16[256,128]{1,0:T(8,128)(2,1)S(1)} %bitcast.7), channel_id=1, source_target_pairs={{0,8},{1,25},{2,10},{3,27},{4,12},{5,29},{6,14},{7,31},{8,0},{9,17... | collective-permute-start | bytes 196616 | tf_op jit(solution)/shard_map/ppermute | solution.py:446
  4.5 2.6 %collective-permute-start.4 = (bf16[128,128]{1,0:T(8,128)(2,1)S(1)}, bf16[128,128]{1,0:T(8,128)(2,1)S(1)}, u32[]{:S(2)}, u32[]{:S(2)}) collective-permute-start(bf16[128,128]{1,0:T(8,128)(2,1)S(1)} %constant_dynamic-slice_fusion), channel_id=1, source_target_pairs={{0,16},{2,18},{4,20},{6,22},{8,24},{10,26},{12,28},{14,30},{16,0},... | collective-permute-start | bytes 98312 | tf_op jit(solution)/shard_map/ppermute | solution.py:402
  7.1 2.4 %collective-permute-start.2 = (bf16[128,128]{1,0:T(8,128)(2,1)S(1)}, bf16[128,128]{1,0:T(8,128)(2,1)S(1)}, u32[]{:S(2)}, u32[]{:S(2)}) collective-permute-start(bf16[128,128]{1,0:T(8,128)(2,1)S(1)} %constant_dynamic-slice_fusion), channel_id=1, source_target_pairs={{0,6},{2,4},{4,2},{6,0},{8,14},{10,12},{12,10},{14,8},{16,22},{18,... | collective-permute-start | bytes 98312 | tf_op jit(solution)/shard_map/ppermute | solution.py:402
  10.6 1.3 %collective-permute-done.2 = bf16[128,128]{1,0:T(8,128)(2,1)S(1)} collective-permute-done((bf16[128,128]{1,0:T(8,128)(2,1)S(1)}, bf16[128,128]{1,0:T(8,128)(2,1)S(1)}, u32[]{:S(2)}, u32[]{:S(2)}) %collective-permute-start.2) | collective-permute-done | bytes 32800 | tf_op jit(solution)/shard_map/ppermute | solution.py:402
  11.9 1.5 %collective-permute-done.1 = bf16[128,128]{1,0:T(8,128)(2,1)S(1)} collective-permute-done((bf16[128,128]{1,0:T(8,128)(2,1)S(1)}, bf16[128,128]{1,0:T(8,128)(2,1)S(1)}, u32[]{:S(2)}, u32[]{:S(2)}) %collective-permute-start.1) | collective-permute-done | bytes 32800 | tf_op jit(solution)/shard_map/ppermute | solution.py:402
  14.0 1.7 %collective-permute-start.5 = (bf16[384,128]{1,0:T(8,128)(2,1)S(1)}, bf16[384,128]{1,0:T(8,128)(2,1)S(1)}, u32[]{:S(2)}, u32[]{:S(2)}) collective-permute-start(bf16[384,128]{1,0:T(8,128)(2,1)S(1)} %pad_maximum_fusion.line_ref), channel_id=1, source_target_pairs={{0,6},{2,4},{4,2},{6,0},{8,14},{10,12},{12,10},{14,8},{16,22},{18,... | collective-permute-start | bytes 294920 | tf_op jit(solution)/shard_map/ppermute | solution.py:402
  16.0 1.5 %collective-permute-start.6 = (bf16[384,128]{1,0:T(8,128)(2,1)S(1)}, bf16[384,128]{1,0:T(8,128)(2,1)S(1)}, u32[]{:S(2)}, u32[]{:S(2)}) collective-permute-start(bf16[384,128]{1,0:T(8,128)(2,1)S(1)} %pad_maximum_fusion.line_ref), channel_id=1, source_target_pairs={{0,2},{2,0},{4,6},{6,4},{8,10},{10,8},{12,14},{14,12},{16,18},{18,... | collective-permute-start | bytes 294920 | tf_op jit(solution)/shard_map/ppermute | solution.py:402
  17.5 1.3 %shard_map.76 = (bf16[2,2,512,128]{3,2,1,0:T(8,128)(2,1)S(1)}, bf16[2,2,128,512]{3,2,1,0:T(8,128)(2,1)S(1)}, s32[2,1,512]{2,1,0:T(1,128)S(1)}, s32[8,128]{1,0:T(...) custom-call(s32[8]{0:T(128)} %lengths_hbm.1, bf16[128,1024]{1,0:T(8,128)(2,1)} %q_hbm.1, ...), custom_call_target="tpu_custom_call" | custom-call | tf_op jit(solution)/shard_map/pallas_call | solution.py:318
  18.8 0.7 %collective-permute-done.5.refs_5_ = bf16[384,128]{1,0:T(8,128)(2,1)S(1)} collective-permute-done((bf16[384,128]{1,0:T(8,128)(2,1)S(1)}, bf16[384,128]{1,0:T(8,128)(2,1)S(1)}, u32[]{:S(2)}, u32[]{:S(2)}) %collective-permute-start.5) | collective-permute-done | bytes 98336 | tf_op jit(solution)/shard_map/ppermute | solution.py:402
  19.6 0.9 %collective-permute-done.7.refs_4_ = bf16[384,128]{1,0:T(8,128)(2,1)S(1)} collective-permute-done((bf16[384,128]{1,0:T(8,128)(2,1)S(1)}, bf16[384,128]{1,0:T(8,128)(2,1)S(1)}, u32[]{:S(2)}, u32[]{:S(2)}) %collective-permute-start.7) | collective-permute-done | bytes 98336 | tf_op jit(solution)/shard_map/ppermute | solution.py:402
  22.3 2.3 %shard_map.77 = (bf16[2304,128]{1,0:T(8,128)(2,1)S(1)}, bf16[2,4,2048,128]{3,2,1,0:T(8,128)(2,1)S(1)}, f32[2,2304,128]{2,1,0:T(8,128)S(1)}, bf16[512,128]{1,0:T(...) custom-call(s32[8,128]{1,0:T(8,128)S(1)} %get-tuple-element.34.tiles, ...), custom_call_target="tpu_custom_call", output_to_operand_aliasing={{2}: (4, {})} | custom-call | tf_op jit(solution)/shard_map/pallas_call | solution.py:350
  26.0 3.1 %collective-permute-start.15 = (bf16[384,128]{1,0:T(8,128)(2,1)S(1)}, bf16[384,128]{1,0:T(8,128)(2,1)S(1)}, u32[]{:S(2)}, u32[]{:S(2)}) collective-permute-start(bf16[384,128]{1,0:T(8,128)(2,1)S(1)} %add_convert_fusion.4), channel_id=1, source_target_pairs={{0,6},{2,4},{4,2},{6,0},{8,14},{10,12},{12,10},{14,8},{16,22},{18,... | collective-permute-start | bytes 294920 | tf_op jit(solution)/shard_map/ppermute | solution.py:402
  29.3 0.9 %collective-permute-start.19 = (bf16[384,128]{1,0:T(8,128)(2,1)S(1)}, bf16[384,128]{1,0:T(8,128)(2,1)S(1)}, u32[]{:S(2)}, u32[]{:S(2)}) collective-permute-start(bf16[384,128]{1,0:T(8,128)(2,1)S(1)} %add_convert_fusion.2), channel_id=1, source_target_pairs={{0,2},{2,0},{4,6},{6,4},{8,10},{10,8},{12,14},{14,12},{16,18},{18,... | collective-permute-start | bytes 294920 | tf_op jit(solution)/shard_map/ppermute | solution.py:402
  30.3 2.0 %shard_map.78 = (bf16[128,1024]{1,0:T(8,128)(2,1)}, bf16[384,128]{1,0:T(8,128)(2,1)S(1)}) custom-call(s32[8,128]{1,0:T(8,128)S(1)} %get-tuple-element.34.tiles_ref, bf16[2304,128]{1,0:T(8,128)(2,1)S(1)} %get-tuple-element.47.keys_ref, bf16[2,4,2048,128]{3,2,1,0:T(8,128)(2,1)S(1)} %get-tuple-element.48.dlogits_ref, ...), custom_call_target="tpu_custom_call" | custom-call | tf_op jit(solution)/shard_map/pallas_call | solution.py:381
  32.4 2.1 %collective-permute-done.17 = bf16[384,128]{1,0:T(8,128)(2,1)S(1)} collective-permute-done((bf16[384,128]{1,0:T(8,128)(2,1)S(1)}, bf16[384,128]{1,0:T(8,128)(2,1)S(1)}, u32[]{:S(2)}, u32[]{:S(2)}) %collective-permute-start.17) | collective-permute-done | bytes 98336 | tf_op jit(solution)/shard_map/ppermute | solution.py:402
  34.8 4.0 %collective-permute-start.24 = (bf16[128,128]{1,0:T(8,128)(2,1)S(1)}, bf16[128,128]{1,0:T(8,128)(2,1)S(1)}, u32[]{:S(2)}, u32[]{:S(2)}) collective-permute-start(bf16[128,128]{1,0:T(8,128)(2,1)S(1)} %get-tuple-element.66), channel_id=1, source_target_pairs={{0,24},{2,26},{4,28},{6,30},{8,16},{10,18},{12,20},{14,22},{16,8},... | collective-permute-start | bytes 98312 | tf_op jit(solution)/shard_map/ppermute | solution.py:402
  38.8 0.6 %collective-permute-start.25 = (bf16[128,128]{1,0:T(8,128)(2,1)S(1)}, bf16[128,128]{1,0:T(8,128)(2,1)S(1)}, u32[]{:S(2)}, u32[]{:S(2)}) collective-permute-start(bf16[128,128]{1,0:T(8,128)(2,1)S(1)} %get-tuple-element.68), channel_id=1, source_target_pairs={{0,8},{2,10},{4,12},{6,14},{8,0},{10,2},{12,4},{14,6},{16,24},{18,... | collective-permute-start | bytes 98312 | tf_op jit(solution)/shard_map/ppermute | solution.py:402
  39.5 1.6 %collective-permute-start.21 = (bf16[128,128]{1,0:T(8,128)(2,1)S(1)}, bf16[128,128]{1,0:T(8,128)(2,1)S(1)}, u32[]{:S(2)}, u32[]{:S(2)}) collective-permute-start(bf16[128,128]{1,0:T(8,128)(2,1)S(1)} %get-tuple-element.63), channel_id=1, source_target_pairs={{0,2},{2,0},{4,6},{6,4},{8,10},{10,8},{12,14},{14,12},{16,18},{18,... | collective-permute-start | bytes 98312 | tf_op jit(solution)/shard_map/ppermute | solution.py:402
  41.1 1.4 %collective-permute-start.23 = (bf16[128,128]{1,0:T(8,128)(2,1)S(1)}, bf16[128,128]{1,0:T(8,128)(2,1)S(1)}, u32[]{:S(2)}, u32[]{:S(2)}) collective-permute-start(bf16[128,128]{1,0:T(8,128)(2,1)S(1)} %get-tuple-element.64), channel_id=1, source_target_pairs={{0,6},{2,4},{4,2},{6,0},{8,14},{10,12},{12,10},{14,8},{16,22},{18,... | collective-permute-start | bytes 98312 | tf_op jit(solution)/shard_map/ppermute | solution.py:402
  42.5 0.6 %collective-permute-start.22 = (bf16[128,128]{1,0:T(8,128)(2,1)S(1)}, bf16[128,128]{1,0:T(8,128)(2,1)S(1)}, u32[]{:S(2)}, u32[]{:S(2)}) collective-permute-start(bf16[128,128]{1,0:T(8,128)(2,1)S(1)} %get-tuple-element.65), channel_id=1, source_target_pairs={{0,4},{2,6},{4,0},{6,2},{8,12},{10,14},{12,8},{14,10},{16,20},{18,... | collective-permute-start | bytes 98312 | tf_op jit(solution)/shard_map/ppermute | solution.py:402
  43.0 0.6 %collective-permute-done.26 = bf16[128,128]{1,0:T(8,128)(2,1)S(1)} collective-permute-done((bf16[128,128]{1,0:T(8,128)(2,1)S(1)}, bf16[128,128]{1,0:T(8,128)(2,1)S(1)}, u32[]{:S(2)}, u32[]{:S(2)}) %collective-permute-start.26) | collective-permute-done | bytes 32800 | tf_op jit(solution)/shard_map/ppermute | solution.py:402
  43.7 2.2 %collective-permute-done.23 = bf16[128,128]{1,0:T(8,128)(2,1)S(1)} collective-permute-done((bf16[128,128]{1,0:T(8,128)(2,1)S(1)}, bf16[128,128]{1,0:T(8,128)(2,1)S(1)}, u32[]{:S(2)}, u32[]{:S(2)}) %collective-permute-start.23) | collective-permute-done | bytes 32800 | tf_op jit(solution)/shard_map/ppermute | solution.py:402
  46.4 0.6 %fusion.2 = (bf16[64,128]{1,0:T(8,128)(2,1)}, bf16[64,128]{1,0:T(8,128)(2,1)}) fusion(bf16[128,128]{1,0:T(8,128)(2,1)S(1)} %add_convert_fusion.6), kind=kLoop, calls=%fused_computation.15 | loop fusion | bytes 65536 | tf_op jit(solution)/shard_map/slice | solution.py:506
  (49 shorter events, 6.5 us)
Async XLA Ops:
  1.4 9.2 %collective-permute-start.3 = (bf16[256,128]{1,0:T(8,128)(2,1)S(1)}, bf16[256,128]{1,0:T(8,128)(2,1)S(1)}, u32[]{:S(2)}, u32[]{:S(2)}) collective-permute-start(bf16[256,128]{1,0:T(8,128)(2,1)S(1)} %bitcast.7), channel_id=1, source_target_pairs={{0,8},{1,25},{2,10},{3,27},{4,12},{5,29},{6,14},{7,31},{8,0},{9,17... | collective-permute-start | bytes 196616 | tf_op jit(solution)/shard_map/ppermute | solution.py:446
  4.5 6.1 %collective-permute-start.4 = (bf16[128,128]{1,0:T(8,128)(2,1)S(1)}, bf16[128,128]{1,0:T(8,128)(2,1)S(1)}, u32[]{:S(2)}, u32[]{:S(2)}) collective-permute-start(bf16[128,128]{1,0:T(8,128)(2,1)S(1)} %constant_dynamic-slice_fusion), channel_id=1, source_target_pairs={{0,16},{2,18},{4,20},{6,22},{8,24},{10,26},{12,28},{14,30},{16,0},... | collective-permute-start | bytes 98312 | tf_op jit(solution)/shard_map/ppermute | solution.py:402
  7.1 4.8 %collective-permute-start.2 = (bf16[128,128]{1,0:T(8,128)(2,1)S(1)}, bf16[128,128]{1,0:T(8,128)(2,1)S(1)}, u32[]{:S(2)}, u32[]{:S(2)}) collective-permute-start(bf16[128,128]{1,0:T(8,128)(2,1)S(1)} %constant_dynamic-slice_fusion), channel_id=1, source_target_pairs={{0,6},{2,4},{4,2},{6,0},{8,14},{10,12},{12,10},{14,8},{16,22},{18,... | collective-permute-start | bytes 98312 | tf_op jit(solution)/shard_map/ppermute | solution.py:402
  9.5 3.9 %collective-permute-start.1 = (bf16[128,128]{1,0:T(8,128)(2,1)S(1)}, bf16[128,128]{1,0:T(8,128)(2,1)S(1)}, u32[]{:S(2)}, u32[]{:S(2)}) collective-permute-start(bf16[128,128]{1,0:T(8,128)(2,1)S(1)} %constant_dynamic-slice_fusion), channel_id=1, source_target_pairs={{0,4},{2,6},{4,0},{6,2},{8,12},{10,14},{12,8},{14,10},{16,20},{18,... | collective-permute-start | bytes 98312 | tf_op jit(solution)/shard_map/ppermute | solution.py:402
  10.0 3.9 %collective-permute-start = (bf16[128,128]{1,0:T(8,128)(2,1)S(1)}, bf16[128,128]{1,0:T(8,128)(2,1)S(1)}, u32[]{:S(2)}, u32[]{:S(2)}) collective-permute-start(bf16[128,128]{1,0:T(8,128)(2,1)S(1)} %constant_dynamic-slice_fusion), channel_id=1, source_target_pairs={{0,2},{2,0},{4,6},{6,4},{8,10},{10,8},{12,14},{14,12},{16,18},{18,... | collective-permute-start | bytes 98312 | tf_op jit(solution)/shard_map/ppermute | solution.py:402
  14.0 5.5 %collective-permute-start.5 = (bf16[384,128]{1,0:T(8,128)(2,1)S(1)}, bf16[384,128]{1,0:T(8,128)(2,1)S(1)}, u32[]{:S(2)}, u32[]{:S(2)}) collective-permute-start(bf16[384,128]{1,0:T(8,128)(2,1)S(1)} %pad_maximum_fusion.line_ref), channel_id=1, source_target_pairs={{0,6},{2,4},{4,2},{6,0},{8,14},{10,12},{12,10},{14,8},{16,22},{18,... | collective-permute-start | bytes 294920 | tf_op jit(solution)/shard_map/ppermute | solution.py:402
  15.6 4.9 %collective-permute-start.7 = (bf16[384,128]{1,0:T(8,128)(2,1)S(1)}, bf16[384,128]{1,0:T(8,128)(2,1)S(1)}, u32[]{:S(2)}, u32[]{:S(2)}) collective-permute-start(bf16[384,128]{1,0:T(8,128)(2,1)S(1)} %pad_maximum_fusion.line_ref), channel_id=1, source_target_pairs={{0,4},{2,6},{4,0},{6,2},{8,12},{10,14},{12,8},{14,10},{16,20},{18,... | collective-permute-start | bytes 294920 | tf_op jit(solution)/shard_map/ppermute | solution.py:402
  16.0 4.8 %collective-permute-start.6 = (bf16[384,128]{1,0:T(8,128)(2,1)S(1)}, bf16[384,128]{1,0:T(8,128)(2,1)S(1)}, u32[]{:S(2)}, u32[]{:S(2)}) collective-permute-start(bf16[384,128]{1,0:T(8,128)(2,1)S(1)} %pad_maximum_fusion.line_ref), channel_id=1, source_target_pairs={{0,2},{2,0},{4,6},{6,4},{8,10},{10,8},{12,14},{14,12},{16,18},{18,... | collective-permute-start | bytes 294920 | tf_op jit(solution)/shard_map/ppermute | solution.py:402
  18.7 2.6 %collective-permute-start.9 = (bf16[384,128]{1,0:T(8,128)(2,1)S(1)}, bf16[384,128]{1,0:T(8,128)(2,1)S(1)}, u32[]{:S(2)}, u32[]{:S(2)}) collective-permute-start(bf16[384,128]{1,0:T(8,128)(2,1)S(1)} %get-tuple-element.45.refs_2_), channel_id=1, source_target_pairs={{0,1},{1,0},{2,3},{3,2},{4,5},{5,4},{6,7},{7,6},{8,9},{9,8},{10,11... | collective-permute-start | bytes 294920 | tf_op jit(solution)/shard_map/ppermute | solution.py:402
  19.5 2.6 %collective-permute-start.8 = (bf16[384,128]{1,0:T(8,128)(2,1)S(1)}, bf16[384,128]{1,0:T(8,128)(2,1)S(1)}, u32[]{:S(2)}, u32[]{:S(2)}) collective-permute-start(bf16[384,128]{1,0:T(8,128)(2,1)S(1)} %constant_dynamic-update-slice_fusion.refs_1_), channel_id=1, source_target_pairs={{0,1},{1,0},{2,3},{3,2},{4,5},{5,4},{6,7},{7,6},{8,9},{9,8},{10,11... | collective-permute-start | bytes 294920 | tf_op jit(solution)/shard_map/ppermute | solution.py:402
  24.6 1.4 %collective-permute-start.14 = (bf16[384,128]{1,0:T(8,128)(2,1)S(1)}, bf16[384,128]{1,0:T(8,128)(2,1)S(1)}, u32[]{:S(2)}, u32[]{:S(2)}) collective-permute-start(bf16[384,128]{1,0:T(8,128)(2,1)S(1)} %get-tuple-element.54), channel_id=1, source_target_pairs={{0,1},{1,0},{2,3},{3,2},{4,5},{5,4},{6,7},{7,6},{8,9},{9,8},{10,11... | collective-permute-start | bytes 294920 | tf_op jit(solution)/shard_map/ppermute | solution.py:402
  25.0 5.3 %collective-permute-start.13 = (bf16[384,128]{1,0:T(8,128)(2,1)S(1)}, bf16[384,128]{1,0:T(8,128)(2,1)S(1)}, u32[]{:S(2)}, u32[]{:S(2)}) collective-permute-start(bf16[384,128]{1,0:T(8,128)(2,1)S(1)} %get-tuple-element.50), channel_id=1, source_target_pairs={{0,1},{1,0},{2,3},{3,2},{4,5},{5,4},{6,7},{7,6},{8,9},{9,8},{10,11... | collective-permute-start | bytes 294920 | tf_op jit(solution)/shard_map/ppermute | solution.py:402
  25.2 3.9 %collective-permute-start.16 = (bf16[384,128]{1,0:T(8,128)(2,1)S(1)}, bf16[384,128]{1,0:T(8,128)(2,1)S(1)}, u32[]{:S(2)}, u32[]{:S(2)}) collective-permute-start(bf16[384,128]{1,0:T(8,128)(2,1)S(1)} %get-tuple-element.56), channel_id=1, source_target_pairs={{0,1},{1,0},{2,3},{3,2},{4,5},{5,4},{6,7},{7,6},{8,9},{9,8},{10,11... | collective-permute-start | bytes 294920 | tf_op jit(solution)/shard_map/ppermute | solution.py:402
  25.5 3.8 %collective-permute-start.18 = (bf16[384,128]{1,0:T(8,128)(2,1)S(1)}, bf16[384,128]{1,0:T(8,128)(2,1)S(1)}, u32[]{:S(2)}, u32[]{:S(2)}) collective-permute-start(bf16[384,128]{1,0:T(8,128)(2,1)S(1)} %get-tuple-element.58), channel_id=1, source_target_pairs={{0,1},{1,0},{2,3},{3,2},{4,5},{5,4},{6,7},{7,6},{8,9},{9,8},{10,11... | collective-permute-start | bytes 294920 | tf_op jit(solution)/shard_map/ppermute | solution.py:402
  25.7 6.5 %collective-permute-start.20 = (bf16[512,128]{1,0:T(8,128)(2,1)S(1)}, bf16[512,128]{1,0:T(8,128)(2,1)S(1)}, u32[]{:S(2)}, u32[]{:S(2)}) collective-permute-start(bf16[512,128]{1,0:T(8,128)(2,1)S(1)} %get-tuple-element.60), channel_id=1, source_target_pairs={{0,1},{1,0},{2,3},{3,2},{4,5},{5,4},{6,7},{7,6},{8,9},{9,8},{10,11... | collective-permute-start | bytes 393224 | tf_op jit(solution)/shard_map/ppermute | solution.py:402
  26.0 6.4 %collective-permute-start.15 = (bf16[384,128]{1,0:T(8,128)(2,1)S(1)}, bf16[384,128]{1,0:T(8,128)(2,1)S(1)}, u32[]{:S(2)}, u32[]{:S(2)}) collective-permute-start(bf16[384,128]{1,0:T(8,128)(2,1)S(1)} %add_convert_fusion.4), channel_id=1, source_target_pairs={{0,6},{2,4},{4,2},{6,0},{8,14},{10,12},{12,10},{14,8},{16,22},{18,... | collective-permute-start | bytes 294920 | tf_op jit(solution)/shard_map/ppermute | solution.py:402
  29.2 5.3 %collective-permute-start.17 = (bf16[384,128]{1,0:T(8,128)(2,1)S(1)}, bf16[384,128]{1,0:T(8,128)(2,1)S(1)}, u32[]{:S(2)}, u32[]{:S(2)}) collective-permute-start(bf16[384,128]{1,0:T(8,128)(2,1)S(1)} %add_convert_fusion.3), channel_id=1, source_target_pairs={{0,4},{2,6},{4,0},{6,2},{8,12},{10,14},{12,8},{14,10},{16,20},{18,... | collective-permute-start | bytes 294920 | tf_op jit(solution)/shard_map/ppermute | solution.py:402
  29.3 5.4 %collective-permute-start.19 = (bf16[384,128]{1,0:T(8,128)(2,1)S(1)}, bf16[384,128]{1,0:T(8,128)(2,1)S(1)}, u32[]{:S(2)}, u32[]{:S(2)}) collective-permute-start(bf16[384,128]{1,0:T(8,128)(2,1)S(1)} %add_convert_fusion.2), channel_id=1, source_target_pairs={{0,2},{2,0},{4,6},{6,4},{8,10},{10,8},{12,14},{14,12},{16,18},{18,... | collective-permute-start | bytes 294920 | tf_op jit(solution)/shard_map/ppermute | solution.py:402
  34.8 7.7 %collective-permute-start.24 = (bf16[128,128]{1,0:T(8,128)(2,1)S(1)}, bf16[128,128]{1,0:T(8,128)(2,1)S(1)}, u32[]{:S(2)}, u32[]{:S(2)}) collective-permute-start(bf16[128,128]{1,0:T(8,128)(2,1)S(1)} %get-tuple-element.66), channel_id=1, source_target_pairs={{0,24},{2,26},{4,28},{6,30},{8,16},{10,18},{12,20},{14,22},{16,8},... | collective-permute-start | bytes 98312 | tf_op jit(solution)/shard_map/ppermute | solution.py:402
  38.8 4.8 %collective-permute-start.26 = (bf16[128,128]{1,0:T(8,128)(2,1)S(1)}, bf16[128,128]{1,0:T(8,128)(2,1)S(1)}, u32[]{:S(2)}, u32[]{:S(2)}) collective-permute-start(bf16[128,128]{1,0:T(8,128)(2,1)S(1)} %get-tuple-element.67), channel_id=1, source_target_pairs={{0,16},{2,18},{4,20},{6,22},{8,24},{10,26},{12,28},{14,30},{16,0},... | collective-permute-start | bytes 98312 | tf_op jit(solution)/shard_map/ppermute | solution.py:402
  38.8 4.8 %collective-permute-start.25 = (bf16[128,128]{1,0:T(8,128)(2,1)S(1)}, bf16[128,128]{1,0:T(8,128)(2,1)S(1)}, u32[]{:S(2)}, u32[]{:S(2)}) collective-permute-start(bf16[128,128]{1,0:T(8,128)(2,1)S(1)} %get-tuple-element.68), channel_id=1, source_target_pairs={{0,8},{2,10},{4,12},{6,14},{8,0},{10,2},{12,4},{14,6},{16,24},{18,... | collective-permute-start | bytes 98312 | tf_op jit(solution)/shard_map/ppermute | solution.py:402
  39.5 4.2 %collective-permute-start.21 = (bf16[128,128]{1,0:T(8,128)(2,1)S(1)}, bf16[128,128]{1,0:T(8,128)(2,1)S(1)}, u32[]{:S(2)}, u32[]{:S(2)}) collective-permute-start(bf16[128,128]{1,0:T(8,128)(2,1)S(1)} %get-tuple-element.63), channel_id=1, source_target_pairs={{0,2},{2,0},{4,6},{6,4},{8,10},{10,8},{12,14},{14,12},{16,18},{18,... | collective-permute-start | bytes 98312 | tf_op jit(solution)/shard_map/ppermute | solution.py:402
  41.1 4.8 %collective-permute-start.23 = (bf16[128,128]{1,0:T(8,128)(2,1)S(1)}, bf16[128,128]{1,0:T(8,128)(2,1)S(1)}, u32[]{:S(2)}, u32[]{:S(2)}) collective-permute-start(bf16[128,128]{1,0:T(8,128)(2,1)S(1)} %get-tuple-element.64), channel_id=1, source_target_pairs={{0,6},{2,4},{4,2},{6,0},{8,14},{10,12},{12,10},{14,8},{16,22},{18,... | collective-permute-start | bytes 98312 | tf_op jit(solution)/shard_map/ppermute | solution.py:402
  42.5 3.9 %collective-permute-start.22 = (bf16[128,128]{1,0:T(8,128)(2,1)S(1)}, bf16[128,128]{1,0:T(8,128)(2,1)S(1)}, u32[]{:S(2)}, u32[]{:S(2)}) collective-permute-start(bf16[128,128]{1,0:T(8,128)(2,1)S(1)} %get-tuple-element.65), channel_id=1, source_target_pairs={{0,4},{2,6},{4,0},{6,2},{8,12},{10,14},{12,8},{14,10},{16,20},{18,... | collective-permute-start | bytes 98312 | tf_op jit(solution)/shard_map/ppermute | solution.py:402
  (3 other events, 3.9 us)

commit v4 on v3

--- a/solution.py
+++ b/solution.py
@@ -97,20 +97,15 @@
 
 
 def paired_moves(inner, part_rows, ctx_index, dp_index):
-    yield 0, 0, ctx_index, 0
-    yield 0, 2 * part_rows, ctx_index, part_rows
     for side in range(2):
         holder = dp_index ^ side
-        pieces = 1 + side * (inner + 1)
-        for offset in range(1, inner):
-            near = ctx_index ^ offset
-            yield pieces, 2 * (offset - 1) * part_rows, near, holder * part_rows
         for offset in range(inner):
-            piece, near = pieces + 1 + offset, ctx_index ^ offset
+            piece, near = side * inner + offset, ctx_index ^ offset
             whole = near ^ jnp.where(holder == 1, 3 * inner, inner)
-            yield piece, 0, whole, 0
-            yield piece, 2 * part_rows, whole, part_rows
-            yield piece, 4 * part_rows, near ^ (2 * inner), holder * part_rows
+            yield piece, 0, near, holder * part_rows
+            yield piece, 2 * part_rows, near ^ (2 * inner), holder * part_rows
+            yield piece, 4 * part_rows, whole, 0
+            yield piece, 6 * part_rows, whole, part_rows
 
 
 def part_moves(ctx_count, dp_count, inner, part_rows, ctx_index, dp_index):
@@ -444,14 +439,10 @@
         for dp in range(2)
     ]
     whole = lax.ppermute(own, ("ctx", "dp"), pairs)
-    away = jnp.concatenate([whole, swap(own_half, "ctx", 2 * inner)], axis=0)
-    nears = [swap(own_half, "ctx", offset) for offset in range(1, inner)]
-    nears, away = lax.optimization_barrier((nears, away))
-    aways = [swap(away, "ctx", offset) for offset in range(1, inner)]
-    nears, aways[-1] = lax.optimization_barrier((nears, aways[-1]))
-    held = [jnp.concatenate(nears, axis=0), away] + aways
-    prepared, held[1] = run_prepare(away)
-    return prepared, [own] + held + [swap(piece, "dp", 1) for piece in held]
+    line = jnp.concatenate([own_half, swap(own_half, "ctx", 2 * inner), whole], axis=0)
+    plane = [line] + [swap(line, "ctx", offset) for offset in range(1, inner)]
+    prepared, plane[0] = run_prepare(line)
+    return prepared, plane + [swap(piece, "dp", 1) for piece in plane]
 
 
 def body(queries, keys, values, out_grads, doc_lengths):
@@ -491,11 +482,11 @@
     query_grads, plane_sums[0] = query_side(
         ctx_count, tile, tiles, keys_ordered, dlogits, plane_sums[0], tok_rows
     )
+    plane_sums[0], home = lax.optimization_barrier((plane_sums[0], home))
     line_sum = total_of(
         [plane_sums[0]]
         + [swap(plane_sums[offset], "ctx", offset) for offset in reversed(range(1, inner))]
     )
-    line_sum, home = lax.optimization_barrier((line_sum, home))
     blocks = jnp.split(line_sum, outer - 1, axis=0)
     home = jnp.split(home, inner, axis=0)
     kv_grads = total_of(

time: 47.3 us -> 44.7 us (0.945)
  starting transfers between devices: 27 us -> 22.9 us
  Pallas kernels: 5.49 us -> 8.96 us
  waiting for transfers between devices: 12.1 us -> 10.2 us
    ppermute x26 -> x22, starting transfers between devices: 23.9 us -> 19.8 us  [swap(): return lax.ppermute(value, axis, pairs)]
    pallas_call x1, Pallas kernels: 2.27 us -> 4.88 us  [attend(): pl.pallas_call(functools.partial(attend_kernel, ctx_count, dp_count, inne...]
    ppermute x26 -> x22, waiting for transfers between devices: 12.1 us -> 10.2 us  [swap(): return lax.ppermute(value, axis, pairs)]
    pallas_call x1, Pallas kernels: 1.97 us -> 2.82 us  [query_side(): pl.pallas_call(functools.partial(query_kernel, ctx_count, tile), out_shap...]
  transfers between devices with their start and end apart: 27 -> 23, of which waited for: 15 -> 7; matrix products, arithmetic and copies ran while one was open for 0% -> 1% of each run, Pallas kernels for 7% -> 9%
where the time goes in v4:
time: 44.7 us; the launch traced here: 44.5 us
  starting transfers between devices  22.9 us (51%)
  waiting for transfers between devices  10.2 us (23%)
  Pallas kernels  8.96 us (20%)
  other arithmetic  1.05 us (2%)
  between operations  0.75 us (2%)
  local copies, waits for them, and re-layouts  0.64 us (1%)
    ppermute x22, starting transfers between devices, swap(): return lax.ppermute(value, axis, pairs)  19.8 us
    ppermute x22, waiting for transfers between devices, swap(): return lax.ppermute(value, axis, pairs)  10.2 us
    pallas_call x1, Pallas kernels, attend(): pl.pallas_call(functools.partial(attend_kernel, ctx_count, dp_count, inne...  4.88 us
    ppermute x1, starting transfers between devices, gather_paired(): whole = lax.ppermute(own, ('ctx', 'dp'), pairs)  3.08 us
    pallas_call x1, Pallas kernels, query_side(): pl.pallas_call(functools.partial(query_kernel, ctx_count, tile), out_shap...  2.82 us
    pallas_call x1, Pallas kernels, prepare(): pl.pallas_call(functools.partial(prepare_kernel, ctx_count, tile), out_sh...  1.26 us
  transfers between devices with their start and end apart: 23, of which 7 were waited for; matrix products, arithmetic and copies ran while one was open for 1% of the time, Pallas kernels for 9%

profile of v4, /device:TPU:0, one launch (start us, length us, event | category | flops | bytes accessed | tf_op | source)
XLA Modules:
  0.0 44.5 jit_solution(18225675784770245847)
XLA Ops:
  0.6 0.8 %pad_maximum_fusion.1 = bf16[2,2,64,128]{3,2,1,0:T(8,128)(2,1)S(1)} fusion(bf16[2,1,64,128]{3,2,1,0:T(8,128)(2,1)} %bitcast.9, bf16[2,1,64,128]{3,2,1,0:T(8,128)(2,1)} %bitcast.10), kind=kLoop, calls=%fused_computation.8 | loop fusion | flops 32768 | bytes 131072 | tf_op jit(solution)/shard_map/max | solution.py:430
  1.4 3.1 %collective-permute-start.1 = (bf16[256,128]{1,0:T(8,128)(2,1)S(1)}, bf16[256,128]{1,0:T(8,128)(2,1)S(1)}, u32[]{:S(2)}, u32[]{:S(2)}) collective-permute-start(bf16[256,128]{1,0:T(8,128)(2,1)S(1)} %bitcast.7), channel_id=1, source_target_pairs={{0,8},{1,25},{2,10},{3,27},{4,12},{5,29},{6,14},{7,31},{8,0},{9,17... | collective-permute-start | bytes 196616 | tf_op jit(solution)/shard_map/ppermute | solution.py:441
  4.5 2.6 %collective-permute-start = (bf16[128,128]{1,0:T(8,128)(2,1)S(1)}, bf16[128,128]{1,0:T(8,128)(2,1)S(1)}, u32[]{:S(2)}, u32[]{:S(2)}) collective-permute-start(bf16[128,128]{1,0:T(8,128)(2,1)S(1)} %constant_dynamic-slice_fusion), channel_id=1, source_target_pairs={{0,16},{2,18},{4,20},{6,22},{8,24},{10,26},{12,28},{14,30},{16,0},... | collective-permute-start | bytes 98312 | tf_op jit(solution)/shard_map/ppermute | solution.py:397
  7.1 2.4 %collective-permute-done = bf16[128,128]{1,0:T(8,128)(2,1)S(1)} collective-permute-done((bf16[128,128]{1,0:T(8,128)(2,1)S(1)}, bf16[128,128]{1,0:T(8,128)(2,1)S(1)}, u32[]{:S(2)}, u32[]{:S(2)}) %collective-permute-start) | collective-permute-done | bytes 32800 | tf_op jit(solution)/shard_map/ppermute | solution.py:397
  9.5 2.5 %collective-permute-start.4 = (bf16[512,128]{1,0:T(8,128)(2,1)S(1)}, bf16[512,128]{1,0:T(8,128)(2,1)S(1)}, u32[]{:S(2)}, u32[]{:S(2)}) collective-permute-start(bf16[512,128]{1,0:T(8,128)(2,1)S(1)} %pad_maximum_fusion.line_ref), channel_id=1, source_target_pairs={{0,6},{2,4},{4,2},{6,0},{8,14},{10,12},{12,10},{14,8},{16,22},{18,... | collective-permute-start | bytes 393224 | tf_op jit(solution)/shard_map/ppermute | solution.py:397
  12.0 0.5 %collective-permute-start.3 = (bf16[512,128]{1,0:T(8,128)(2,1)S(1)}, bf16[512,128]{1,0:T(8,128)(2,1)S(1)}, u32[]{:S(2)}, u32[]{:S(2)}) collective-permute-start(bf16[512,128]{1,0:T(8,128)(2,1)S(1)} %pad_maximum_fusion.line_ref), channel_id=1, source_target_pairs={{0,4},{2,6},{4,0},{6,2},{8,12},{10,14},{12,8},{14,10},{16,20},{18,... | collective-permute-start | bytes 393224 | tf_op jit(solution)/shard_map/ppermute | solution.py:397
  12.5 0.5 %collective-permute-start.2 = (bf16[512,128]{1,0:T(8,128)(2,1)S(1)}, bf16[512,128]{1,0:T(8,128)(2,1)S(1)}, u32[]{:S(2)}, u32[]{:S(2)}) collective-permute-start(bf16[512,128]{1,0:T(8,128)(2,1)S(1)} %pad_maximum_fusion.line_ref), channel_id=1, source_target_pairs={{0,2},{2,0},{4,6},{6,4},{8,10},{10,8},{12,14},{14,12},{16,18},{18,... | collective-permute-start | bytes 393224 | tf_op jit(solution)/shard_map/ppermute | solution.py:397
  13.0 1.3 %shard_map.76 = (bf16[2,2,512,128]{3,2,1,0:T(8,128)(2,1)S(1)}, bf16[2,2,128,512]{3,2,1,0:T(8,128)(2,1)S(1)}, s32[2,1,512]{2,1,0:T(1,128)S(1)}, s32[8,128]{1,0:T(...) custom-call(s32[8]{0:T(128)} %lengths_hbm.1, bf16[128,1024]{1,0:T(8,128)(2,1)} %q_hbm.1, ...), custom_call_target="tpu_custom_call" | custom-call | tf_op jit(solution)/shard_map/pallas_call | solution.py:313
  14.4 2.3 %collective-permute-done.4.refs_3_ = bf16[512,128]{1,0:T(8,128)(2,1)S(1)} collective-permute-done((bf16[512,128]{1,0:T(8,128)(2,1)S(1)}, bf16[512,128]{1,0:T(8,128)(2,1)S(1)}, u32[]{:S(2)}, u32[]{:S(2)}) %collective-permute-start.4) | collective-permute-done | bytes 131104 | tf_op jit(solution)/shard_map/ppermute | solution.py:397
  16.7 2.6 %collective-permute-done.3.refs_2_ = bf16[512,128]{1,0:T(8,128)(2,1)S(1)} collective-permute-done((bf16[512,128]{1,0:T(8,128)(2,1)S(1)}, bf16[512,128]{1,0:T(8,128)(2,1)S(1)}, u32[]{:S(2)}, u32[]{:S(2)}) %collective-permute-start.3) | collective-permute-done | bytes 131104 | tf_op jit(solution)/shard_map/ppermute | solution.py:397
  19.8 0.8 %collective-permute-done.7.refs_6_ = bf16[512,128]{1,0:T(8,128)(2,1)S(1)} collective-permute-done((bf16[512,128]{1,0:T(8,128)(2,1)S(1)}, bf16[512,128]{1,0:T(8,128)(2,1)S(1)}, u32[]{:S(2)}, u32[]{:S(2)}) %collective-permute-start.7) | collective-permute-done | bytes 131104 | tf_op jit(solution)/shard_map/ppermute | solution.py:397
  20.8 4.9 %shard_map.77 = (bf16[2304,128]{1,0:T(8,128)(2,1)S(1)}, bf16[2,4,2048,128]{3,2,1,0:T(8,128)(2,1)S(1)}, f32[2,2304,128]{2,1,0:T(8,128)S(1)}, bf16[512,128]{1,0:T(...) custom-call(s32[8,128]{1,0:T(8,128)S(1)} %get-tuple-element.25.tiles, ...), custom_call_target="tpu_custom_call", output_to_operand_aliasing={{2}: (4, {})} | custom-call | tf_op jit(solution)/shard_map/pallas_call | solution.py:345
  27.2 1.2 %collective-permute-start.15 = (bf16[384,128]{1,0:T(8,128)(2,1)S(1)}, bf16[384,128]{1,0:T(8,128)(2,1)S(1)}, u32[]{:S(2)}, u32[]{:S(2)}) collective-permute-start(bf16[384,128]{1,0:T(8,128)(2,1)S(1)} %add_convert_fusion.4), channel_id=1, source_target_pairs={{0,6},{2,4},{4,2},{6,0},{8,14},{10,12},{12,10},{14,8},{16,22},{18,... | collective-permute-start | bytes 294920 | tf_op jit(solution)/shard_map/ppermute | solution.py:397
  28.3 1.9 %collective-permute-start.17 = (bf16[384,128]{1,0:T(8,128)(2,1)S(1)}, bf16[384,128]{1,0:T(8,128)(2,1)S(1)}, u32[]{:S(2)}, u32[]{:S(2)}) collective-permute-start(bf16[384,128]{1,0:T(8,128)(2,1)S(1)} %add_convert_fusion.3), channel_id=1, source_target_pairs={{0,4},{2,6},{4,0},{6,2},{8,12},{10,14},{12,8},{14,10},{16,20},{18,... | collective-permute-start | bytes 294920 | tf_op jit(solution)/shard_map/ppermute | solution.py:397
  30.3 0.6 %collective-permute-start.19 = (bf16[384,128]{1,0:T(8,128)(2,1)S(1)}, bf16[384,128]{1,0:T(8,128)(2,1)S(1)}, u32[]{:S(2)}, u32[]{:S(2)}) collective-permute-start(bf16[384,128]{1,0:T(8,128)(2,1)S(1)} %add_convert_fusion.2), channel_id=1, source_target_pairs={{0,2},{2,0},{4,6},{6,4},{8,10},{10,8},{12,14},{14,12},{16,18},{18,... | collective-permute-start | bytes 294920 | tf_op jit(solution)/shard_map/ppermute | solution.py:397
  31.0 2.8 %shard_map.78 = (bf16[128,1024]{1,0:T(8,128)(2,1)}, bf16[384,128]{1,0:T(8,128)(2,1)S(1)}) custom-call(s32[8,128]{1,0:T(8,128)S(1)} %get-tuple-element.25.tiles_ref, bf16[2304,128]{1,0:T(8,128)(2,1)S(1)} %get-tuple-element.31.keys_ref, bf16[2,4,2048,128]{3,2,1,0:T(8,128)(2,1)S(1)} %get-tuple-element.32.dlogits_ref, ...), custom_call_target="tpu_custom_call" | custom-call | tf_op jit(solution)/shard_map/pallas_call | solution.py:376
  33.9 1.6 %collective-permute-start.11 = (bf16[128,128]{1,0:T(8,128)(2,1)S(1)}, bf16[128,128]{1,0:T(8,128)(2,1)S(1)}, u32[]{:S(2)}, u32[]{:S(2)}) collective-permute-start(bf16[128,128]{1,0:T(8,128)(2,1)S(1)} %get-tuple-element.47), channel_id=1, source_target_pairs={{0,2},{2,0},{4,6},{6,4},{8,10},{10,8},{12,14},{14,12},{16,18},{18,... | collective-permute-start | bytes 98312 | tf_op jit(solution)/shard_map/ppermute | solution.py:397
  35.4 1.5 %collective-permute-start.13 = (bf16[128,128]{1,0:T(8,128)(2,1)S(1)}, bf16[128,128]{1,0:T(8,128)(2,1)S(1)}, u32[]{:S(2)}, u32[]{:S(2)}) collective-permute-start(bf16[128,128]{1,0:T(8,128)(2,1)S(1)} %get-tuple-element.48), channel_id=1, source_target_pairs={{0,6},{2,4},{4,2},{6,0},{8,14},{10,12},{12,10},{14,8},{16,22},{18,... | collective-permute-start | bytes 98312 | tf_op jit(solution)/shard_map/ppermute | solution.py:397
  36.9 0.5 %collective-permute-start.12 = (bf16[128,128]{1,0:T(8,128)(2,1)S(1)}, bf16[128,128]{1,0:T(8,128)(2,1)S(1)}, u32[]{:S(2)}, u32[]{:S(2)}) collective-permute-start(bf16[128,128]{1,0:T(8,128)(2,1)S(1)} %get-tuple-element.49), channel_id=1, source_target_pairs={{0,4},{2,6},{4,0},{6,2},{8,12},{10,14},{12,8},{14,10},{16,20},{18,... | collective-permute-start | bytes 98312 | tf_op jit(solution)/shard_map/ppermute | solution.py:397
  37.6 0.6 %collective-permute-start.22 = (bf16[128,128]{1,0:T(8,128)(2,1)S(1)}, bf16[128,128]{1,0:T(8,128)(2,1)S(1)}, u32[]{:S(2)}, u32[]{:S(2)}) collective-permute-start(bf16[128,128]{1,0:T(8,128)(2,1)S(1)} %get-tuple-element.51), channel_id=1, source_target_pairs={{0,16},{2,18},{4,20},{6,22},{8,24},{10,26},{12,28},{14,30},{16,0},... | collective-permute-start | bytes 98312 | tf_op jit(solution)/shard_map/ppermute | solution.py:397
  38.1 3.8 %collective-permute-start.21 = (bf16[128,128]{1,0:T(8,128)(2,1)S(1)}, bf16[128,128]{1,0:T(8,128)(2,1)S(1)}, u32[]{:S(2)}, u32[]{:S(2)}) collective-permute-start(bf16[128,128]{1,0:T(8,128)(2,1)S(1)} %get-tuple-element.52), channel_id=1, source_target_pairs={{0,8},{2,10},{4,12},{6,14},{8,0},{10,2},{12,4},{14,6},{16,24},{18,... | collective-permute-start | bytes 98312 | tf_op jit(solution)/shard_map/ppermute | solution.py:397
  42.0 1.3 %collective-permute-done.20 = bf16[128,128]{1,0:T(8,128)(2,1)S(1)} collective-permute-done((bf16[128,128]{1,0:T(8,128)(2,1)S(1)}, bf16[128,128]{1,0:T(8,128)(2,1)S(1)}, u32[]{:S(2)}, u32[]{:S(2)}) %collective-permute-start.20) | collective-permute-done | bytes 32800 | tf_op jit(solution)/shard_map/ppermute | solution.py:397
  43.3 0.6 %collective-permute-done.21 = bf16[128,128]{1,0:T(8,128)(2,1)S(1)} collective-permute-done((bf16[128,128]{1,0:T(8,128)(2,1)S(1)}, bf16[128,128]{1,0:T(8,128)(2,1)S(1)}, u32[]{:S(2)}, u32[]{:S(2)}) %collective-permute-start.21) | collective-permute-done | bytes 32800 | tf_op jit(solution)/shard_map/ppermute | solution.py:397
  43.9 0.6 %fusion.2 = (bf16[64,128]{1,0:T(8,128)(2,1)}, bf16[64,128]{1,0:T(8,128)(2,1)}) fusion(bf16[128,128]{1,0:T(8,128)(2,1)S(1)} %add_convert_fusion.6), kind=kLoop, calls=%fused_computation.12 | loop fusion | bytes 65536 | tf_op jit(solution)/shard_map/slice | solution.py:497
  (38 shorter events, 2.6 us)
Async XLA Ops:
  1.4 8.1 %collective-permute-start.1 = (bf16[256,128]{1,0:T(8,128)(2,1)S(1)}, bf16[256,128]{1,0:T(8,128)(2,1)S(1)}, u32[]{:S(2)}, u32[]{:S(2)}) collective-permute-start(bf16[256,128]{1,0:T(8,128)(2,1)S(1)} %bitcast.7), channel_id=1, source_target_pairs={{0,8},{1,25},{2,10},{3,27},{4,12},{5,29},{6,14},{7,31},{8,0},{9,17... | collective-permute-start | bytes 196616 | tf_op jit(solution)/shard_map/ppermute | solution.py:441
  4.5 5.0 %collective-permute-start = (bf16[128,128]{1,0:T(8,128)(2,1)S(1)}, bf16[128,128]{1,0:T(8,128)(2,1)S(1)}, u32[]{:S(2)}, u32[]{:S(2)}) collective-permute-start(bf16[128,128]{1,0:T(8,128)(2,1)S(1)} %constant_dynamic-slice_fusion), channel_id=1, source_target_pairs={{0,16},{2,18},{4,20},{6,22},{8,24},{10,26},{12,28},{14,30},{16,0},... | collective-permute-start | bytes 98312 | tf_op jit(solution)/shard_map/ppermute | solution.py:397
  9.5 7.2 %collective-permute-start.4 = (bf16[512,128]{1,0:T(8,128)(2,1)S(1)}, bf16[512,128]{1,0:T(8,128)(2,1)S(1)}, u32[]{:S(2)}, u32[]{:S(2)}) collective-permute-start(bf16[512,128]{1,0:T(8,128)(2,1)S(1)} %pad_maximum_fusion.line_ref), channel_id=1, source_target_pairs={{0,6},{2,4},{4,2},{6,0},{8,14},{10,12},{12,10},{14,8},{16,22},{18,... | collective-permute-start | bytes 393224 | tf_op jit(solution)/shard_map/ppermute | solution.py:397
  12.0 7.3 %collective-permute-start.3 = (bf16[512,128]{1,0:T(8,128)(2,1)S(1)}, bf16[512,128]{1,0:T(8,128)(2,1)S(1)}, u32[]{:S(2)}, u32[]{:S(2)}) collective-permute-start(bf16[512,128]{1,0:T(8,128)(2,1)S(1)} %pad_maximum_fusion.line_ref), channel_id=1, source_target_pairs={{0,4},{2,6},{4,0},{6,2},{8,12},{10,14},{12,8},{14,10},{16,20},{18,... | collective-permute-start | bytes 393224 | tf_op jit(solution)/shard_map/ppermute | solution.py:397
  12.5 6.9 %collective-permute-start.2 = (bf16[512,128]{1,0:T(8,128)(2,1)S(1)}, bf16[512,128]{1,0:T(8,128)(2,1)S(1)}, u32[]{:S(2)}, u32[]{:S(2)}) collective-permute-start(bf16[512,128]{1,0:T(8,128)(2,1)S(1)} %pad_maximum_fusion.line_ref), channel_id=1, source_target_pairs={{0,2},{2,0},{4,6},{6,4},{8,10},{10,8},{12,14},{14,12},{16,18},{18,... | collective-permute-start | bytes 393224 | tf_op jit(solution)/shard_map/ppermute | solution.py:397
  14.3 5.5 %collective-permute-start.5 = (bf16[512,128]{1,0:T(8,128)(2,1)S(1)}, bf16[512,128]{1,0:T(8,128)(2,1)S(1)}, u32[]{:S(2)}, u32[]{:S(2)}) collective-permute-start(bf16[512,128]{1,0:T(8,128)(2,1)S(1)} %get-tuple-element.30.refs_0_), channel_id=1, source_target_pairs={{0,1},{1,0},{2,3},{3,2},{4,5},{5,4},{6,7},{7,6},{8,9},{9,8},{10,11... | collective-permute-start | bytes 393224 | tf_op jit(solution)/shard_map/ppermute | solution.py:397
  16.7 3.1 %collective-permute-start.8 = (bf16[512,128]{1,0:T(8,128)(2,1)S(1)}, bf16[512,128]{1,0:T(8,128)(2,1)S(1)}, u32[]{:S(2)}, u32[]{:S(2)}) collective-permute-start(bf16[512,128]{1,0:T(8,128)(2,1)S(1)} %collective-permute-done.4.refs_3_), channel_id=1, source_target_pairs={{0,1},{1,0},{2,3},{3,2},{4,5},{5,4},{6,7},{7,6},{8,9},{9,8},{10,11... | collective-permute-start | bytes 393224 | tf_op jit(solution)/shard_map/ppermute | solution.py:397
  19.3 1.3 %collective-permute-start.7 = (bf16[512,128]{1,0:T(8,128)(2,1)S(1)}, bf16[512,128]{1,0:T(8,128)(2,1)S(1)}, u32[]{:S(2)}, u32[]{:S(2)}) collective-permute-start(bf16[512,128]{1,0:T(8,128)(2,1)S(1)} %collective-permute-done.3.refs_2_), channel_id=1, source_target_pairs={{0,1},{1,0},{2,3},{3,2},{4,5},{5,4},{6,7},{7,6},{8,9},{9,8},{10,11... | collective-permute-start | bytes 393224 | tf_op jit(solution)/shard_map/ppermute | solution.py:397
  19.4 1.4 %collective-permute-start.6 = (bf16[512,128]{1,0:T(8,128)(2,1)S(1)}, bf16[512,128]{1,0:T(8,128)(2,1)S(1)}, u32[]{:S(2)}, u32[]{:S(2)}) collective-permute-start(bf16[512,128]{1,0:T(8,128)(2,1)S(1)} %collective-permute-done.2.refs_1_), channel_id=1, source_target_pairs={{0,1},{1,0},{2,3},{3,2},{4,5},{5,4},{6,7},{7,6},{8,9},{9,8},{10,11... | collective-permute-start | bytes 393224 | tf_op jit(solution)/shard_map/ppermute | solution.py:397
  25.7 1.4 %collective-permute-start.14 = (bf16[384,128]{1,0:T(8,128)(2,1)S(1)}, bf16[384,128]{1,0:T(8,128)(2,1)S(1)}, u32[]{:S(2)}, u32[]{:S(2)}) collective-permute-start(bf16[384,128]{1,0:T(8,128)(2,1)S(1)} %get-tuple-element.42), channel_id=1, source_target_pairs={{0,1},{1,0},{2,3},{3,2},{4,5},{5,4},{6,7},{7,6},{8,9},{9,8},{10,11... | collective-permute-start | bytes 294920 | tf_op jit(solution)/shard_map/ppermute | solution.py:397
  26.1 4.8 %collective-permute-start.9 = (bf16[384,128]{1,0:T(8,128)(2,1)S(1)}, bf16[384,128]{1,0:T(8,128)(2,1)S(1)}, u32[]{:S(2)}, u32[]{:S(2)}) collective-permute-start(bf16[384,128]{1,0:T(8,128)(2,1)S(1)} %get-tuple-element.34), channel_id=1, source_target_pairs={{0,1},{1,0},{2,3},{3,2},{4,5},{5,4},{6,7},{7,6},{8,9},{9,8},{10,11... | collective-permute-start | bytes 294920 | tf_op jit(solution)/shard_map/ppermute | solution.py:397
  26.3 2.0 %collective-permute-start.16 = (bf16[384,128]{1,0:T(8,128)(2,1)S(1)}, bf16[384,128]{1,0:T(8,128)(2,1)S(1)}, u32[]{:S(2)}, u32[]{:S(2)}) collective-permute-start(bf16[384,128]{1,0:T(8,128)(2,1)S(1)} %get-tuple-element.44), channel_id=1, source_target_pairs={{0,1},{1,0},{2,3},{3,2},{4,5},{5,4},{6,7},{7,6},{8,9},{9,8},{10,11... | collective-permute-start | bytes 294920 | tf_op jit(solution)/shard_map/ppermute | solution.py:397
  26.6 3.7 %collective-permute-start.18 = (bf16[384,128]{1,0:T(8,128)(2,1)S(1)}, bf16[384,128]{1,0:T(8,128)(2,1)S(1)}, u32[]{:S(2)}, u32[]{:S(2)}) collective-permute-start(bf16[384,128]{1,0:T(8,128)(2,1)S(1)} %get-tuple-element.46), channel_id=1, source_target_pairs={{0,1},{1,0},{2,3},{3,2},{4,5},{5,4},{6,7},{7,6},{8,9},{9,8},{10,11... | collective-permute-start | bytes 294920 | tf_op jit(solution)/shard_map/ppermute | solution.py:397
  26.8 7.0 %collective-permute-start.10 = (bf16[512,128]{1,0:T(8,128)(2,1)S(1)}, bf16[512,128]{1,0:T(8,128)(2,1)S(1)}, u32[]{:S(2)}, u32[]{:S(2)}) collective-permute-start(bf16[512,128]{1,0:T(8,128)(2,1)S(1)} %get-tuple-element.38), channel_id=1, source_target_pairs={{0,1},{1,0},{2,3},{3,2},{4,5},{5,4},{6,7},{7,6},{8,9},{9,8},{10,11... | collective-permute-start | bytes 393224 | tf_op jit(solution)/shard_map/ppermute | solution.py:397
  27.2 9.7 %collective-permute-start.15 = (bf16[384,128]{1,0:T(8,128)(2,1)S(1)}, bf16[384,128]{1,0:T(8,128)(2,1)S(1)}, u32[]{:S(2)}, u32[]{:S(2)}) collective-permute-start(bf16[384,128]{1,0:T(8,128)(2,1)S(1)} %add_convert_fusion.4), channel_id=1, source_target_pairs={{0,6},{2,4},{4,2},{6,0},{8,14},{10,12},{12,10},{14,8},{16,22},{18,... | collective-permute-start | bytes 294920 | tf_op jit(solution)/shard_map/ppermute | solution.py:397
  28.3 9.1 %collective-permute-start.17 = (bf16[384,128]{1,0:T(8,128)(2,1)S(1)}, bf16[384,128]{1,0:T(8,128)(2,1)S(1)}, u32[]{:S(2)}, u32[]{:S(2)}) collective-permute-start(bf16[384,128]{1,0:T(8,128)(2,1)S(1)} %add_convert_fusion.3), channel_id=1, source_target_pairs={{0,4},{2,6},{4,0},{6,2},{8,12},{10,14},{12,8},{14,10},{16,20},{18,... | collective-permute-start | bytes 294920 | tf_op jit(solution)/shard_map/ppermute | solution.py:397
  30.3 7.1 %collective-permute-start.19 = (bf16[384,128]{1,0:T(8,128)(2,1)S(1)}, bf16[384,128]{1,0:T(8,128)(2,1)S(1)}, u32[]{:S(2)}, u32[]{:S(2)}) collective-permute-start(bf16[384,128]{1,0:T(8,128)(2,1)S(1)} %add_convert_fusion.2), channel_id=1, source_target_pairs={{0,2},{2,0},{4,6},{6,4},{8,10},{10,8},{12,14},{14,12},{16,18},{18,... | collective-permute-start | bytes 294920 | tf_op jit(solution)/shard_map/ppermute | solution.py:397
  33.9 4.3 %collective-permute-start.11 = (bf16[128,128]{1,0:T(8,128)(2,1)S(1)}, bf16[128,128]{1,0:T(8,128)(2,1)S(1)}, u32[]{:S(2)}, u32[]{:S(2)}) collective-permute-start(bf16[128,128]{1,0:T(8,128)(2,1)S(1)} %get-tuple-element.47), channel_id=1, source_target_pairs={{0,2},{2,0},{4,6},{6,4},{8,10},{10,8},{12,14},{14,12},{16,18},{18,... | collective-permute-start | bytes 98312 | tf_op jit(solution)/shard_map/ppermute | solution.py:397
  35.4 6.6 %collective-permute-start.13 = (bf16[128,128]{1,0:T(8,128)(2,1)S(1)}, bf16[128,128]{1,0:T(8,128)(2,1)S(1)}, u32[]{:S(2)}, u32[]{:S(2)}) collective-permute-start(bf16[128,128]{1,0:T(8,128)(2,1)S(1)} %get-tuple-element.48), channel_id=1, source_target_pairs={{0,6},{2,4},{4,2},{6,0},{8,14},{10,12},{12,10},{14,8},{16,22},{18,... | collective-permute-start | bytes 98312 | tf_op jit(solution)/shard_map/ppermute | solution.py:397
  36.9 5.1 %collective-permute-start.12 = (bf16[128,128]{1,0:T(8,128)(2,1)S(1)}, bf16[128,128]{1,0:T(8,128)(2,1)S(1)}, u32[]{:S(2)}, u32[]{:S(2)}) collective-permute-start(bf16[128,128]{1,0:T(8,128)(2,1)S(1)} %get-tuple-element.49), channel_id=1, source_target_pairs={{0,4},{2,6},{4,0},{6,2},{8,12},{10,14},{12,8},{14,10},{16,20},{18,... | collective-permute-start | bytes 98312 | tf_op jit(solution)/shard_map/ppermute | solution.py:397
  37.5 5.8 %collective-permute-start.20 = (bf16[128,128]{1,0:T(8,128)(2,1)S(1)}, bf16[128,128]{1,0:T(8,128)(2,1)S(1)}, u32[]{:S(2)}, u32[]{:S(2)}) collective-permute-start(bf16[128,128]{1,0:T(8,128)(2,1)S(1)} %get-tuple-element.50), channel_id=1, source_target_pairs={{0,24},{2,26},{4,28},{6,30},{8,16},{10,18},{12,20},{14,22},{16,8},... | collective-permute-start | bytes 98312 | tf_op jit(solution)/shard_map/ppermute | solution.py:397
  37.6 5.7 %collective-permute-start.22 = (bf16[128,128]{1,0:T(8,128)(2,1)S(1)}, bf16[128,128]{1,0:T(8,128)(2,1)S(1)}, u32[]{:S(2)}, u32[]{:S(2)}) collective-permute-start(bf16[128,128]{1,0:T(8,128)(2,1)S(1)} %get-tuple-element.51), channel_id=1, source_target_pairs={{0,16},{2,18},{4,20},{6,22},{8,24},{10,26},{12,28},{14,30},{16,0},... | collective-permute-start | bytes 98312 | tf_op jit(solution)/shard_map/ppermute | solution.py:397
  38.1 5.7 %collective-permute-start.21 = (bf16[128,128]{1,0:T(8,128)(2,1)S(1)}, bf16[128,128]{1,0:T(8,128)(2,1)S(1)}, u32[]{:S(2)}, u32[]{:S(2)}) collective-permute-start(bf16[128,128]{1,0:T(8,128)(2,1)S(1)} %get-tuple-element.52), channel_id=1, source_target_pairs={{0,8},{2,10},{4,12},{6,14},{8,0},{10,2},{12,4},{14,6},{16,24},{18,... | collective-permute-start | bytes 98312 | tf_op jit(solution)/shard_map/ppermute | solution.py:397

commit v5 on v1

--- a/solution.py
+++ b/solution.py
@@ -24,6 +24,10 @@
 def span_first(half, ctx_count, span_rows):
     ctx_index = lax.axis_index("ctx")
     return (ctx_index if half == 0 else 2 * ctx_count - 1 - ctx_index) * span_rows
+
+
+def tile_count(tiles_ref, half):
+    return jnp.max(tiles_ref[half]).astype(jnp.int32)
 
 
 def prepare_kernel(
@@ -57,8 +61,6 @@
     lengths_copy.start()
     same_ref[...] = line_ref[...]
     zero_ref[...] = jnp.zeros_like(zero_ref)
-    lane = lax.broadcasted_iota(jnp.int32, tiles_ref.shape, 1)
-    tiles = jnp.zeros(tiles_ref.shape, jnp.int32)
     lengths_copy.wait()
     for half in range(2):
         first = span_first(half, ctx_count, span_rows)
@@ -74,8 +76,7 @@
             first_key = jnp.where(first >= end, end, first_key)
         starts_ref[half] = doc_start
         count = (first + span_rows - first_key + tile - 1) // tile
-        tiles = jnp.where(lane == half, count, tiles)
-    tiles_ref[...] = tiles
+        tiles_ref[half] = jnp.full(tiles_ref.shape[1:], count.astype(jnp.float32))
     for slot, copy in enumerate(copies):
         copy.wait()
         for half in range(2):
@@ -120,7 +121,7 @@
     refs = refs[piece_count:]
     keys_ref, dlogits_ref, acc_ref = refs[:3]
     dkv_refs = refs[3 : piece_count + 3]
-    values_ref, terms_ref, dweights_ref, tops_ref, counts_ref, sem = refs[piece_count + 3 :]
+    values_ref, terms_ref, dweights_ref, tops_ref = refs[piece_count + 3 :]
     cols, head_width = stack_ref.shape[2:]
     tok_rows = (keys_ref.shape[0] - tile) // ctx_count
     part_rows = tok_rows // dp_count
@@ -128,8 +129,6 @@
     scale = head_width ** (-0.5)
     ctx_index = lax.axis_index("ctx")
     dp_index = lax.axis_index("dp")
-    count_copy = pltpu.make_async_copy(tiles_ref, counts_ref, sem)
-    count_copy.start()
 
     def rows_of(row, owner, start):
         position = row_position(owner, start, ctx_count, part_rows, span_rows)
@@ -146,7 +145,6 @@
         key_rows, value_rows, ordered = rows_of(*place)
         keys_ref[ordered, :] = kv_refs[piece][key_rows, :]
         values_ref[ordered, :] = kv_refs[piece][value_rows, :]
-    count_copy.wait()
     group = min(256, cols)
     groups = [slice(start, start + group) for start in range(0, cols, group)]
 
@@ -156,14 +154,14 @@
             lax.broadcasted_iota(jnp.int32, (1, group), 1), jnp.int32(span_rows)
         )
         doc_start = starts_ref[half]
-        count = counts_ref[0, half]
+        count = tile_count(tiles_ref, half)
 
         def tile_rows(index):
             position = first + span_rows - (index + 1) * tile
             rows = pl.ds(pl.multiple_of(tile + position, span_rows), tile)
             return position, rows, pl.ds(pl.multiple_of(index * tile, tile), tile)
 
-        def sums_step(index, state, diagonal=False):
+        def sums_step(index, state):
             position, rows, slot = tile_rows(index)
             key_block, value_block = keys_ref[rows, :], values_ref[rows, :]
             all_logits = [
@@ -181,9 +179,9 @@
                 groups, all_logits, all_dweights, state
             ):
                 key_pos = lax.broadcasted_iota(jnp.int32, logits.shape, 0)
-                live = key_pos >= doc_start[:, lanes] - position
-                if diagonal:
-                    live = live & (key_pos <= query_pos - position)
+                live = (key_pos >= doc_start[:, lanes] - position) & (
+                    key_pos <= query_pos - position
+                )
                 logits = jnp.where(live, logits * (scale * math.log2(math.e)), masked_value)
                 new_top = jnp.maximum(top, jnp.max(logits, axis=0, keepdims=True))
                 terms = jnp.exp2(logits - new_top)
@@ -202,8 +200,7 @@
 
         zero = jnp.zeros((1, group), jnp.float32)
         empty = (jnp.full_like(zero, masked_value), zero, zero)
-        sums = sums_step(0, (empty,) * len(groups), diagonal=True)
-        sums = lax.fori_loop(1, count, sums_step, sums)
+        sums = lax.fori_loop(0, count, sums_step, (empty,) * len(groups))
         top, total, mixed = (jnp.concatenate(part, axis=1) for part in zip(*sums))
         inverse = 1.0 / total
         delta = mixed * inverse
@@ -247,17 +244,12 @@
     dq_ref,
     same_ref,
     sum_ref,
-    counts_ref,
-    sem,
 ):
     tok_rows = dq_ref.shape[0]
     head_width = keys_ref.shape[1]
     span_rows = tok_rows // 2
     scale = head_width ** (-0.5)
-    count_copy = pltpu.make_async_copy(tiles_ref, counts_ref, sem)
-    count_copy.start()
     same_ref[...] = passed_ref[...]
-    count_copy.wait()
     for half in range(2):
         end = span_first(half, ctx_count, span_rows) + span_rows
         sum_ref[...] = jnp.zeros_like(sum_ref)
@@ -273,7 +265,7 @@
             )
             return carry
 
-        lax.fori_loop(0, counts_ref[0, half], query_step, 0)
+        lax.fori_loop(0, tile_count(tiles_ref, half), query_step, 0)
         grads = (scale * sum_ref[...]).T.astype(jnp.bfloat16)
         for head in range(dq_ref.shape[1] // head_width):
             dq_ref[
@@ -294,7 +286,7 @@
             jax.ShapeDtypeStruct((2, 2, cols, head_width), jnp.bfloat16),
             jax.ShapeDtypeStruct((2, 2, head_width, cols), jnp.bfloat16),
             jax.ShapeDtypeStruct((2, 1, cols), jnp.int32),
-            jax.ShapeDtypeStruct((8, 128), jnp.int32),
+            jax.ShapeDtypeStruct((2, 8, 128), jnp.float32),
             jax.ShapeDtypeStruct((2, tile + ctx_count * tok_rows, head_width), jnp.float32),
             jax.ShapeDtypeStruct(line.shape, line.dtype),
         ),
@@ -330,8 +322,6 @@
             pltpu.VMEM((slots * tile, cols), jnp.float32),
             pltpu.VMEM((slots * tile, cols), jnp.float32),
             pltpu.VMEM((slots, cols), jnp.float32),
-            pltpu.SMEM((8, 128), jnp.int32),
-            pltpu.SemaphoreType.DMA,
         ],
         input_output_aliases={4: 2},
         compiler_params=pltpu.CompilerParams(vmem_limit_bytes=32 * 1024 * 1024),
@@ -354,8 +344,6 @@
         out_specs=(vmem, vmem),
         scratch_shapes=[
             pltpu.VMEM((head_width, cols), jnp.float32),
-            pltpu.SMEM((8, 128), jnp.int32),
-            pltpu.SemaphoreType.DMA,
         ],
         compiler_params=pltpu.CompilerParams(vmem_limit_bytes=8 * 1024 * 1024),
     )(tiles, keys_ordered, dlogits, passed)
@@ -388,11 +376,11 @@
 
 def paired_line(keys, values, inner, part_rows):
     head_width = keys.shape[1]
+    lowest = jnp.array(-jnp.inf, keys.dtype)
     halves = (2, 1, part_rows, head_width)
-    own = jnp.where(
-        lax.broadcasted_iota(jnp.int32, (2, 2, part_rows, head_width), 1) == 0,
-        keys.reshape(halves),
-        values.reshape(halves),
+    own = jnp.maximum(
+        lax.pad(keys.reshape(halves), lowest, ((0, 0, 0), (0, 1, 0), (0, 0, 0), (0, 0, 0))),
+        lax.pad(values.reshape(halves), lowest, ((0, 0, 0), (1, 0, 0), (0, 0, 0), (0, 0, 0))),
     ).reshape(4 * part_rows, head_width)
     rows = 2 * part_rows
     own_half = lax.dynamic_slice_in_dim(own, lax.axis_index("dp") * rows, rows, 0)

time: 44.5 us -> 44.9 us (level); the launches traced: 44.5 us -> 44 us
    select_n x1 -> x0, other arithmetic: 0.87 us -> none  [paired_line(): jnp.where(lax.broadcasted_iota(jnp.int32, (2, 2, part_rows, head_width),...]
    max x0 -> x1, other arithmetic: none -> 0.79 us  [paired_line(): jnp.maximum(lax.pad(keys.reshape(halves), lowest, ((0, 0, 0), (0, 1, 0),...]
  transfers between devices with their start and end apart: 19 -> 19, of which waited for: 11 -> 10; matrix products, arithmetic and copies ran while one was open for 0% -> 0% of each run, Pallas kernels for 7% -> 7%
where the time goes in v5:
time: 44.9 us; the launch traced here: 44 us
  starting transfers between devices  19.4 us (43%)
  waiting for transfers between devices  16.8 us (37%)
  Pallas kernels  5.48 us (12%)
  other arithmetic  1.04 us (2%)
  between operations  0.71 us (2%)
  local copies, waits for them, and re-layouts  0.63 us (1%)
    ppermute x18, waiting for transfers between devices, swap(): return lax.ppermute(value, axis, pairs)  16.8 us
    ppermute x18, starting transfers between devices, swap(): return lax.ppermute(value, axis, pairs)  16.3 us
    ppermute x1, starting transfers between devices, paired_line(): whole = lax.ppermute(own, ('ctx', 'dp'), pairs)  3.08 us
    pallas_call x1, Pallas kernels, attend(): pl.pallas_call(functools.partial(attend_kernel, ctx_count, dp_count, inne...  2.51 us
    pallas_call x1, Pallas kernels, query_side(): pl.pallas_call(functools.partial(query_kernel, ctx_count, tile), out_shap...  1.72 us
    pallas_call x1, Pallas kernels, prepare(): pl.pallas_call(functools.partial(prepare_kernel, ctx_count, tile), out_sh...  1.25 us
  transfers between devices with their start and end apart: 19, of which 10 were waited for; matrix products, arithmetic and copies ran while one was open for 0% of the time, Pallas kernels for 7%

profile of v5, /device:TPU:0, one launch (start us, length us, event | category | flops | bytes accessed | tf_op | source)
XLA Modules:
  0.0 44.0 jit_solution(4689224218019134678)
XLA Ops:
  0.6 0.8 %pad_maximum_fusion.1 = bf16[2,2,64,128]{3,2,1,0:T(8,128)(2,1)S(1)} fusion(bf16[2,1,64,128]{3,2,1,0:T(8,128)(2,1)} %bitcast.9, bf16[2,1,64,128]{3,2,1,0:T(8,128)(2,1)} %bitcast.10), kind=kLoop, calls=%fused_computation.7 | loop fusion | flops 32768 | bytes 131072 | tf_op jit(solution)/shard_map/max | solution.py:381
  1.4 3.1 %collective-permute-start.1 = (bf16[256,128]{1,0:T(8,128)(2,1)S(1)}, bf16[256,128]{1,0:T(8,128)(2,1)S(1)}, u32[]{:S(2)}, u32[]{:S(2)}) collective-permute-start(bf16[256,128]{1,0:T(8,128)(2,1)S(1)} %bitcast.7), channel_id=1, source_target_pairs={{0,8},{1,25},{2,10},{3,27},{4,12},{5,29},{6,14},{7,31},{8,0},{9,17... | collective-permute-start | bytes 196616 | tf_op jit(solution)/shard_map/ppermute | solution.py:392
  4.5 2.6 %collective-permute-start = (bf16[128,128]{1,0:T(8,128)(2,1)S(1)}, bf16[128,128]{1,0:T(8,128)(2,1)S(1)}, u32[]{:S(2)}, u32[]{:S(2)}) collective-permute-start(bf16[128,128]{1,0:T(8,128)(2,1)S(1)} %constant_dynamic-slice_fusion), channel_id=1, source_target_pairs={{0,16},{2,18},{4,20},{6,22},{8,24},{10,26},{12,28},{14,30},{16,0},... | collective-permute-start | bytes 98312 | tf_op jit(solution)/shard_map/ppermute | solution.py:354
  7.1 2.4 %collective-permute-done = bf16[128,128]{1,0:T(8,128)(2,1)S(1)} collective-permute-done((bf16[128,128]{1,0:T(8,128)(2,1)S(1)}, bf16[128,128]{1,0:T(8,128)(2,1)S(1)}, u32[]{:S(2)}, u32[]{:S(2)}) %collective-permute-start) | collective-permute-done | bytes 32800 | tf_op jit(solution)/shard_map/ppermute | solution.py:354
  9.5 2.5 %collective-permute-start.4 = (bf16[512,128]{1,0:T(8,128)(2,1)S(1)}, bf16[512,128]{1,0:T(8,128)(2,1)S(1)}, u32[]{:S(2)}, u32[]{:S(2)}) collective-permute-start(bf16[512,128]{1,0:T(8,128)(2,1)S(1)} %pad_maximum_fusion.line_ref), channel_id=1, source_target_pairs={{0,6},{2,4},{4,2},{6,0},{8,14},{10,12},{12,10},{14,8},{16,22},{18,... | collective-permute-start | bytes 393224 | tf_op jit(solution)/shard_map/ppermute | solution.py:354
  12.0 0.5 %collective-permute-start.3 = (bf16[512,128]{1,0:T(8,128)(2,1)S(1)}, bf16[512,128]{1,0:T(8,128)(2,1)S(1)}, u32[]{:S(2)}, u32[]{:S(2)}) collective-permute-start(bf16[512,128]{1,0:T(8,128)(2,1)S(1)} %pad_maximum_fusion.line_ref), channel_id=1, source_target_pairs={{0,4},{2,6},{4,0},{6,2},{8,12},{10,14},{12,8},{14,10},{16,20},{18,... | collective-permute-start | bytes 393224 | tf_op jit(solution)/shard_map/ppermute | solution.py:354
  12.5 0.5 %collective-permute-start.2 = (bf16[512,128]{1,0:T(8,128)(2,1)S(1)}, bf16[512,128]{1,0:T(8,128)(2,1)S(1)}, u32[]{:S(2)}, u32[]{:S(2)}) collective-permute-start(bf16[512,128]{1,0:T(8,128)(2,1)S(1)} %pad_maximum_fusion.line_ref), channel_id=1, source_target_pairs={{0,2},{2,0},{4,6},{6,4},{8,10},{10,8},{12,14},{14,12},{16,18},{18,... | collective-permute-start | bytes 393224 | tf_op jit(solution)/shard_map/ppermute | solution.py:354
  13.0 1.3 %shard_map.76 = (bf16[2,2,512,128]{3,2,1,0:T(8,128)(2,1)S(1)}, bf16[2,2,128,512]{3,2,1,0:T(8,128)(2,1)S(1)}, s32[2,1,512]{2,1,0:T(1,128)S(1)}, f32[2,8,128]{2,1,...) custom-call(s32[8]{0:T(128)} %lengths_hbm.1, bf16[128,1024]{1,0:T(8,128)(2,1)} %q_hbm.1, ...), custom_call_target="tpu_custom_call" | custom-call | tf_op jit(solution)/shard_map/pallas_call | solution.py:283
  14.4 2.3 %collective-permute-done.4.refs_3_ = bf16[512,128]{1,0:T(8,128)(2,1)S(1)} collective-permute-done((bf16[512,128]{1,0:T(8,128)(2,1)S(1)}, bf16[512,128]{1,0:T(8,128)(2,1)S(1)}, u32[]{:S(2)}, u32[]{:S(2)}) %collective-permute-start.4) | collective-permute-done | bytes 131104 | tf_op jit(solution)/shard_map/ppermute | solution.py:354
  16.7 2.6 %collective-permute-done.3.refs_2_ = bf16[512,128]{1,0:T(8,128)(2,1)S(1)} collective-permute-done((bf16[512,128]{1,0:T(8,128)(2,1)S(1)}, bf16[512,128]{1,0:T(8,128)(2,1)S(1)}, u32[]{:S(2)}, u32[]{:S(2)}) %collective-permute-start.3) | collective-permute-done | bytes 131104 | tf_op jit(solution)/shard_map/ppermute | solution.py:354
  19.4 0.4 collective-permute-start.6
  19.8 0.8 %collective-permute-done.7.refs_6_ = bf16[512,128]{1,0:T(8,128)(2,1)S(1)} collective-permute-done((bf16[512,128]{1,0:T(8,128)(2,1)S(1)}, bf16[512,128]{1,0:T(8,128)(2,1)S(1)}, u32[]{:S(2)}, u32[]{:S(2)}) %collective-permute-start.7) | collective-permute-done | bytes 131104 | tf_op jit(solution)/shard_map/ppermute | solution.py:354
  20.8 2.5 %shard_map.77 = (bf16[2304,128]{1,0:T(8,128)(2,1)S(1)}, bf16[2,4,2048,128]{3,2,1,0:T(8,128)(2,1)S(1)}, f32[2,2304,128]{2,1,0:T(8,128)S(1)}, bf16[512,128]{1,0:T(...) custom-call(f32[2,8,128]{2,1,0:T(8,128)S(1)} %get-tuple-element.21.t, ...), custom_call_target="tpu_custom_call", output_to_operand_aliasing={{2}: (4, {})} | custom-call | tf_op jit(solution)/shard_map/pallas_call | solution.py:308
  24.8 1.1 %collective-permute-start.11 = (bf16[512,128]{1,0:T(8,128)(2,1)S(1)}, bf16[512,128]{1,0:T(8,128)(2,1)S(1)}, u32[]{:S(2)}, u32[]{:S(2)}) collective-permute-start(bf16[512,128]{1,0:T(8,128)(2,1)S(1)} %add_convert_fusion.3), channel_id=1, source_target_pairs={{0,6},{2,4},{4,2},{6,0},{8,14},{10,12},{12,10},{14,8},{16,22},{18,... | collective-permute-start | bytes 393224 | tf_op jit(solution)/shard_map/ppermute | solution.py:354
  25.9 2.0 %collective-permute-start.13 = (bf16[512,128]{1,0:T(8,128)(2,1)S(1)}, bf16[512,128]{1,0:T(8,128)(2,1)S(1)}, u32[]{:S(2)}, u32[]{:S(2)}) collective-permute-start(bf16[512,128]{1,0:T(8,128)(2,1)S(1)} %add_convert_fusion.2), channel_id=1, source_target_pairs={{0,4},{2,6},{4,0},{6,2},{8,12},{10,14},{12,8},{14,10},{16,20},{18,... | collective-permute-start | bytes 393224 | tf_op jit(solution)/shard_map/ppermute | solution.py:354
  28.0 0.6 %collective-permute-start.15 = (bf16[512,128]{1,0:T(8,128)(2,1)S(1)}, bf16[512,128]{1,0:T(8,128)(2,1)S(1)}, u32[]{:S(2)}, u32[]{:S(2)}) collective-permute-start(bf16[512,128]{1,0:T(8,128)(2,1)S(1)} %add_convert_fusion.1), channel_id=1, source_target_pairs={{0,2},{2,0},{4,6},{6,4},{8,10},{10,8},{12,14},{14,12},{16,18},{18,... | collective-permute-start | bytes 393224 | tf_op jit(solution)/shard_map/ppermute | solution.py:354
  28.6 1.7 %shard_map.78 = (bf16[128,1024]{1,0:T(8,128)(2,1)}, bf16[512,128]{1,0:T(8,128)(2,1)S(1)}) custom-call(f32[2,8,128]{2,1,0:T(8,128)S(1)} %get-tuple-element.21.tiles_ref, bf16[2304,128]{1,0:T(8,128)(2,1)S(1)} %get-tuple-element.27.keys_ref, bf16[2,4,2048,128]{3,2,1,0:T(8,128)(2,1)S(1)} %get-tuple-element.28.dlogits_ref, ...), custom_call_target="tpu_custom_call" | custom-call | tf_op jit(solution)/shard_map/pallas_call | solution.py:335
  30.3 1.8 %collective-permute-done.11 = bf16[512,128]{1,0:T(8,128)(2,1)S(1)} collective-permute-done((bf16[512,128]{1,0:T(8,128)(2,1)S(1)}, bf16[512,128]{1,0:T(8,128)(2,1)S(1)}, u32[]{:S(2)}, u32[]{:S(2)}) %collective-permute-start.11) | collective-permute-done | bytes 131104 | tf_op jit(solution)/shard_map/ppermute | solution.py:354
  32.1 2.2 %collective-permute-done.13 = bf16[512,128]{1,0:T(8,128)(2,1)S(1)} collective-permute-done((bf16[512,128]{1,0:T(8,128)(2,1)S(1)}, bf16[512,128]{1,0:T(8,128)(2,1)S(1)}, u32[]{:S(2)}, u32[]{:S(2)}) %collective-permute-start.13) | collective-permute-done | bytes 131104 | tf_op jit(solution)/shard_map/ppermute | solution.py:354
  34.4 4.2 %collective-permute-start.16 = (bf16[128,128]{1,0:T(8,128)(2,1)S(1)}, bf16[128,128]{1,0:T(8,128)(2,1)S(1)}, u32[]{:S(2)}, u32[]{:S(2)}) collective-permute-start(bf16[128,128]{1,0:T(8,128)(2,1)S(1)} %get-tuple-element.39), channel_id=1, source_target_pairs={{0,24},{2,26},{4,28},{6,30},{8,16},{10,18},{12,20},{14,22},{16,8},... | collective-permute-start | bytes 98312 | tf_op jit(solution)/shard_map/ppermute | solution.py:354
  38.6 0.6 %collective-permute-start.17 = (bf16[128,128]{1,0:T(8,128)(2,1)S(1)}, bf16[128,128]{1,0:T(8,128)(2,1)S(1)}, u32[]{:S(2)}, u32[]{:S(2)}) collective-permute-start(bf16[128,128]{1,0:T(8,128)(2,1)S(1)} %get-tuple-element.41), channel_id=1, source_target_pairs={{0,8},{2,10},{4,12},{6,14},{8,0},{10,2},{12,4},{14,6},{16,24},{18,... | collective-permute-start | bytes 98312 | tf_op jit(solution)/shard_map/ppermute | solution.py:354
  39.2 1.3 %collective-permute-done.16 = bf16[128,128]{1,0:T(8,128)(2,1)S(1)} collective-permute-done((bf16[128,128]{1,0:T(8,128)(2,1)S(1)}, bf16[128,128]{1,0:T(8,128)(2,1)S(1)}, u32[]{:S(2)}, u32[]{:S(2)}) %collective-permute-start.16) | collective-permute-done | bytes 32800 | tf_op jit(solution)/shard_map/ppermute | solution.py:354
  40.5 2.9 %collective-permute-done.18 = bf16[128,128]{1,0:T(8,128)(2,1)S(1)} collective-permute-done((bf16[128,128]{1,0:T(8,128)(2,1)S(1)}, bf16[128,128]{1,0:T(8,128)(2,1)S(1)}, u32[]{:S(2)}, u32[]{:S(2)}) %collective-permute-start.18) | collective-permute-done | bytes 32800 | tf_op jit(solution)/shard_map/ppermute | solution.py:354
  43.4 0.6 %fusion.1 = (bf16[64,128]{1,0:T(8,128)(2,1)}, bf16[64,128]{1,0:T(8,128)(2,1)}) fusion(bf16[128,128]{1,0:T(8,128)(2,1)S(1)} %add_convert_fusion.5), kind=kLoop, calls=%fused_computation.10 | loop fusion | bytes 65536 | tf_op jit(solution)/shard_map/slice | solution.py:437
  (28 shorter events, 2.1 us)
Async XLA Ops:
  1.4 8.1 %collective-permute-start.1 = (bf16[256,128]{1,0:T(8,128)(2,1)S(1)}, bf16[256,128]{1,0:T(8,128)(2,1)S(1)}, u32[]{:S(2)}, u32[]{:S(2)}) collective-permute-start(bf16[256,128]{1,0:T(8,128)(2,1)S(1)} %bitcast.7), channel_id=1, source_target_pairs={{0,8},{1,25},{2,10},{3,27},{4,12},{5,29},{6,14},{7,31},{8,0},{9,17... | collective-permute-start | bytes 196616 | tf_op jit(solution)/shard_map/ppermute | solution.py:392
  4.5 5.0 %collective-permute-start = (bf16[128,128]{1,0:T(8,128)(2,1)S(1)}, bf16[128,128]{1,0:T(8,128)(2,1)S(1)}, u32[]{:S(2)}, u32[]{:S(2)}) collective-permute-start(bf16[128,128]{1,0:T(8,128)(2,1)S(1)} %constant_dynamic-slice_fusion), channel_id=1, source_target_pairs={{0,16},{2,18},{4,20},{6,22},{8,24},{10,26},{12,28},{14,30},{16,0},... | collective-permute-start | bytes 98312 | tf_op jit(solution)/shard_map/ppermute | solution.py:354
  9.5 7.2 %collective-permute-start.4 = (bf16[512,128]{1,0:T(8,128)(2,1)S(1)}, bf16[512,128]{1,0:T(8,128)(2,1)S(1)}, u32[]{:S(2)}, u32[]{:S(2)}) collective-permute-start(bf16[512,128]{1,0:T(8,128)(2,1)S(1)} %pad_maximum_fusion.line_ref), channel_id=1, source_target_pairs={{0,6},{2,4},{4,2},{6,0},{8,14},{10,12},{12,10},{14,8},{16,22},{18,... | collective-permute-start | bytes 393224 | tf_op jit(solution)/shard_map/ppermute | solution.py:354
  12.0 7.3 %collective-permute-start.3 = (bf16[512,128]{1,0:T(8,128)(2,1)S(1)}, bf16[512,128]{1,0:T(8,128)(2,1)S(1)}, u32[]{:S(2)}, u32[]{:S(2)}) collective-permute-start(bf16[512,128]{1,0:T(8,128)(2,1)S(1)} %pad_maximum_fusion.line_ref), channel_id=1, source_target_pairs={{0,4},{2,6},{4,0},{6,2},{8,12},{10,14},{12,8},{14,10},{16,20},{18,... | collective-permute-start | bytes 393224 | tf_op jit(solution)/shard_map/ppermute | solution.py:354
  12.5 6.9 %collective-permute-start.2 = (bf16[512,128]{1,0:T(8,128)(2,1)S(1)}, bf16[512,128]{1,0:T(8,128)(2,1)S(1)}, u32[]{:S(2)}, u32[]{:S(2)}) collective-permute-start(bf16[512,128]{1,0:T(8,128)(2,1)S(1)} %pad_maximum_fusion.line_ref), channel_id=1, source_target_pairs={{0,2},{2,0},{4,6},{6,4},{8,10},{10,8},{12,14},{14,12},{16,18},{18,... | collective-permute-start | bytes 393224 | tf_op jit(solution)/shard_map/ppermute | solution.py:354
  14.3 5.5 %collective-permute-start.5 = (bf16[512,128]{1,0:T(8,128)(2,1)S(1)}, bf16[512,128]{1,0:T(8,128)(2,1)S(1)}, u32[]{:S(2)}, u32[]{:S(2)}) collective-permute-start(bf16[512,128]{1,0:T(8,128)(2,1)S(1)} %get-tuple-element.26.refs_0_), channel_id=1, source_target_pairs={{0,1},{1,0},{2,3},{3,2},{4,5},{5,4},{6,7},{7,6},{8,9},{9,8},{10,11... | collective-permute-start | bytes 393224 | tf_op jit(solution)/shard_map/ppermute | solution.py:354
  16.7 3.1 %collective-permute-start.8 = (bf16[512,128]{1,0:T(8,128)(2,1)S(1)}, bf16[512,128]{1,0:T(8,128)(2,1)S(1)}, u32[]{:S(2)}, u32[]{:S(2)}) collective-permute-start(bf16[512,128]{1,0:T(8,128)(2,1)S(1)} %collective-permute-done.4.refs_3_), channel_id=1, source_target_pairs={{0,1},{1,0},{2,3},{3,2},{4,5},{5,4},{6,7},{7,6},{8,9},{9,8},{10,11... | collective-permute-start | bytes 393224 | tf_op jit(solution)/shard_map/ppermute | solution.py:354
  19.3 1.3 %collective-permute-start.7 = (bf16[512,128]{1,0:T(8,128)(2,1)S(1)}, bf16[512,128]{1,0:T(8,128)(2,1)S(1)}, u32[]{:S(2)}, u32[]{:S(2)}) collective-permute-start(bf16[512,128]{1,0:T(8,128)(2,1)S(1)} %collective-permute-done.3.refs_2_), channel_id=1, source_target_pairs={{0,1},{1,0},{2,3},{3,2},{4,5},{5,4},{6,7},{7,6},{8,9},{9,8},{10,11... | collective-permute-start | bytes 393224 | tf_op jit(solution)/shard_map/ppermute | solution.py:354
  19.4 1.4 %collective-permute-start.6 = (bf16[512,128]{1,0:T(8,128)(2,1)S(1)}, bf16[512,128]{1,0:T(8,128)(2,1)S(1)}, u32[]{:S(2)}, u32[]{:S(2)}) collective-permute-start(bf16[512,128]{1,0:T(8,128)(2,1)S(1)} %collective-permute-done.2.refs_1_), channel_id=1, source_target_pairs={{0,1},{1,0},{2,3},{3,2},{4,5},{5,4},{6,7},{7,6},{8,9},{9,8},{10,11... | collective-permute-start | bytes 393224 | tf_op jit(solution)/shard_map/ppermute | solution.py:354
  23.3 1.4 %collective-permute-start.10 = (bf16[512,128]{1,0:T(8,128)(2,1)S(1)}, bf16[512,128]{1,0:T(8,128)(2,1)S(1)}, u32[]{:S(2)}, u32[]{:S(2)}) collective-permute-start(bf16[512,128]{1,0:T(8,128)(2,1)S(1)} %get-tuple-element.34), channel_id=1, source_target_pairs={{0,1},{1,0},{2,3},{3,2},{4,5},{5,4},{6,7},{7,6},{8,9},{9,8},{10,11... | collective-permute-start | bytes 393224 | tf_op jit(solution)/shard_map/ppermute | solution.py:354
  23.7 4.8 %collective-permute-start.9 = (bf16[512,128]{1,0:T(8,128)(2,1)S(1)}, bf16[512,128]{1,0:T(8,128)(2,1)S(1)}, u32[]{:S(2)}, u32[]{:S(2)}) collective-permute-start(bf16[512,128]{1,0:T(8,128)(2,1)S(1)} %get-tuple-element.30), channel_id=1, source_target_pairs={{0,1},{1,0},{2,3},{3,2},{4,5},{5,4},{6,7},{7,6},{8,9},{9,8},{10,11... | collective-permute-start | bytes 393224 | tf_op jit(solution)/shard_map/ppermute | solution.py:354
  23.9 2.0 %collective-permute-start.12 = (bf16[512,128]{1,0:T(8,128)(2,1)S(1)}, bf16[512,128]{1,0:T(8,128)(2,1)S(1)}, u32[]{:S(2)}, u32[]{:S(2)}) collective-permute-start(bf16[512,128]{1,0:T(8,128)(2,1)S(1)} %get-tuple-element.36), channel_id=1, source_target_pairs={{0,1},{1,0},{2,3},{3,2},{4,5},{5,4},{6,7},{7,6},{8,9},{9,8},{10,11... | collective-permute-start | bytes 393224 | tf_op jit(solution)/shard_map/ppermute | solution.py:354
  24.2 3.7 %collective-permute-start.14 = (bf16[512,128]{1,0:T(8,128)(2,1)S(1)}, bf16[512,128]{1,0:T(8,128)(2,1)S(1)}, u32[]{:S(2)}, u32[]{:S(2)}) collective-permute-start(bf16[512,128]{1,0:T(8,128)(2,1)S(1)} %get-tuple-element.38), channel_id=1, source_target_pairs={{0,1},{1,0},{2,3},{3,2},{4,5},{5,4},{6,7},{7,6},{8,9},{9,8},{10,11... | collective-permute-start | bytes 393224 | tf_op jit(solution)/shard_map/ppermute | solution.py:354
  24.8 7.3 %collective-permute-start.11 = (bf16[512,128]{1,0:T(8,128)(2,1)S(1)}, bf16[512,128]{1,0:T(8,128)(2,1)S(1)}, u32[]{:S(2)}, u32[]{:S(2)}) collective-permute-start(bf16[512,128]{1,0:T(8,128)(2,1)S(1)} %add_convert_fusion.3), channel_id=1, source_target_pairs={{0,6},{2,4},{4,2},{6,0},{8,14},{10,12},{12,10},{14,8},{16,22},{18,... | collective-permute-start | bytes 393224 | tf_op jit(solution)/shard_map/ppermute | solution.py:354
  25.9 8.3 %collective-permute-start.13 = (bf16[512,128]{1,0:T(8,128)(2,1)S(1)}, bf16[512,128]{1,0:T(8,128)(2,1)S(1)}, u32[]{:S(2)}, u32[]{:S(2)}) collective-permute-start(bf16[512,128]{1,0:T(8,128)(2,1)S(1)} %add_convert_fusion.2), channel_id=1, source_target_pairs={{0,4},{2,6},{4,0},{6,2},{8,12},{10,14},{12,8},{14,10},{16,20},{18,... | collective-permute-start | bytes 393224 | tf_op jit(solution)/shard_map/ppermute | solution.py:354
  28.0 6.3 %collective-permute-start.15 = (bf16[512,128]{1,0:T(8,128)(2,1)S(1)}, bf16[512,128]{1,0:T(8,128)(2,1)S(1)}, u32[]{:S(2)}, u32[]{:S(2)}) collective-permute-start(bf16[512,128]{1,0:T(8,128)(2,1)S(1)} %add_convert_fusion.1), channel_id=1, source_target_pairs={{0,2},{2,0},{4,6},{6,4},{8,10},{10,8},{12,14},{14,12},{16,18},{18,... | collective-permute-start | bytes 393224 | tf_op jit(solution)/shard_map/ppermute | solution.py:354
  34.4 6.1 %collective-permute-start.16 = (bf16[128,128]{1,0:T(8,128)(2,1)S(1)}, bf16[128,128]{1,0:T(8,128)(2,1)S(1)}, u32[]{:S(2)}, u32[]{:S(2)}) collective-permute-start(bf16[128,128]{1,0:T(8,128)(2,1)S(1)} %get-tuple-element.39), channel_id=1, source_target_pairs={{0,24},{2,26},{4,28},{6,30},{8,16},{10,18},{12,20},{14,22},{16,8},... | collective-permute-start | bytes 98312 | tf_op jit(solution)/shard_map/ppermute | solution.py:354
  38.6 4.8 %collective-permute-start.18 = (bf16[128,128]{1,0:T(8,128)(2,1)S(1)}, bf16[128,128]{1,0:T(8,128)(2,1)S(1)}, u32[]{:S(2)}, u32[]{:S(2)}) collective-permute-start(bf16[128,128]{1,0:T(8,128)(2,1)S(1)} %get-tuple-element.40), channel_id=1, source_target_pairs={{0,16},{2,18},{4,20},{6,22},{8,24},{10,26},{12,28},{14,30},{16,0},... | collective-permute-start | bytes 98312 | tf_op jit(solution)/shard_map/ppermute | solution.py:354
  38.6 4.8 %collective-permute-start.17 = (bf16[128,128]{1,0:T(8,128)(2,1)S(1)}, bf16[128,128]{1,0:T(8,128)(2,1)S(1)}, u32[]{:S(2)}, u32[]{:S(2)}) collective-permute-start(bf16[128,128]{1,0:T(8,128)(2,1)S(1)} %get-tuple-element.41), channel_id=1, source_target_pairs={{0,8},{2,10},{4,12},{6,14},{8,0},{10,2},{12,4},{14,6},{16,24},{18,... | collective-permute-start | bytes 98312 | tf_op jit(solution)/shard_map/ppermute | solution.py:354

commit v6 on v5

--- a/solution.py
+++ b/solution.py
@@ -400,7 +400,7 @@
     outer = ctx_count // inner
     tok_rows, head_width = keys.shape
     part_rows = tok_rows // dp_count
-    tile = math.gcd(256, ctx_count * tok_rows)
+    tile = math.gcd(128, ctx_count * tok_rows)
     if outer == 4 and dp_count == 2:
         line = paired_line(keys, values, inner, part_rows)
         moves = functools.partial(paired_moves, inner, part_rows)

time: 44.9 us -> 44.5 us (level); the launches traced: 44 us -> 44.8 us
  Pallas kernels: 5.48 us -> 10.6 us
  waiting for transfers between devices: 16.8 us -> 12.8 us
    ppermute x18, waiting for transfers between devices: 16.8 us -> 12.8 us  [swap(): return lax.ppermute(value, axis, pairs)]
    pallas_call x1, Pallas kernels: 2.51 us -> 5.91 us  [attend(): pl.pallas_call(functools.partial(attend_kernel, ctx_count, dp_count, inne...]
    pallas_call x1, Pallas kernels: 1.72 us -> 3.43 us  [query_side(): pl.pallas_call(functools.partial(query_kernel, ctx_count, tile), out_shap...]
  transfers between devices with their start and end apart: 19 -> 19, of which waited for: 10 -> 10; matrix products, arithmetic and copies ran while one was open for 0% -> 0% of each run, Pallas kernels for 7% -> 10%
where the time goes in v6:
time: 44.5 us; the launch traced here: 44.8 us
  starting transfers between devices  19 us (43%)
  waiting for transfers between devices  12.8 us (29%)
  Pallas kernels  10.6 us (24%)
  other arithmetic  1.04 us (2%)
  between operations  0.72 us (2%)
  local copies, waits for them, and re-layouts  0.63 us (1%)
    ppermute x18, starting transfers between devices, swap(): return lax.ppermute(value, axis, pairs)  15.9 us
    ppermute x18, waiting for transfers between devices, swap(): return lax.ppermute(value, axis, pairs)  12.8 us
    pallas_call x1, Pallas kernels, attend(): pl.pallas_call(functools.partial(attend_kernel, ctx_count, dp_count, inne...  5.91 us
    pallas_call x1, Pallas kernels, query_side(): pl.pallas_call(functools.partial(query_kernel, ctx_count, tile), out_shap...  3.43 us
    ppermute x1, starting transfers between devices, paired_line(): whole = lax.ppermute(own, ('ctx', 'dp'), pairs)  3.08 us
    pallas_call x1, Pallas kernels, prepare(): pl.pallas_call(functools.partial(prepare_kernel, ctx_count, tile), out_sh...  1.25 us
  transfers between devices with their start and end apart: 19, of which 10 were waited for; matrix products, arithmetic and copies ran while one was open for 0% of the time, Pallas kernels for 10%

profile of v6, /device:TPU:0, one launch (start us, length us, event | category | flops | bytes accessed | tf_op | source)
XLA Modules:
  0.0 44.8 jit_solution(3899444902872917511)
XLA Ops:
  0.6 0.8 %pad_maximum_fusion.1 = bf16[2,2,64,128]{3,2,1,0:T(8,128)(2,1)S(1)} fusion(bf16[2,1,64,128]{3,2,1,0:T(8,128)(2,1)} %bitcast.9, bf16[2,1,64,128]{3,2,1,0:T(8,128)(2,1)} %bitcast.10), kind=kLoop, calls=%fused_computation.7 | loop fusion | flops 32768 | bytes 131072 | tf_op jit(solution)/shard_map/max | solution.py:381
  1.4 3.1 %collective-permute-start.1 = (bf16[256,128]{1,0:T(8,128)(2,1)S(1)}, bf16[256,128]{1,0:T(8,128)(2,1)S(1)}, u32[]{:S(2)}, u32[]{:S(2)}) collective-permute-start(bf16[256,128]{1,0:T(8,128)(2,1)S(1)} %bitcast.7), channel_id=1, source_target_pairs={{0,8},{1,25},{2,10},{3,27},{4,12},{5,29},{6,14},{7,31},{8,0},{9,17... | collective-permute-start | bytes 196616 | tf_op jit(solution)/shard_map/ppermute | solution.py:392
  4.5 2.6 %collective-permute-start = (bf16[128,128]{1,0:T(8,128)(2,1)S(1)}, bf16[128,128]{1,0:T(8,128)(2,1)S(1)}, u32[]{:S(2)}, u32[]{:S(2)}) collective-permute-start(bf16[128,128]{1,0:T(8,128)(2,1)S(1)} %constant_dynamic-slice_fusion), channel_id=1, source_target_pairs={{0,16},{2,18},{4,20},{6,22},{8,24},{10,26},{12,28},{14,30},{16,0},... | collective-permute-start | bytes 98312 | tf_op jit(solution)/shard_map/ppermute | solution.py:354
  7.1 2.4 %collective-permute-done = bf16[128,128]{1,0:T(8,128)(2,1)S(1)} collective-permute-done((bf16[128,128]{1,0:T(8,128)(2,1)S(1)}, bf16[128,128]{1,0:T(8,128)(2,1)S(1)}, u32[]{:S(2)}, u32[]{:S(2)}) %collective-permute-start) | collective-permute-done | bytes 32800 | tf_op jit(solution)/shard_map/ppermute | solution.py:354
  9.5 2.5 %collective-permute-start.4 = (bf16[512,128]{1,0:T(8,128)(2,1)S(1)}, bf16[512,128]{1,0:T(8,128)(2,1)S(1)}, u32[]{:S(2)}, u32[]{:S(2)}) collective-permute-start(bf16[512,128]{1,0:T(8,128)(2,1)S(1)} %pad_maximum_fusion.line_ref), channel_id=1, source_target_pairs={{0,6},{2,4},{4,2},{6,0},{8,14},{10,12},{12,10},{14,8},{16,22},{18,... | collective-permute-start | bytes 393224 | tf_op jit(solution)/shard_map/ppermute | solution.py:354
  12.0 0.5 %collective-permute-start.3 = (bf16[512,128]{1,0:T(8,128)(2,1)S(1)}, bf16[512,128]{1,0:T(8,128)(2,1)S(1)}, u32[]{:S(2)}, u32[]{:S(2)}) collective-permute-start(bf16[512,128]{1,0:T(8,128)(2,1)S(1)} %pad_maximum_fusion.line_ref), channel_id=1, source_target_pairs={{0,4},{2,6},{4,0},{6,2},{8,12},{10,14},{12,8},{14,10},{16,20},{18,... | collective-permute-start | bytes 393224 | tf_op jit(solution)/shard_map/ppermute | solution.py:354
  12.5 0.5 %collective-permute-start.2 = (bf16[512,128]{1,0:T(8,128)(2,1)S(1)}, bf16[512,128]{1,0:T(8,128)(2,1)S(1)}, u32[]{:S(2)}, u32[]{:S(2)}) collective-permute-start(bf16[512,128]{1,0:T(8,128)(2,1)S(1)} %pad_maximum_fusion.line_ref), channel_id=1, source_target_pairs={{0,2},{2,0},{4,6},{6,4},{8,10},{10,8},{12,14},{14,12},{16,18},{18,... | collective-permute-start | bytes 393224 | tf_op jit(solution)/shard_map/ppermute | solution.py:354
  13.0 1.3 %shard_map.76 = (bf16[2,2,512,128]{3,2,1,0:T(8,128)(2,1)S(1)}, bf16[2,2,128,512]{3,2,1,0:T(8,128)(2,1)S(1)}, s32[2,1,512]{2,1,0:T(1,128)S(1)}, f32[2,8,128]{2,1,...) custom-call(s32[8]{0:T(128)} %lengths_hbm.1, bf16[128,1024]{1,0:T(8,128)(2,1)} %q_hbm.1, ...), custom_call_target="tpu_custom_call" | custom-call | tf_op jit(solution)/shard_map/pallas_call | solution.py:283
  14.4 2.3 %collective-permute-done.4.refs_3_ = bf16[512,128]{1,0:T(8,128)(2,1)S(1)} collective-permute-done((bf16[512,128]{1,0:T(8,128)(2,1)S(1)}, bf16[512,128]{1,0:T(8,128)(2,1)S(1)}, u32[]{:S(2)}, u32[]{:S(2)}) %collective-permute-start.4) | collective-permute-done | bytes 131104 | tf_op jit(solution)/shard_map/ppermute | solution.py:354
  16.7 2.6 %collective-permute-done.3.refs_2_ = bf16[512,128]{1,0:T(8,128)(2,1)S(1)} collective-permute-done((bf16[512,128]{1,0:T(8,128)(2,1)S(1)}, bf16[512,128]{1,0:T(8,128)(2,1)S(1)}, u32[]{:S(2)}, u32[]{:S(2)}) %collective-permute-start.3) | collective-permute-done | bytes 131104 | tf_op jit(solution)/shard_map/ppermute | solution.py:354
  19.4 0.4 collective-permute-start.6
  19.8 0.8 %collective-permute-done.7.refs_6_ = bf16[512,128]{1,0:T(8,128)(2,1)S(1)} collective-permute-done((bf16[512,128]{1,0:T(8,128)(2,1)S(1)}, bf16[512,128]{1,0:T(8,128)(2,1)S(1)}, u32[]{:S(2)}, u32[]{:S(2)}) %collective-permute-start.7) | collective-permute-done | bytes 131104 | tf_op jit(solution)/shard_map/ppermute | solution.py:354
  20.8 5.9 %shard_map.77 = (bf16[2176,128]{1,0:T(8,128)(2,1)S(1)}, bf16[2,4,2048,128]{3,2,1,0:T(8,128)(2,1)S(1)}, f32[2,2176,128]{2,1,0:T(8,128)S(1)}, bf16[512,128]{1,0:T(...) custom-call(f32[2,8,128]{2,1,0:T(8,128)S(1)} %get-tuple-element.21.t, ...), custom_call_target="tpu_custom_call", output_to_operand_aliasing={{2}: (4, {})} | custom-call | tf_op jit(solution)/shard_map/pallas_call | solution.py:308
  26.7 0.4 collective-permute-start.10
  27.8 0.3 collective-permute-done.10
  28.2 1.3 %collective-permute-start.11 = (bf16[512,128]{1,0:T(8,128)(2,1)S(1)}, bf16[512,128]{1,0:T(8,128)(2,1)S(1)}, u32[]{:S(2)}, u32[]{:S(2)}) collective-permute-start(bf16[512,128]{1,0:T(8,128)(2,1)S(1)} %add_convert_fusion.3), channel_id=1, source_target_pairs={{0,6},{2,4},{4,2},{6,0},{8,14},{10,12},{12,10},{14,8},{16,22},{18,... | collective-permute-start | bytes 393224 | tf_op jit(solution)/shard_map/ppermute | solution.py:354
  29.5 1.3 %collective-permute-start.13 = (bf16[512,128]{1,0:T(8,128)(2,1)S(1)}, bf16[512,128]{1,0:T(8,128)(2,1)S(1)}, u32[]{:S(2)}, u32[]{:S(2)}) collective-permute-start(bf16[512,128]{1,0:T(8,128)(2,1)S(1)} %add_convert_fusion.2), channel_id=1, source_target_pairs={{0,4},{2,6},{4,0},{6,2},{8,12},{10,14},{12,8},{14,10},{16,20},{18,... | collective-permute-start | bytes 393224 | tf_op jit(solution)/shard_map/ppermute | solution.py:354
  30.9 1.1 %collective-permute-start.15 = (bf16[512,128]{1,0:T(8,128)(2,1)S(1)}, bf16[512,128]{1,0:T(8,128)(2,1)S(1)}, u32[]{:S(2)}, u32[]{:S(2)}) collective-permute-start(bf16[512,128]{1,0:T(8,128)(2,1)S(1)} %add_convert_fusion.1), channel_id=1, source_target_pairs={{0,2},{2,0},{4,6},{6,4},{8,10},{10,8},{12,14},{14,12},{16,18},{18,... | collective-permute-start | bytes 393224 | tf_op jit(solution)/shard_map/ppermute | solution.py:354
  32.0 3.4 %shard_map.78 = (bf16[128,1024]{1,0:T(8,128)(2,1)}, bf16[512,128]{1,0:T(8,128)(2,1)S(1)}) custom-call(f32[2,8,128]{2,1,0:T(8,128)S(1)} %get-tuple-element.21.tiles_ref, bf16[2176,128]{1,0:T(8,128)(2,1)S(1)} %get-tuple-element.27.keys_ref, bf16[2,4,2048,128]{3,2,1,0:T(8,128)(2,1)S(1)} %get-tuple-element.28.dlogits_ref, ...), custom_call_target="tpu_custom_call" | custom-call | tf_op jit(solution)/shard_map/pallas_call | solution.py:335
  35.5 2.2 %collective-permute-done.13 = bf16[512,128]{1,0:T(8,128)(2,1)S(1)} collective-permute-done((bf16[512,128]{1,0:T(8,128)(2,1)S(1)}, bf16[512,128]{1,0:T(8,128)(2,1)S(1)}, u32[]{:S(2)}, u32[]{:S(2)}) %collective-permute-start.13) | collective-permute-done | bytes 131104 | tf_op jit(solution)/shard_map/ppermute | solution.py:354
  38.0 4.3 %collective-permute-start.17 = (bf16[128,128]{1,0:T(8,128)(2,1)S(1)}, bf16[128,128]{1,0:T(8,128)(2,1)S(1)}, u32[]{:S(2)}, u32[]{:S(2)}) collective-permute-start(bf16[128,128]{1,0:T(8,128)(2,1)S(1)} %get-tuple-element.41), channel_id=1, source_target_pairs={{0,8},{2,10},{4,12},{6,14},{8,0},{10,2},{12,4},{14,6},{16,24},{18,... | collective-permute-start | bytes 98312 | tf_op jit(solution)/shard_map/ppermute | solution.py:354
  42.2 1.4 %collective-permute-done.16 = bf16[128,128]{1,0:T(8,128)(2,1)S(1)} collective-permute-done((bf16[128,128]{1,0:T(8,128)(2,1)S(1)}, bf16[128,128]{1,0:T(8,128)(2,1)S(1)}, u32[]{:S(2)}, u32[]{:S(2)}) %collective-permute-start.16) | collective-permute-done | bytes 32800 | tf_op jit(solution)/shard_map/ppermute | solution.py:354
  43.7 0.5 %collective-permute-done.17 = bf16[128,128]{1,0:T(8,128)(2,1)S(1)} collective-permute-done((bf16[128,128]{1,0:T(8,128)(2,1)S(1)}, bf16[128,128]{1,0:T(8,128)(2,1)S(1)}, u32[]{:S(2)}, u32[]{:S(2)}) %collective-permute-start.17) | collective-permute-done | bytes 32800 | tf_op jit(solution)/shard_map/ppermute | solution.py:354
  44.2 0.6 %fusion.1 = (bf16[64,128]{1,0:T(8,128)(2,1)}, bf16[64,128]{1,0:T(8,128)(2,1)}) fusion(bf16[128,128]{1,0:T(8,128)(2,1)S(1)} %add_convert_fusion.5), kind=kLoop, calls=%fused_computation.10 | loop fusion | bytes 65536 | tf_op jit(solution)/shard_map/slice | solution.py:437
  (28 shorter events, 1.6 us)
Async XLA Ops:
  1.4 8.1 %collective-permute-start.1 = (bf16[256,128]{1,0:T(8,128)(2,1)S(1)}, bf16[256,128]{1,0:T(8,128)(2,1)S(1)}, u32[]{:S(2)}, u32[]{:S(2)}) collective-permute-start(bf16[256,128]{1,0:T(8,128)(2,1)S(1)} %bitcast.7), channel_id=1, source_target_pairs={{0,8},{1,25},{2,10},{3,27},{4,12},{5,29},{6,14},{7,31},{8,0},{9,17... | collective-permute-start | bytes 196616 | tf_op jit(solution)/shard_map/ppermute | solution.py:392
  4.5 5.0 %collective-permute-start = (bf16[128,128]{1,0:T(8,128)(2,1)S(1)}, bf16[128,128]{1,0:T(8,128)(2,1)S(1)}, u32[]{:S(2)}, u32[]{:S(2)}) collective-permute-start(bf16[128,128]{1,0:T(8,128)(2,1)S(1)} %constant_dynamic-slice_fusion), channel_id=1, source_target_pairs={{0,16},{2,18},{4,20},{6,22},{8,24},{10,26},{12,28},{14,30},{16,0},... | collective-permute-start | bytes 98312 | tf_op jit(solution)/shard_map/ppermute | solution.py:354
  9.5 7.2 %collective-permute-start.4 = (bf16[512,128]{1,0:T(8,128)(2,1)S(1)}, bf16[512,128]{1,0:T(8,128)(2,1)S(1)}, u32[]{:S(2)}, u32[]{:S(2)}) collective-permute-start(bf16[512,128]{1,0:T(8,128)(2,1)S(1)} %pad_maximum_fusion.line_ref), channel_id=1, source_target_pairs={{0,6},{2,4},{4,2},{6,0},{8,14},{10,12},{12,10},{14,8},{16,22},{18,... | collective-permute-start | bytes 393224 | tf_op jit(solution)/shard_map/ppermute | solution.py:354
  12.0 7.3 %collective-permute-start.3 = (bf16[512,128]{1,0:T(8,128)(2,1)S(1)}, bf16[512,128]{1,0:T(8,128)(2,1)S(1)}, u32[]{:S(2)}, u32[]{:S(2)}) collective-permute-start(bf16[512,128]{1,0:T(8,128)(2,1)S(1)} %pad_maximum_fusion.line_ref), channel_id=1, source_target_pairs={{0,4},{2,6},{4,0},{6,2},{8,12},{10,14},{12,8},{14,10},{16,20},{18,... | collective-permute-start | bytes 393224 | tf_op jit(solution)/shard_map/ppermute | solution.py:354
  12.5 6.9 %collective-permute-start.2 = (bf16[512,128]{1,0:T(8,128)(2,1)S(1)}, bf16[512,128]{1,0:T(8,128)(2,1)S(1)}, u32[]{:S(2)}, u32[]{:S(2)}) collective-permute-start(bf16[512,128]{1,0:T(8,128)(2,1)S(1)} %pad_maximum_fusion.line_ref), channel_id=1, source_target_pairs={{0,2},{2,0},{4,6},{6,4},{8,10},{10,8},{12,14},{14,12},{16,18},{18,... | collective-permute-start | bytes 393224 | tf_op jit(solution)/shard_map/ppermute | solution.py:354
  14.3 5.5 %collective-permute-start.5 = (bf16[512,128]{1,0:T(8,128)(2,1)S(1)}, bf16[512,128]{1,0:T(8,128)(2,1)S(1)}, u32[]{:S(2)}, u32[]{:S(2)}) collective-permute-start(bf16[512,128]{1,0:T(8,128)(2,1)S(1)} %get-tuple-element.26.refs_0_), channel_id=1, source_target_pairs={{0,1},{1,0},{2,3},{3,2},{4,5},{5,4},{6,7},{7,6},{8,9},{9,8},{10,11... | collective-permute-start | bytes 393224 | tf_op jit(solution)/shard_map/ppermute | solution.py:354
  16.7 3.1 %collective-permute-start.8 = (bf16[512,128]{1,0:T(8,128)(2,1)S(1)}, bf16[512,128]{1,0:T(8,128)(2,1)S(1)}, u32[]{:S(2)}, u32[]{:S(2)}) collective-permute-start(bf16[512,128]{1,0:T(8,128)(2,1)S(1)} %collective-permute-done.4.refs_3_), channel_id=1, source_target_pairs={{0,1},{1,0},{2,3},{3,2},{4,5},{5,4},{6,7},{7,6},{8,9},{9,8},{10,11... | collective-permute-start | bytes 393224 | tf_op jit(solution)/shard_map/ppermute | solution.py:354
  19.3 1.3 %collective-permute-start.7 = (bf16[512,128]{1,0:T(8,128)(2,1)S(1)}, bf16[512,128]{1,0:T(8,128)(2,1)S(1)}, u32[]{:S(2)}, u32[]{:S(2)}) collective-permute-start(bf16[512,128]{1,0:T(8,128)(2,1)S(1)} %collective-permute-done.3.refs_2_), channel_id=1, source_target_pairs={{0,1},{1,0},{2,3},{3,2},{4,5},{5,4},{6,7},{7,6},{8,9},{9,8},{10,11... | collective-permute-start | bytes 393224 | tf_op jit(solution)/shard_map/ppermute | solution.py:354
  19.4 1.4 %collective-permute-start.6 = (bf16[512,128]{1,0:T(8,128)(2,1)S(1)}, bf16[512,128]{1,0:T(8,128)(2,1)S(1)}, u32[]{:S(2)}, u32[]{:S(2)}) collective-permute-start(bf16[512,128]{1,0:T(8,128)(2,1)S(1)} %collective-permute-done.2.refs_1_), channel_id=1, source_target_pairs={{0,1},{1,0},{2,3},{3,2},{4,5},{5,4},{6,7},{7,6},{8,9},{9,8},{10,11... | collective-permute-start | bytes 393224 | tf_op jit(solution)/shard_map/ppermute | solution.py:354
  26.7 1.4 %collective-permute-start.10 = (bf16[512,128]{1,0:T(8,128)(2,1)S(1)}, bf16[512,128]{1,0:T(8,128)(2,1)S(1)}, u32[]{:S(2)}, u32[]{:S(2)}) collective-permute-start(bf16[512,128]{1,0:T(8,128)(2,1)S(1)} %get-tuple-element.34), channel_id=1, source_target_pairs={{0,1},{1,0},{2,3},{3,2},{4,5},{5,4},{6,7},{7,6},{8,9},{9,8},{10,11... | collective-permute-start | bytes 393224 | tf_op jit(solution)/shard_map/ppermute | solution.py:354
  27.1 4.8 %collective-permute-start.9 = (bf16[512,128]{1,0:T(8,128)(2,1)S(1)}, bf16[512,128]{1,0:T(8,128)(2,1)S(1)}, u32[]{:S(2)}, u32[]{:S(2)}) collective-permute-start(bf16[512,128]{1,0:T(8,128)(2,1)S(1)} %get-tuple-element.30), channel_id=1, source_target_pairs={{0,1},{1,0},{2,3},{3,2},{4,5},{5,4},{6,7},{7,6},{8,9},{9,8},{10,11... | collective-permute-start | bytes 393224 | tf_op jit(solution)/shard_map/ppermute | solution.py:354
  27.3 2.2 %collective-permute-start.12 = (bf16[512,128]{1,0:T(8,128)(2,1)S(1)}, bf16[512,128]{1,0:T(8,128)(2,1)S(1)}, u32[]{:S(2)}, u32[]{:S(2)}) collective-permute-start(bf16[512,128]{1,0:T(8,128)(2,1)S(1)} %get-tuple-element.36), channel_id=1, source_target_pairs={{0,1},{1,0},{2,3},{3,2},{4,5},{5,4},{6,7},{7,6},{8,9},{9,8},{10,11... | collective-permute-start | bytes 393224 | tf_op jit(solution)/shard_map/ppermute | solution.py:354
  27.6 3.2 %collective-permute-start.14 = (bf16[512,128]{1,0:T(8,128)(2,1)S(1)}, bf16[512,128]{1,0:T(8,128)(2,1)S(1)}, u32[]{:S(2)}, u32[]{:S(2)}) collective-permute-start(bf16[512,128]{1,0:T(8,128)(2,1)S(1)} %get-tuple-element.38), channel_id=1, source_target_pairs={{0,1},{1,0},{2,3},{3,2},{4,5},{5,4},{6,7},{7,6},{8,9},{9,8},{10,11... | collective-permute-start | bytes 393224 | tf_op jit(solution)/shard_map/ppermute | solution.py:354
  28.2 7.3 %collective-permute-start.11 = (bf16[512,128]{1,0:T(8,128)(2,1)S(1)}, bf16[512,128]{1,0:T(8,128)(2,1)S(1)}, u32[]{:S(2)}, u32[]{:S(2)}) collective-permute-start(bf16[512,128]{1,0:T(8,128)(2,1)S(1)} %add_convert_fusion.3), channel_id=1, source_target_pairs={{0,6},{2,4},{4,2},{6,0},{8,14},{10,12},{12,10},{14,8},{16,22},{18,... | collective-permute-start | bytes 393224 | tf_op jit(solution)/shard_map/ppermute | solution.py:354
  29.5 8.1 %collective-permute-start.13 = (bf16[512,128]{1,0:T(8,128)(2,1)S(1)}, bf16[512,128]{1,0:T(8,128)(2,1)S(1)}, u32[]{:S(2)}, u32[]{:S(2)}) collective-permute-start(bf16[512,128]{1,0:T(8,128)(2,1)S(1)} %add_convert_fusion.2), channel_id=1, source_target_pairs={{0,4},{2,6},{4,0},{6,2},{8,12},{10,14},{12,8},{14,10},{16,20},{18,... | collective-permute-start | bytes 393224 | tf_op jit(solution)/shard_map/ppermute | solution.py:354
  30.9 6.8 %collective-permute-start.15 = (bf16[512,128]{1,0:T(8,128)(2,1)S(1)}, bf16[512,128]{1,0:T(8,128)(2,1)S(1)}, u32[]{:S(2)}, u32[]{:S(2)}) collective-permute-start(bf16[512,128]{1,0:T(8,128)(2,1)S(1)} %add_convert_fusion.1), channel_id=1, source_target_pairs={{0,2},{2,0},{4,6},{6,4},{8,10},{10,8},{12,14},{14,12},{16,18},{18,... | collective-permute-start | bytes 393224 | tf_op jit(solution)/shard_map/ppermute | solution.py:354
  37.8 5.9 %collective-permute-start.16 = (bf16[128,128]{1,0:T(8,128)(2,1)S(1)}, bf16[128,128]{1,0:T(8,128)(2,1)S(1)}, u32[]{:S(2)}, u32[]{:S(2)}) collective-permute-start(bf16[128,128]{1,0:T(8,128)(2,1)S(1)} %get-tuple-element.39), channel_id=1, source_target_pairs={{0,24},{2,26},{4,28},{6,30},{8,16},{10,18},{12,20},{14,22},{16,8},... | collective-permute-start | bytes 98312 | tf_op jit(solution)/shard_map/ppermute | solution.py:354
  37.9 5.8 %collective-permute-start.18 = (bf16[128,128]{1,0:T(8,128)(2,1)S(1)}, bf16[128,128]{1,0:T(8,128)(2,1)S(1)}, u32[]{:S(2)}, u32[]{:S(2)}) collective-permute-start(bf16[128,128]{1,0:T(8,128)(2,1)S(1)} %get-tuple-element.40), channel_id=1, source_target_pairs={{0,16},{2,18},{4,20},{6,22},{8,24},{10,26},{12,28},{14,30},{16,0},... | collective-permute-start | bytes 98312 | tf_op jit(solution)/shard_map/ppermute | solution.py:354
  38.0 6.2 %collective-permute-start.17 = (bf16[128,128]{1,0:T(8,128)(2,1)S(1)}, bf16[128,128]{1,0:T(8,128)(2,1)S(1)}, u32[]{:S(2)}, u32[]{:S(2)}) collective-permute-start(bf16[128,128]{1,0:T(8,128)(2,1)S(1)} %get-tuple-element.41), channel_id=1, source_target_pairs={{0,8},{2,10},{4,12},{6,14},{8,0},{10,2},{12,4},{14,6},{16,24},{18,... | collective-permute-start | bytes 98312 | tf_op jit(solution)/shard_map/ppermute | solution.py:354

commit v7 on v5

--- a/solution.py
+++ b/solution.py
@@ -121,7 +121,7 @@
     refs = refs[piece_count:]
     keys_ref, dlogits_ref, acc_ref = refs[:3]
     dkv_refs = refs[3 : piece_count + 3]
-    values_ref, terms_ref, dweights_ref, tops_ref = refs[piece_count + 3 :]
+    values_ref, terms_ref, dweights_ref, tops_ref, stats_ref = refs[piece_count + 3 :]
     cols, head_width = stack_ref.shape[2:]
     tok_rows = (keys_ref.shape[0] - tile) // ctx_count
     part_rows = tok_rows // dp_count
@@ -147,84 +147,83 @@
         values_ref[ordered, :] = kv_refs[piece][value_rows, :]
     group = min(256, cols)
     groups = [slice(start, start + group) for start in range(0, cols, group)]
-
+    counts = [tile_count(tiles_ref, half) for half in range(2)]
+    firsts = [span_first(half, ctx_count, span_rows) for half in range(2)]
+    offset_in_span = lax.rem(
+        lax.broadcasted_iota(jnp.int32, (1, group), 1), jnp.int32(span_rows)
+    )
     for half in range(2):
-        first = span_first(half, ctx_count, span_rows)
-        query_pos = first + lax.rem(
-            lax.broadcasted_iota(jnp.int32, (1, group), 1), jnp.int32(span_rows)
+        stats_ref[half, 0:1, :] = jnp.full((1, cols), masked_value, jnp.float32)
+        stats_ref[half, 1:3, :] = jnp.zeros((2, cols), jnp.float32)
+
+    def tile_place(step):
+        half = (step >= counts[0]).astype(jnp.int32)
+        index = step - half * counts[0]
+        first = jnp.where(half == 1, firsts[1], firsts[0])
+        position = first + span_rows - (index + 1) * tile
+        rows = pl.ds(pl.multiple_of(tile + position, span_rows), tile)
+        slot = pl.ds(pl.multiple_of(step * tile, tile), tile)
+        return half, index, first, position, rows, slot
+
+    def sums_step(step, carry):
+        half, _, first, position, rows, slot = tile_place(step)
+        key_block, value_block = keys_ref[rows, :], values_ref[rows, :]
+        all_logits = [
+            jnp.dot(key_block, flip_ref[half, 0, :, lanes], preferred_element_type=jnp.float32)
+            for lanes in groups
+        ]
+        all_dweights = [
+            jnp.dot(value_block, flip_ref[half, 1, :, lanes], preferred_element_type=jnp.float32)
+            for lanes in groups
+        ]
+        for lanes, logits, dweights in zip(groups, all_logits, all_dweights):
+            top = stats_ref[half, 0:1, lanes]
+            key_pos = lax.broadcasted_iota(jnp.int32, logits.shape, 0)
+            live = (key_pos >= starts_ref[half, :, lanes] - position) & (
+                key_pos <= offset_in_span + (first - position)
+            )
+            logits = jnp.where(live, logits * (scale * math.log2(math.e)), masked_value)
+            new_top = jnp.maximum(top, jnp.max(logits, axis=0, keepdims=True))
+            terms = jnp.exp2(logits - new_top)
+            terms_ref[slot, lanes] = terms
+            dweights_ref[slot, lanes] = dweights
+            tops_ref[pl.ds(step, 1), lanes] = new_top
+            decay = jnp.exp2(top - new_top)
+            stats_ref[half, 0:1, lanes] = new_top
+            stats_ref[half, 1:2, lanes] = stats_ref[half, 1:2, lanes] * decay + jnp.sum(
+                terms, axis=0, keepdims=True
+            )
+            stats_ref[half, 2:3, lanes] = stats_ref[half, 2:3, lanes] * decay + jnp.sum(
+                terms * dweights, axis=0, keepdims=True
+            )
+        return carry
+
+    lax.fori_loop(0, counts[0] + counts[1], sums_step, 0)
+    for half in range(2):
+        inverse = 1.0 / stats_ref[half, 1:2, :]
+        stats_ref[half, 1:2, :] = inverse
+        stats_ref[half, 2:3, :] = stats_ref[half, 2:3, :] * inverse
+
+    def grads_step(step, carry):
+        half, index, _, _, rows, slot = tile_place(step)
+        top, inverse, delta = (stats_ref[half, row : row + 1, :] for row in range(3))
+        factor = jnp.exp2(tops_ref[pl.ds(step, 1), :] - top) * inverse
+        weights = terms_ref[slot, :] * factor
+        dlogits = (weights * (dweights_ref[slot, :] - delta)).astype(jnp.bfloat16)
+        kept = pl.ds(pl.multiple_of(index * tile, tile), tile)
+        for lane_block in range(cols // head_width):
+            dlogits_ref[half, lane_block, kept, :] = dlogits[
+                :, lane_block * head_width : (lane_block + 1) * head_width
+            ]
+        acc_ref[1, rows, :] += jnp.dot(
+            weights.astype(jnp.bfloat16), stack_ref[half, 1], preferred_element_type=jnp.float32
         )
-        doc_start = starts_ref[half]
-        count = tile_count(tiles_ref, half)
-
-        def tile_rows(index):
-            position = first + span_rows - (index + 1) * tile
-            rows = pl.ds(pl.multiple_of(tile + position, span_rows), tile)
-            return position, rows, pl.ds(pl.multiple_of(index * tile, tile), tile)
-
-        def sums_step(index, state):
-            position, rows, slot = tile_rows(index)
-            key_block, value_block = keys_ref[rows, :], values_ref[rows, :]
-            all_logits = [
-                jnp.dot(key_block, flip_ref[half, 0, :, lanes], preferred_element_type=jnp.float32)
-                for lanes in groups
-            ]
-            all_dweights = [
-                jnp.dot(
-                    value_block, flip_ref[half, 1, :, lanes], preferred_element_type=jnp.float32
-                )
-                for lanes in groups
-            ]
-            following = []
-            for lanes, logits, dweights, (top, total, mixed) in zip(
-                groups, all_logits, all_dweights, state
-            ):
-                key_pos = lax.broadcasted_iota(jnp.int32, logits.shape, 0)
-                live = (key_pos >= doc_start[:, lanes] - position) & (
-                    key_pos <= query_pos - position
-                )
-                logits = jnp.where(live, logits * (scale * math.log2(math.e)), masked_value)
-                new_top = jnp.maximum(top, jnp.max(logits, axis=0, keepdims=True))
-                terms = jnp.exp2(logits - new_top)
-                terms_ref[slot, lanes] = terms
-                dweights_ref[slot, lanes] = dweights
-                tops_ref[pl.ds(index, 1), lanes] = new_top
-                decay = jnp.exp2(top - new_top)
-                following.append(
-                    (
-                        new_top,
-                        total * decay + jnp.sum(terms, axis=0, keepdims=True),
-                        mixed * decay + jnp.sum(terms * dweights, axis=0, keepdims=True),
-                    )
-                )
-            return tuple(following)
-
-        zero = jnp.zeros((1, group), jnp.float32)
-        empty = (jnp.full_like(zero, masked_value), zero, zero)
-        sums = lax.fori_loop(0, count, sums_step, (empty,) * len(groups))
-        top, total, mixed = (jnp.concatenate(part, axis=1) for part in zip(*sums))
-        inverse = 1.0 / total
-        delta = mixed * inverse
-
-        def grads_step(index, carry):
-            _, rows, slot = tile_rows(index)
-            factor = jnp.exp2(tops_ref[pl.ds(index, 1), :] - top) * inverse
-            weights = terms_ref[slot, :] * factor
-            dlogits = (weights * (dweights_ref[slot, :] - delta)).astype(jnp.bfloat16)
-            for lane_block in range(cols // head_width):
-                dlogits_ref[half, lane_block, slot, :] = dlogits[
-                    :, lane_block * head_width : (lane_block + 1) * head_width
-                ]
-            acc_ref[1, rows, :] += jnp.dot(
-                weights.astype(jnp.bfloat16),
-                stack_ref[half, 1],
-                preferred_element_type=jnp.float32,
-            )
-            acc_ref[0, rows, :] += jnp.dot(
-                dlogits, stack_ref[half, 0], preferred_element_type=jnp.float32
-            )
-            return carry
-
-        lax.fori_loop(0, count, grads_step, 0)
+        acc_ref[0, rows, :] += jnp.dot(
+            dlogits, stack_ref[half, 0], preferred_element_type=jnp.float32
+        )
+        return carry
+
+    lax.fori_loop(0, counts[0] + counts[1], grads_step, 0)
 
     for piece, *place in staged_moves(
         ctx_count, dp_count, inner, part_rows, ctx_index, dp_index
@@ -305,6 +304,7 @@
     cols, head_width = stacked.shape[2:]
     seq = dp_count * inner * pieces[0].shape[0] // 2
     slots = -(-seq // tile)
+    steps = slots + -(-(seq // 2) // tile)
     results = pl.pallas_call(
         functools.partial(attend_kernel, ctx_count, dp_count, inner, tile, moves),
         out_shape=[
@@ -319,9 +319,10 @@
         out_specs=[vmem] * (3 + len(pieces)),
         scratch_shapes=[
             pltpu.VMEM((tile + seq, head_width), jnp.bfloat16),
-            pltpu.VMEM((slots * tile, cols), jnp.float32),
-            pltpu.VMEM((slots * tile, cols), jnp.float32),
-            pltpu.VMEM((slots, cols), jnp.float32),
+            pltpu.VMEM((steps * tile, cols), jnp.float32),
+            pltpu.VMEM((steps * tile, cols), jnp.float32),
+            pltpu.VMEM((steps, cols), jnp.float32),
+            pltpu.VMEM((2, 8, cols), jnp.float32),
         ],
         input_output_aliases={4: 2},
         compiler_params=pltpu.CompilerParams(vmem_limit_bytes=32 * 1024 * 1024),

time: 44.9 us -> 44.4 us (0.989); the launches traced: 44 us -> 45.1 us
  starting transfers between devices: 19.4 us -> 21.2 us
  Pallas kernels: 5.48 us -> 4.4 us
    ppermute x18, starting transfers between devices: 16.3 us -> 18.1 us  [swap(): return lax.ppermute(value, axis, pairs)]
    pallas_call x1, Pallas kernels: 2.51 us -> 1.64 us  [attend(): pl.pallas_call(functools.partial(attend_kernel, ctx_count, dp_count, inne...]
  transfers between devices with their start and end apart: 19 -> 19, of which waited for: 10 -> 11; matrix products, arithmetic and copies ran while one was open for 0% -> 0% of each run, Pallas kernels for 7% -> 6%
where the time goes in v7:
time: 44.4 us; the launch traced here: 45.1 us
  starting transfers between devices  21.2 us (48%)
  waiting for transfers between devices  17.1 us (39%)
  Pallas kernels  4.4 us (10%)
  other arithmetic  1.04 us (2%)
  between operations  0.71 us (2%)
  local copies, waits for them, and re-layouts  0.63 us (1%)
    ppermute x18, starting transfers between devices, swap(): return lax.ppermute(value, axis, pairs)  18.1 us
    ppermute x18, waiting for transfers between devices, swap(): return lax.ppermute(value, axis, pairs)  17.1 us
    ppermute x1, starting transfers between devices, paired_line(): whole = lax.ppermute(own, ('ctx', 'dp'), pairs)  3.08 us
    pallas_call x1, Pallas kernels, attend(): pl.pallas_call(functools.partial(attend_kernel, ctx_count, dp_count, inne...  1.64 us
    pallas_call x1, Pallas kernels, query_side(): pl.pallas_call(functools.partial(query_kernel, ctx_count, tile), out_shap...  1.5 us
    pallas_call x1, Pallas kernels, prepare(): pl.pallas_call(functools.partial(prepare_kernel, ctx_count, tile), out_sh...  1.25 us
  transfers between devices with their start and end apart: 19, of which 11 were waited for; matrix products, arithmetic and copies ran while one was open for 0% of the time, Pallas kernels for 6%

profile of v7, /device:TPU:0, one launch (start us, length us, event | category | flops | bytes accessed | tf_op | source)
XLA Modules:
  0.0 45.1 jit_solution(8332131198054822474)
XLA Ops:
  0.6 0.8 %pad_maximum_fusion.1 = bf16[2,2,64,128]{3,2,1,0:T(8,128)(2,1)S(1)} fusion(bf16[2,1,64,128]{3,2,1,0:T(8,128)(2,1)} %bitcast.9, bf16[2,1,64,128]{3,2,1,0:T(8,128)(2,1)} %bitcast.10), kind=kLoop, calls=%fused_computation.7 | loop fusion | flops 32768 | bytes 131072 | tf_op jit(solution)/shard_map/max | solution.py:382
  1.4 3.1 %collective-permute-start.1 = (bf16[256,128]{1,0:T(8,128)(2,1)S(1)}, bf16[256,128]{1,0:T(8,128)(2,1)S(1)}, u32[]{:S(2)}, u32[]{:S(2)}) collective-permute-start(bf16[256,128]{1,0:T(8,128)(2,1)S(1)} %bitcast.7), channel_id=1, source_target_pairs={{0,8},{1,25},{2,10},{3,27},{4,12},{5,29},{6,14},{7,31},{8,0},{9,17... | collective-permute-start | bytes 196616 | tf_op jit(solution)/shard_map/ppermute | solution.py:393
  4.5 2.6 %collective-permute-start = (bf16[128,128]{1,0:T(8,128)(2,1)S(1)}, bf16[128,128]{1,0:T(8,128)(2,1)S(1)}, u32[]{:S(2)}, u32[]{:S(2)}) collective-permute-start(bf16[128,128]{1,0:T(8,128)(2,1)S(1)} %constant_dynamic-slice_fusion), channel_id=1, source_target_pairs={{0,16},{2,18},{4,20},{6,22},{8,24},{10,26},{12,28},{14,30},{16,0},... | collective-permute-start | bytes 98312 | tf_op jit(solution)/shard_map/ppermute | solution.py:355
  7.1 2.4 %collective-permute-done = bf16[128,128]{1,0:T(8,128)(2,1)S(1)} collective-permute-done((bf16[128,128]{1,0:T(8,128)(2,1)S(1)}, bf16[128,128]{1,0:T(8,128)(2,1)S(1)}, u32[]{:S(2)}, u32[]{:S(2)}) %collective-permute-start) | collective-permute-done | bytes 32800 | tf_op jit(solution)/shard_map/ppermute | solution.py:355
  9.5 2.5 %collective-permute-start.4 = (bf16[512,128]{1,0:T(8,128)(2,1)S(1)}, bf16[512,128]{1,0:T(8,128)(2,1)S(1)}, u32[]{:S(2)}, u32[]{:S(2)}) collective-permute-start(bf16[512,128]{1,0:T(8,128)(2,1)S(1)} %pad_maximum_fusion.line_ref), channel_id=1, source_target_pairs={{0,6},{2,4},{4,2},{6,0},{8,14},{10,12},{12,10},{14,8},{16,22},{18,... | collective-permute-start | bytes 393224 | tf_op jit(solution)/shard_map/ppermute | solution.py:355
  12.0 0.5 %collective-permute-start.3 = (bf16[512,128]{1,0:T(8,128)(2,1)S(1)}, bf16[512,128]{1,0:T(8,128)(2,1)S(1)}, u32[]{:S(2)}, u32[]{:S(2)}) collective-permute-start(bf16[512,128]{1,0:T(8,128)(2,1)S(1)} %pad_maximum_fusion.line_ref), channel_id=1, source_target_pairs={{0,4},{2,6},{4,0},{6,2},{8,12},{10,14},{12,8},{14,10},{16,20},{18,... | collective-permute-start | bytes 393224 | tf_op jit(solution)/shard_map/ppermute | solution.py:355
  12.5 0.5 %collective-permute-start.2 = (bf16[512,128]{1,0:T(8,128)(2,1)S(1)}, bf16[512,128]{1,0:T(8,128)(2,1)S(1)}, u32[]{:S(2)}, u32[]{:S(2)}) collective-permute-start(bf16[512,128]{1,0:T(8,128)(2,1)S(1)} %pad_maximum_fusion.line_ref), channel_id=1, source_target_pairs={{0,2},{2,0},{4,6},{6,4},{8,10},{10,8},{12,14},{14,12},{16,18},{18,... | collective-permute-start | bytes 393224 | tf_op jit(solution)/shard_map/ppermute | solution.py:355
  13.0 1.3 %shard_map.76 = (bf16[2,2,512,128]{3,2,1,0:T(8,128)(2,1)S(1)}, bf16[2,2,128,512]{3,2,1,0:T(8,128)(2,1)S(1)}, s32[2,1,512]{2,1,0:T(1,128)S(1)}, f32[2,8,128]{2,1,...) custom-call(s32[8]{0:T(128)} %lengths_hbm.1, bf16[128,1024]{1,0:T(8,128)(2,1)} %q_hbm.1, ...), custom_call_target="tpu_custom_call" | custom-call | tf_op jit(solution)/shard_map/pallas_call | solution.py:282
  14.4 2.3 %collective-permute-done.4.refs_3_ = bf16[512,128]{1,0:T(8,128)(2,1)S(1)} collective-permute-done((bf16[512,128]{1,0:T(8,128)(2,1)S(1)}, bf16[512,128]{1,0:T(8,128)(2,1)S(1)}, u32[]{:S(2)}, u32[]{:S(2)}) %collective-permute-start.4) | collective-permute-done | bytes 131104 | tf_op jit(solution)/shard_map/ppermute | solution.py:355
  16.7 2.6 %collective-permute-done.3.refs_2_ = bf16[512,128]{1,0:T(8,128)(2,1)S(1)} collective-permute-done((bf16[512,128]{1,0:T(8,128)(2,1)S(1)}, bf16[512,128]{1,0:T(8,128)(2,1)S(1)}, u32[]{:S(2)}, u32[]{:S(2)}) %collective-permute-start.3) | collective-permute-done | bytes 131104 | tf_op jit(solution)/shard_map/ppermute | solution.py:355
  19.4 0.4 collective-permute-start.6
  19.8 0.8 %collective-permute-done.7.refs_6_ = bf16[512,128]{1,0:T(8,128)(2,1)S(1)} collective-permute-done((bf16[512,128]{1,0:T(8,128)(2,1)S(1)}, bf16[512,128]{1,0:T(8,128)(2,1)S(1)}, u32[]{:S(2)}, u32[]{:S(2)}) %collective-permute-start.7) | collective-permute-done | bytes 131104 | tf_op jit(solution)/shard_map/ppermute | solution.py:355
  20.8 1.6 %shard_map.77 = (bf16[2304,128]{1,0:T(8,128)(2,1)S(1)}, bf16[2,4,2048,128]{3,2,1,0:T(8,128)(2,1)S(1)}, f32[2,2304,128]{2,1,0:T(8,128)S(1)}, bf16[512,128]{1,0:T(...) custom-call(f32[2,8,128]{2,1,0:T(8,128)S(1)} %get-tuple-element.21.t, ...), custom_call_target="tpu_custom_call", output_to_operand_aliasing={{2}: (4, {})} | custom-call | tf_op jit(solution)/shard_map/pallas_call | solution.py:308
  23.9 1.8 %collective-permute-start.11 = (bf16[512,128]{1,0:T(8,128)(2,1)S(1)}, bf16[512,128]{1,0:T(8,128)(2,1)S(1)}, u32[]{:S(2)}, u32[]{:S(2)}) collective-permute-start(bf16[512,128]{1,0:T(8,128)(2,1)S(1)} %add_convert_fusion.3), channel_id=1, source_target_pairs={{0,6},{2,4},{4,2},{6,0},{8,14},{10,12},{12,10},{14,8},{16,22},{18,... | collective-permute-start | bytes 393224 | tf_op jit(solution)/shard_map/ppermute | solution.py:355
  25.8 1.3 %collective-permute-start.13 = (bf16[512,128]{1,0:T(8,128)(2,1)S(1)}, bf16[512,128]{1,0:T(8,128)(2,1)S(1)}, u32[]{:S(2)}, u32[]{:S(2)}) collective-permute-start(bf16[512,128]{1,0:T(8,128)(2,1)S(1)} %add_convert_fusion.2), channel_id=1, source_target_pairs={{0,4},{2,6},{4,0},{6,2},{8,12},{10,14},{12,8},{14,10},{16,20},{18,... | collective-permute-start | bytes 393224 | tf_op jit(solution)/shard_map/ppermute | solution.py:355
  27.1 0.6 %collective-permute-start.15 = (bf16[512,128]{1,0:T(8,128)(2,1)S(1)}, bf16[512,128]{1,0:T(8,128)(2,1)S(1)}, u32[]{:S(2)}, u32[]{:S(2)}) collective-permute-start(bf16[512,128]{1,0:T(8,128)(2,1)S(1)} %add_convert_fusion.1), channel_id=1, source_target_pairs={{0,2},{2,0},{4,6},{6,4},{8,10},{10,8},{12,14},{14,12},{16,18},{18,... | collective-permute-start | bytes 393224 | tf_op jit(solution)/shard_map/ppermute | solution.py:355
  27.7 1.5 %shard_map.78 = (bf16[128,1024]{1,0:T(8,128)(2,1)}, bf16[512,128]{1,0:T(8,128)(2,1)S(1)}) custom-call(f32[2,8,128]{2,1,0:T(8,128)S(1)} %get-tuple-element.21.tiles_ref, bf16[2304,128]{1,0:T(8,128)(2,1)S(1)} %get-tuple-element.27.keys_ref, bf16[2,4,2048,128]{3,2,1,0:T(8,128)(2,1)S(1)} %get-tuple-element.28.dlogits_ref, ...), custom_call_target="tpu_custom_call" | custom-call | tf_op jit(solution)/shard_map/pallas_call | solution.py:336
  29.2 2.0 %collective-permute-done.11 = bf16[512,128]{1,0:T(8,128)(2,1)S(1)} collective-permute-done((bf16[512,128]{1,0:T(8,128)(2,1)S(1)}, bf16[512,128]{1,0:T(8,128)(2,1)S(1)}, u32[]{:S(2)}, u32[]{:S(2)}) %collective-permute-start.11) | collective-permute-done | bytes 131104 | tf_op jit(solution)/shard_map/ppermute | solution.py:355
  31.2 2.2 %collective-permute-done.13 = bf16[512,128]{1,0:T(8,128)(2,1)S(1)} collective-permute-done((bf16[512,128]{1,0:T(8,128)(2,1)S(1)}, bf16[512,128]{1,0:T(8,128)(2,1)S(1)}, u32[]{:S(2)}, u32[]{:S(2)}) %collective-permute-start.13) | collective-permute-done | bytes 131104 | tf_op jit(solution)/shard_map/ppermute | solution.py:355
  33.6 6.0 %collective-permute-start.16 = (bf16[128,128]{1,0:T(8,128)(2,1)S(1)}, bf16[128,128]{1,0:T(8,128)(2,1)S(1)}, u32[]{:S(2)}, u32[]{:S(2)}) collective-permute-start(bf16[128,128]{1,0:T(8,128)(2,1)S(1)} %get-tuple-element.39), channel_id=1, source_target_pairs={{0,24},{2,26},{4,28},{6,30},{8,16},{10,18},{12,20},{14,22},{16,8},... | collective-permute-start | bytes 98312 | tf_op jit(solution)/shard_map/ppermute | solution.py:355
  39.7 0.6 %collective-permute-start.17 = (bf16[128,128]{1,0:T(8,128)(2,1)S(1)}, bf16[128,128]{1,0:T(8,128)(2,1)S(1)}, u32[]{:S(2)}, u32[]{:S(2)}) collective-permute-start(bf16[128,128]{1,0:T(8,128)(2,1)S(1)} %get-tuple-element.41), channel_id=1, source_target_pairs={{0,8},{2,10},{4,12},{6,14},{8,0},{10,2},{12,4},{14,6},{16,24},{18,... | collective-permute-start | bytes 98312 | tf_op jit(solution)/shard_map/ppermute | solution.py:355
  40.3 1.3 %collective-permute-done.16 = bf16[128,128]{1,0:T(8,128)(2,1)S(1)} collective-permute-done((bf16[128,128]{1,0:T(8,128)(2,1)S(1)}, bf16[128,128]{1,0:T(8,128)(2,1)S(1)}, u32[]{:S(2)}, u32[]{:S(2)}) %collective-permute-start.16) | collective-permute-done | bytes 32800 | tf_op jit(solution)/shard_map/ppermute | solution.py:355
  41.6 2.9 %collective-permute-done.18 = bf16[128,128]{1,0:T(8,128)(2,1)S(1)} collective-permute-done((bf16[128,128]{1,0:T(8,128)(2,1)S(1)}, bf16[128,128]{1,0:T(8,128)(2,1)S(1)}, u32[]{:S(2)}, u32[]{:S(2)}) %collective-permute-start.18) | collective-permute-done | bytes 32800 | tf_op jit(solution)/shard_map/ppermute | solution.py:355
  44.5 0.6 %fusion.1 = (bf16[64,128]{1,0:T(8,128)(2,1)}, bf16[64,128]{1,0:T(8,128)(2,1)}) fusion(bf16[128,128]{1,0:T(8,128)(2,1)S(1)} %add_convert_fusion.5), kind=kLoop, calls=%fused_computation.10 | loop fusion | bytes 65536 | tf_op jit(solution)/shard_map/slice | solution.py:438
  (28 shorter events, 2.2 us)
Async XLA Ops:
  1.4 8.1 %collective-permute-start.1 = (bf16[256,128]{1,0:T(8,128)(2,1)S(1)}, bf16[256,128]{1,0:T(8,128)(2,1)S(1)}, u32[]{:S(2)}, u32[]{:S(2)}) collective-permute-start(bf16[256,128]{1,0:T(8,128)(2,1)S(1)} %bitcast.7), channel_id=1, source_target_pairs={{0,8},{1,25},{2,10},{3,27},{4,12},{5,29},{6,14},{7,31},{8,0},{9,17... | collective-permute-start | bytes 196616 | tf_op jit(solution)/shard_map/ppermute | solution.py:393
  4.5 5.0 %collective-permute-start = (bf16[128,128]{1,0:T(8,128)(2,1)S(1)}, bf16[128,128]{1,0:T(8,128)(2,1)S(1)}, u32[]{:S(2)}, u32[]{:S(2)}) collective-permute-start(bf16[128,128]{1,0:T(8,128)(2,1)S(1)} %constant_dynamic-slice_fusion), channel_id=1, source_target_pairs={{0,16},{2,18},{4,20},{6,22},{8,24},{10,26},{12,28},{14,30},{16,0},... | collective-permute-start | bytes 98312 | tf_op jit(solution)/shard_map/ppermute | solution.py:355
  9.5 7.2 %collective-permute-start.4 = (bf16[512,128]{1,0:T(8,128)(2,1)S(1)}, bf16[512,128]{1,0:T(8,128)(2,1)S(1)}, u32[]{:S(2)}, u32[]{:S(2)}) collective-permute-start(bf16[512,128]{1,0:T(8,128)(2,1)S(1)} %pad_maximum_fusion.line_ref), channel_id=1, source_target_pairs={{0,6},{2,4},{4,2},{6,0},{8,14},{10,12},{12,10},{14,8},{16,22},{18,... | collective-permute-start | bytes 393224 | tf_op jit(solution)/shard_map/ppermute | solution.py:355
  12.0 7.3 %collective-permute-start.3 = (bf16[512,128]{1,0:T(8,128)(2,1)S(1)}, bf16[512,128]{1,0:T(8,128)(2,1)S(1)}, u32[]{:S(2)}, u32[]{:S(2)}) collective-permute-start(bf16[512,128]{1,0:T(8,128)(2,1)S(1)} %pad_maximum_fusion.line_ref), channel_id=1, source_target_pairs={{0,4},{2,6},{4,0},{6,2},{8,12},{10,14},{12,8},{14,10},{16,20},{18,... | collective-permute-start | bytes 393224 | tf_op jit(solution)/shard_map/ppermute | solution.py:355
  12.5 6.9 %collective-permute-start.2 = (bf16[512,128]{1,0:T(8,128)(2,1)S(1)}, bf16[512,128]{1,0:T(8,128)(2,1)S(1)}, u32[]{:S(2)}, u32[]{:S(2)}) collective-permute-start(bf16[512,128]{1,0:T(8,128)(2,1)S(1)} %pad_maximum_fusion.line_ref), channel_id=1, source_target_pairs={{0,2},{2,0},{4,6},{6,4},{8,10},{10,8},{12,14},{14,12},{16,18},{18,... | collective-permute-start | bytes 393224 | tf_op jit(solution)/shard_map/ppermute | solution.py:355
  14.3 5.5 %collective-permute-start.5 = (bf16[512,128]{1,0:T(8,128)(2,1)S(1)}, bf16[512,128]{1,0:T(8,128)(2,1)S(1)}, u32[]{:S(2)}, u32[]{:S(2)}) collective-permute-start(bf16[512,128]{1,0:T(8,128)(2,1)S(1)} %get-tuple-element.26.refs_0_), channel_id=1, source_target_pairs={{0,1},{1,0},{2,3},{3,2},{4,5},{5,4},{6,7},{7,6},{8,9},{9,8},{10,11... | collective-permute-start | bytes 393224 | tf_op jit(solution)/shard_map/ppermute | solution.py:355
  16.7 3.1 %collective-permute-start.8 = (bf16[512,128]{1,0:T(8,128)(2,1)S(1)}, bf16[512,128]{1,0:T(8,128)(2,1)S(1)}, u32[]{:S(2)}, u32[]{:S(2)}) collective-permute-start(bf16[512,128]{1,0:T(8,128)(2,1)S(1)} %collective-permute-done.4.refs_3_), channel_id=1, source_target_pairs={{0,1},{1,0},{2,3},{3,2},{4,5},{5,4},{6,7},{7,6},{8,9},{9,8},{10,11... | collective-permute-start | bytes 393224 | tf_op jit(solution)/shard_map/ppermute | solution.py:355
  19.3 1.3 %collective-permute-start.7 = (bf16[512,128]{1,0:T(8,128)(2,1)S(1)}, bf16[512,128]{1,0:T(8,128)(2,1)S(1)}, u32[]{:S(2)}, u32[]{:S(2)}) collective-permute-start(bf16[512,128]{1,0:T(8,128)(2,1)S(1)} %collective-permute-done.3.refs_2_), channel_id=1, source_target_pairs={{0,1},{1,0},{2,3},{3,2},{4,5},{5,4},{6,7},{7,6},{8,9},{9,8},{10,11... | collective-permute-start | bytes 393224 | tf_op jit(solution)/shard_map/ppermute | solution.py:355
  19.4 1.4 %collective-permute-start.6 = (bf16[512,128]{1,0:T(8,128)(2,1)S(1)}, bf16[512,128]{1,0:T(8,128)(2,1)S(1)}, u32[]{:S(2)}, u32[]{:S(2)}) collective-permute-start(bf16[512,128]{1,0:T(8,128)(2,1)S(1)} %collective-permute-done.2.refs_1_), channel_id=1, source_target_pairs={{0,1},{1,0},{2,3},{3,2},{4,5},{5,4},{6,7},{7,6},{8,9},{9,8},{10,11... | collective-permute-start | bytes 393224 | tf_op jit(solution)/shard_map/ppermute | solution.py:355
  22.5 1.4 %collective-permute-start.10 = (bf16[512,128]{1,0:T(8,128)(2,1)S(1)}, bf16[512,128]{1,0:T(8,128)(2,1)S(1)}, u32[]{:S(2)}, u32[]{:S(2)}) collective-permute-start(bf16[512,128]{1,0:T(8,128)(2,1)S(1)} %get-tuple-element.34), channel_id=1, source_target_pairs={{0,1},{1,0},{2,3},{3,2},{4,5},{5,4},{6,7},{7,6},{8,9},{9,8},{10,11... | collective-permute-start | bytes 393224 | tf_op jit(solution)/shard_map/ppermute | solution.py:355
  22.9 4.8 %collective-permute-start.9 = (bf16[512,128]{1,0:T(8,128)(2,1)S(1)}, bf16[512,128]{1,0:T(8,128)(2,1)S(1)}, u32[]{:S(2)}, u32[]{:S(2)}) collective-permute-start(bf16[512,128]{1,0:T(8,128)(2,1)S(1)} %get-tuple-element.30), channel_id=1, source_target_pairs={{0,1},{1,0},{2,3},{3,2},{4,5},{5,4},{6,7},{7,6},{8,9},{9,8},{10,11... | collective-permute-start | bytes 393224 | tf_op jit(solution)/shard_map/ppermute | solution.py:355
  23.0 2.7 %collective-permute-start.12 = (bf16[512,128]{1,0:T(8,128)(2,1)S(1)}, bf16[512,128]{1,0:T(8,128)(2,1)S(1)}, u32[]{:S(2)}, u32[]{:S(2)}) collective-permute-start(bf16[512,128]{1,0:T(8,128)(2,1)S(1)} %get-tuple-element.36), channel_id=1, source_target_pairs={{0,1},{1,0},{2,3},{3,2},{4,5},{5,4},{6,7},{7,6},{8,9},{9,8},{10,11... | collective-permute-start | bytes 393224 | tf_op jit(solution)/shard_map/ppermute | solution.py:355
  23.4 3.7 %collective-permute-start.14 = (bf16[512,128]{1,0:T(8,128)(2,1)S(1)}, bf16[512,128]{1,0:T(8,128)(2,1)S(1)}, u32[]{:S(2)}, u32[]{:S(2)}) collective-permute-start(bf16[512,128]{1,0:T(8,128)(2,1)S(1)} %get-tuple-element.38), channel_id=1, source_target_pairs={{0,1},{1,0},{2,3},{3,2},{4,5},{5,4},{6,7},{7,6},{8,9},{9,8},{10,11... | collective-permute-start | bytes 393224 | tf_op jit(solution)/shard_map/ppermute | solution.py:355
  23.9 7.3 %collective-permute-start.11 = (bf16[512,128]{1,0:T(8,128)(2,1)S(1)}, bf16[512,128]{1,0:T(8,128)(2,1)S(1)}, u32[]{:S(2)}, u32[]{:S(2)}) collective-permute-start(bf16[512,128]{1,0:T(8,128)(2,1)S(1)} %add_convert_fusion.3), channel_id=1, source_target_pairs={{0,6},{2,4},{4,2},{6,0},{8,14},{10,12},{12,10},{14,8},{16,22},{18,... | collective-permute-start | bytes 393224 | tf_op jit(solution)/shard_map/ppermute | solution.py:355
  25.8 7.6 %collective-permute-start.13 = (bf16[512,128]{1,0:T(8,128)(2,1)S(1)}, bf16[512,128]{1,0:T(8,128)(2,1)S(1)}, u32[]{:S(2)}, u32[]{:S(2)}) collective-permute-start(bf16[512,128]{1,0:T(8,128)(2,1)S(1)} %add_convert_fusion.2), channel_id=1, source_target_pairs={{0,4},{2,6},{4,0},{6,2},{8,12},{10,14},{12,8},{14,10},{16,20},{18,... | collective-permute-start | bytes 393224 | tf_op jit(solution)/shard_map/ppermute | solution.py:355
  27.1 6.4 %collective-permute-start.15 = (bf16[512,128]{1,0:T(8,128)(2,1)S(1)}, bf16[512,128]{1,0:T(8,128)(2,1)S(1)}, u32[]{:S(2)}, u32[]{:S(2)}) collective-permute-start(bf16[512,128]{1,0:T(8,128)(2,1)S(1)} %add_convert_fusion.1), channel_id=1, source_target_pairs={{0,2},{2,0},{4,6},{6,4},{8,10},{10,8},{12,14},{14,12},{16,18},{18,... | collective-permute-start | bytes 393224 | tf_op jit(solution)/shard_map/ppermute | solution.py:355
  33.6 7.9 %collective-permute-start.16 = (bf16[128,128]{1,0:T(8,128)(2,1)S(1)}, bf16[128,128]{1,0:T(8,128)(2,1)S(1)}, u32[]{:S(2)}, u32[]{:S(2)}) collective-permute-start(bf16[128,128]{1,0:T(8,128)(2,1)S(1)} %get-tuple-element.39), channel_id=1, source_target_pairs={{0,24},{2,26},{4,28},{6,30},{8,16},{10,18},{12,20},{14,22},{16,8},... | collective-permute-start | bytes 98312 | tf_op jit(solution)/shard_map/ppermute | solution.py:355
  39.7 4.8 %collective-permute-start.18 = (bf16[128,128]{1,0:T(8,128)(2,1)S(1)}, bf16[128,128]{1,0:T(8,128)(2,1)S(1)}, u32[]{:S(2)}, u32[]{:S(2)}) collective-permute-start(bf16[128,128]{1,0:T(8,128)(2,1)S(1)} %get-tuple-element.40), channel_id=1, source_target_pairs={{0,16},{2,18},{4,20},{6,22},{8,24},{10,26},{12,28},{14,30},{16,0},... | collective-permute-start | bytes 98312 | tf_op jit(solution)/shard_map/ppermute | solution.py:355
  39.7 4.8 %collective-permute-start.17 = (bf16[128,128]{1,0:T(8,128)(2,1)S(1)}, bf16[128,128]{1,0:T(8,128)(2,1)S(1)}, u32[]{:S(2)}, u32[]{:S(2)}) collective-permute-start(bf16[128,128]{1,0:T(8,128)(2,1)S(1)} %get-tuple-element.41), channel_id=1, source_target_pairs={{0,8},{2,10},{4,12},{6,14},{8,0},{10,2},{12,4},{14,6},{16,24},{18,... | collective-permute-start | bytes 98312 | tf_op jit(solution)/shard_map/ppermute | solution.py:355

commit v8 on v7

--- a/solution.py
+++ b/solution.py
@@ -401,7 +401,7 @@
     outer = ctx_count // inner
     tok_rows, head_width = keys.shape
     part_rows = tok_rows // dp_count
-    tile = math.gcd(256, ctx_count * tok_rows)
+    tile = math.gcd(512, ctx_count * tok_rows)
     if outer == 4 and dp_count == 2:
         line = paired_line(keys, values, inner, part_rows)
         moves = functools.partial(paired_moves, inner, part_rows)

time: 44.4 us -> 43.2 us (0.973); the launches traced: 45.1 us -> 42.7 us
  waiting for transfers between devices: 17.1 us -> 14.7 us
  Pallas kernels: 4.4 us -> 5.28 us
  starting transfers between devices: 21.2 us -> 20.4 us
    ppermute x18, waiting for transfers between devices: 17.1 us -> 14.7 us  [swap(): return lax.ppermute(value, axis, pairs)]
    ppermute x18, starting transfers between devices: 18.1 us -> 17.3 us  [swap(): return lax.ppermute(value, axis, pairs)]
    pallas_call x1, Pallas kernels: 1.64 us -> 2.44 us  [attend(): pl.pallas_call(functools.partial(attend_kernel, ctx_count, dp_count, inne...]
  transfers between devices with their start and end apart: 19 -> 19, of which waited for: 11 -> 10; matrix products, arithmetic and copies ran while one was open for 0% -> 0% of each run, Pallas kernels for 6% -> 7%
where the time goes in v8:
time: 43.2 us; the launch traced here: 42.7 us
  starting transfers between devices  20.4 us (47%)
  waiting for transfers between devices  14.7 us (34%)
  Pallas kernels  5.28 us (12%)
  other arithmetic  1.05 us (2%)
  between operations  0.73 us (2%)
  local copies, waits for them, and re-layouts  0.63 us (1%)
    ppermute x18, starting transfers between devices, swap(): return lax.ppermute(value, axis, pairs)  17.3 us
    ppermute x18, waiting for transfers between devices, swap(): return lax.ppermute(value, axis, pairs)  14.7 us
    ppermute x1, starting transfers between devices, paired_line(): whole = lax.ppermute(own, ('ctx', 'dp'), pairs)  3.08 us
    pallas_call x1, Pallas kernels, attend(): pl.pallas_call(functools.partial(attend_kernel, ctx_count, dp_count, inne...  2.44 us
    pallas_call x1, Pallas kernels, query_side(): pl.pallas_call(functools.partial(query_kernel, ctx_count, tile), out_shap...  1.59 us
    pallas_call x1, Pallas kernels, prepare(): pl.pallas_call(functools.partial(prepare_kernel, ctx_count, tile), out_sh...  1.25 us
  transfers between devices with their start and end apart: 19, of which 10 were waited for; matrix products, arithmetic and copies ran while one was open for 0% of the time, Pallas kernels for 7%

profile of v8, /device:TPU:0, one launch (start us, length us, event | category | flops | bytes accessed | tf_op | source)
XLA Modules:
  0.0 42.7 jit_solution(10329713181067816451)
XLA Ops:
  0.6 0.8 %pad_maximum_fusion.1 = bf16[2,2,64,128]{3,2,1,0:T(8,128)(2,1)S(1)} fusion(bf16[2,1,64,128]{3,2,1,0:T(8,128)(2,1)} %bitcast.9, bf16[2,1,64,128]{3,2,1,0:T(8,128)(2,1)} %bitcast.10), kind=kLoop, calls=%fused_computation.7 | loop fusion | flops 32768 | bytes 131072 | tf_op jit(solution)/shard_map/max | solution.py:382
  1.4 3.1 %collective-permute-start.1 = (bf16[256,128]{1,0:T(8,128)(2,1)S(1)}, bf16[256,128]{1,0:T(8,128)(2,1)S(1)}, u32[]{:S(2)}, u32[]{:S(2)}) collective-permute-start(bf16[256,128]{1,0:T(8,128)(2,1)S(1)} %bitcast.7), channel_id=1, source_target_pairs={{0,8},{1,25},{2,10},{3,27},{4,12},{5,29},{6,14},{7,31},{8,0},{9,17... | collective-permute-start | bytes 196616 | tf_op jit(solution)/shard_map/ppermute | solution.py:393
  4.5 2.6 %collective-permute-start = (bf16[128,128]{1,0:T(8,128)(2,1)S(1)}, bf16[128,128]{1,0:T(8,128)(2,1)S(1)}, u32[]{:S(2)}, u32[]{:S(2)}) collective-permute-start(bf16[128,128]{1,0:T(8,128)(2,1)S(1)} %constant_dynamic-slice_fusion), channel_id=1, source_target_pairs={{0,16},{2,18},{4,20},{6,22},{8,24},{10,26},{12,28},{14,30},{16,0},... | collective-permute-start | bytes 98312 | tf_op jit(solution)/shard_map/ppermute | solution.py:355
  7.1 2.4 %collective-permute-done = bf16[128,128]{1,0:T(8,128)(2,1)S(1)} collective-permute-done((bf16[128,128]{1,0:T(8,128)(2,1)S(1)}, bf16[128,128]{1,0:T(8,128)(2,1)S(1)}, u32[]{:S(2)}, u32[]{:S(2)}) %collective-permute-start) | collective-permute-done | bytes 32800 | tf_op jit(solution)/shard_map/ppermute | solution.py:355
  9.5 2.5 %collective-permute-start.4 = (bf16[512,128]{1,0:T(8,128)(2,1)S(1)}, bf16[512,128]{1,0:T(8,128)(2,1)S(1)}, u32[]{:S(2)}, u32[]{:S(2)}) collective-permute-start(bf16[512,128]{1,0:T(8,128)(2,1)S(1)} %pad_maximum_fusion.line_ref), channel_id=1, source_target_pairs={{0,6},{2,4},{4,2},{6,0},{8,14},{10,12},{12,10},{14,8},{16,22},{18,... | collective-permute-start | bytes 393224 | tf_op jit(solution)/shard_map/ppermute | solution.py:355
  12.0 0.5 %collective-permute-start.3 = (bf16[512,128]{1,0:T(8,128)(2,1)S(1)}, bf16[512,128]{1,0:T(8,128)(2,1)S(1)}, u32[]{:S(2)}, u32[]{:S(2)}) collective-permute-start(bf16[512,128]{1,0:T(8,128)(2,1)S(1)} %pad_maximum_fusion.line_ref), channel_id=1, source_target_pairs={{0,4},{2,6},{4,0},{6,2},{8,12},{10,14},{12,8},{14,10},{16,20},{18,... | collective-permute-start | bytes 393224 | tf_op jit(solution)/shard_map/ppermute | solution.py:355
  12.5 0.5 %collective-permute-start.2 = (bf16[512,128]{1,0:T(8,128)(2,1)S(1)}, bf16[512,128]{1,0:T(8,128)(2,1)S(1)}, u32[]{:S(2)}, u32[]{:S(2)}) collective-permute-start(bf16[512,128]{1,0:T(8,128)(2,1)S(1)} %pad_maximum_fusion.line_ref), channel_id=1, source_target_pairs={{0,2},{2,0},{4,6},{6,4},{8,10},{10,8},{12,14},{14,12},{16,18},{18,... | collective-permute-start | bytes 393224 | tf_op jit(solution)/shard_map/ppermute | solution.py:355
  13.0 1.3 %shard_map.76 = (bf16[2,2,512,128]{3,2,1,0:T(8,128)(2,1)S(1)}, bf16[2,2,128,512]{3,2,1,0:T(8,128)(2,1)S(1)}, s32[2,1,512]{2,1,0:T(1,128)S(1)}, f32[2,8,128]{2,1,...) custom-call(s32[8]{0:T(128)} %lengths_hbm.1, bf16[128,1024]{1,0:T(8,128)(2,1)} %q_hbm.1, ...), custom_call_target="tpu_custom_call" | custom-call | tf_op jit(solution)/shard_map/pallas_call | solution.py:282
  14.4 2.3 %collective-permute-done.4.refs_3_ = bf16[512,128]{1,0:T(8,128)(2,1)S(1)} collective-permute-done((bf16[512,128]{1,0:T(8,128)(2,1)S(1)}, bf16[512,128]{1,0:T(8,128)(2,1)S(1)}, u32[]{:S(2)}, u32[]{:S(2)}) %collective-permute-start.4) | collective-permute-done | bytes 131104 | tf_op jit(solution)/shard_map/ppermute | solution.py:355
  16.7 2.6 %collective-permute-done.3.refs_2_ = bf16[512,128]{1,0:T(8,128)(2,1)S(1)} collective-permute-done((bf16[512,128]{1,0:T(8,128)(2,1)S(1)}, bf16[512,128]{1,0:T(8,128)(2,1)S(1)}, u32[]{:S(2)}, u32[]{:S(2)}) %collective-permute-start.3) | collective-permute-done | bytes 131104 | tf_op jit(solution)/shard_map/ppermute | solution.py:355
  19.4 0.4 collective-permute-start.6
  19.8 0.8 %collective-permute-done.7.refs_6_ = bf16[512,128]{1,0:T(8,128)(2,1)S(1)} collective-permute-done((bf16[512,128]{1,0:T(8,128)(2,1)S(1)}, bf16[512,128]{1,0:T(8,128)(2,1)S(1)}, u32[]{:S(2)}, u32[]{:S(2)}) %collective-permute-start.7) | collective-permute-done | bytes 131104 | tf_op jit(solution)/shard_map/ppermute | solution.py:355
  20.8 2.4 %shard_map.77 = (bf16[2560,128]{1,0:T(8,128)(2,1)S(1)}, bf16[2,4,2048,128]{3,2,1,0:T(8,128)(2,1)S(1)}, f32[2,2560,128]{2,1,0:T(8,128)S(1)}, bf16[512,128]{1,0:T(...) custom-call(f32[2,8,128]{2,1,0:T(8,128)S(1)} %get-tuple-element.21.t, ...), custom_call_target="tpu_custom_call", output_to_operand_aliasing={{2}: (4, {})} | custom-call | tf_op jit(solution)/shard_map/pallas_call | solution.py:308
  24.7 4.0 %collective-permute-start.11 = (bf16[512,128]{1,0:T(8,128)(2,1)S(1)}, bf16[512,128]{1,0:T(8,128)(2,1)S(1)}, u32[]{:S(2)}, u32[]{:S(2)}) collective-permute-start(bf16[512,128]{1,0:T(8,128)(2,1)S(1)} %add_convert_fusion.3), channel_id=1, source_target_pairs={{0,6},{2,4},{4,2},{6,0},{8,14},{10,12},{12,10},{14,8},{16,22},{18,... | collective-permute-start | bytes 393224 | tf_op jit(solution)/shard_map/ppermute | solution.py:355
  28.9 1.0 %collective-permute-start.15 = (bf16[512,128]{1,0:T(8,128)(2,1)S(1)}, bf16[512,128]{1,0:T(8,128)(2,1)S(1)}, u32[]{:S(2)}, u32[]{:S(2)}) collective-permute-start(bf16[512,128]{1,0:T(8,128)(2,1)S(1)} %add_convert_fusion.1), channel_id=1, source_target_pairs={{0,2},{2,0},{4,6},{6,4},{8,10},{10,8},{12,14},{14,12},{16,18},{18,... | collective-permute-start | bytes 393224 | tf_op jit(solution)/shard_map/ppermute | solution.py:355
  29.9 1.6 %shard_map.78 = (bf16[128,1024]{1,0:T(8,128)(2,1)}, bf16[512,128]{1,0:T(8,128)(2,1)S(1)}) custom-call(f32[2,8,128]{2,1,0:T(8,128)S(1)} %get-tuple-element.21.tiles_ref, bf16[2560,128]{1,0:T(8,128)(2,1)S(1)} %get-tuple-element.27.keys_ref, bf16[2,4,2048,128]{3,2,1,0:T(8,128)(2,1)S(1)} %get-tuple-element.28.dlogits_ref, ...), custom_call_target="tpu_custom_call" | custom-call | tf_op jit(solution)/shard_map/pallas_call | solution.py:336
  31.5 1.3 %collective-permute-done.11 = bf16[512,128]{1,0:T(8,128)(2,1)S(1)} collective-permute-done((bf16[512,128]{1,0:T(8,128)(2,1)S(1)}, bf16[512,128]{1,0:T(8,128)(2,1)S(1)}, u32[]{:S(2)}, u32[]{:S(2)}) %collective-permute-start.11) | collective-permute-done | bytes 131104 | tf_op jit(solution)/shard_map/ppermute | solution.py:355
  32.8 2.7 %collective-permute-done.13 = bf16[512,128]{1,0:T(8,128)(2,1)S(1)} collective-permute-done((bf16[512,128]{1,0:T(8,128)(2,1)S(1)}, bf16[512,128]{1,0:T(8,128)(2,1)S(1)}, u32[]{:S(2)}, u32[]{:S(2)}) %collective-permute-start.13) | collective-permute-done | bytes 131104 | tf_op jit(solution)/shard_map/ppermute | solution.py:355
  35.6 1.1 %collective-permute-start.16 = (bf16[128,128]{1,0:T(8,128)(2,1)S(1)}, bf16[128,128]{1,0:T(8,128)(2,1)S(1)}, u32[]{:S(2)}, u32[]{:S(2)}) collective-permute-start(bf16[128,128]{1,0:T(8,128)(2,1)S(1)} %get-tuple-element.39), channel_id=1, source_target_pairs={{0,24},{2,26},{4,28},{6,30},{8,16},{10,18},{12,20},{14,22},{16,8},... | collective-permute-start | bytes 98312 | tf_op jit(solution)/shard_map/ppermute | solution.py:355
  36.7 0.9 %collective-permute-start.18 = (bf16[128,128]{1,0:T(8,128)(2,1)S(1)}, bf16[128,128]{1,0:T(8,128)(2,1)S(1)}, u32[]{:S(2)}, u32[]{:S(2)}) collective-permute-start(bf16[128,128]{1,0:T(8,128)(2,1)S(1)} %get-tuple-element.40), channel_id=1, source_target_pairs={{0,16},{2,18},{4,20},{6,22},{8,24},{10,26},{12,28},{14,30},{16,0},... | collective-permute-start | bytes 98312 | tf_op jit(solution)/shard_map/ppermute | solution.py:355
  37.6 2.5 %collective-permute-start.17 = (bf16[128,128]{1,0:T(8,128)(2,1)S(1)}, bf16[128,128]{1,0:T(8,128)(2,1)S(1)}, u32[]{:S(2)}, u32[]{:S(2)}) collective-permute-start(bf16[128,128]{1,0:T(8,128)(2,1)S(1)} %get-tuple-element.41), channel_id=1, source_target_pairs={{0,8},{2,10},{4,12},{6,14},{8,0},{10,2},{12,4},{14,6},{16,24},{18,... | collective-permute-start | bytes 98312 | tf_op jit(solution)/shard_map/ppermute | solution.py:355
  40.0 1.5 %collective-permute-done.16 = bf16[128,128]{1,0:T(8,128)(2,1)S(1)} collective-permute-done((bf16[128,128]{1,0:T(8,128)(2,1)S(1)}, bf16[128,128]{1,0:T(8,128)(2,1)S(1)}, u32[]{:S(2)}, u32[]{:S(2)}) %collective-permute-start.16) | collective-permute-done | bytes 32800 | tf_op jit(solution)/shard_map/ppermute | solution.py:355
  41.6 0.5 %collective-permute-done.18 = bf16[128,128]{1,0:T(8,128)(2,1)S(1)} collective-permute-done((bf16[128,128]{1,0:T(8,128)(2,1)S(1)}, bf16[128,128]{1,0:T(8,128)(2,1)S(1)}, u32[]{:S(2)}, u32[]{:S(2)}) %collective-permute-start.18) | collective-permute-done | bytes 32800 | tf_op jit(solution)/shard_map/ppermute | solution.py:355
  42.1 0.6 %fusion.1 = (bf16[64,128]{1,0:T(8,128)(2,1)}, bf16[64,128]{1,0:T(8,128)(2,1)}) fusion(bf16[128,128]{1,0:T(8,128)(2,1)S(1)} %add_convert_fusion.5), kind=kLoop, calls=%fused_computation.10 | loop fusion | bytes 65536 | tf_op jit(solution)/shard_map/slice | solution.py:438
  (28 shorter events, 2.1 us)
Async XLA Ops:
  1.4 8.1 %collective-permute-start.1 = (bf16[256,128]{1,0:T(8,128)(2,1)S(1)}, bf16[256,128]{1,0:T(8,128)(2,1)S(1)}, u32[]{:S(2)}, u32[]{:S(2)}) collective-permute-start(bf16[256,128]{1,0:T(8,128)(2,1)S(1)} %bitcast.7), channel_id=1, source_target_pairs={{0,8},{1,25},{2,10},{3,27},{4,12},{5,29},{6,14},{7,31},{8,0},{9,17... | collective-permute-start | bytes 196616 | tf_op jit(solution)/shard_map/ppermute | solution.py:393
  4.5 5.0 %collective-permute-start = (bf16[128,128]{1,0:T(8,128)(2,1)S(1)}, bf16[128,128]{1,0:T(8,128)(2,1)S(1)}, u32[]{:S(2)}, u32[]{:S(2)}) collective-permute-start(bf16[128,128]{1,0:T(8,128)(2,1)S(1)} %constant_dynamic-slice_fusion), channel_id=1, source_target_pairs={{0,16},{2,18},{4,20},{6,22},{8,24},{10,26},{12,28},{14,30},{16,0},... | collective-permute-start | bytes 98312 | tf_op jit(solution)/shard_map/ppermute | solution.py:355
  9.5 7.2 %collective-permute-start.4 = (bf16[512,128]{1,0:T(8,128)(2,1)S(1)}, bf16[512,128]{1,0:T(8,128)(2,1)S(1)}, u32[]{:S(2)}, u32[]{:S(2)}) collective-permute-start(bf16[512,128]{1,0:T(8,128)(2,1)S(1)} %pad_maximum_fusion.line_ref), channel_id=1, source_target_pairs={{0,6},{2,4},{4,2},{6,0},{8,14},{10,12},{12,10},{14,8},{16,22},{18,... | collective-permute-start | bytes 393224 | tf_op jit(solution)/shard_map/ppermute | solution.py:355
  12.0 7.3 %collective-permute-start.3 = (bf16[512,128]{1,0:T(8,128)(2,1)S(1)}, bf16[512,128]{1,0:T(8,128)(2,1)S(1)}, u32[]{:S(2)}, u32[]{:S(2)}) collective-permute-start(bf16[512,128]{1,0:T(8,128)(2,1)S(1)} %pad_maximum_fusion.line_ref), channel_id=1, source_target_pairs={{0,4},{2,6},{4,0},{6,2},{8,12},{10,14},{12,8},{14,10},{16,20},{18,... | collective-permute-start | bytes 393224 | tf_op jit(solution)/shard_map/ppermute | solution.py:355
  12.5 6.9 %collective-permute-start.2 = (bf16[512,128]{1,0:T(8,128)(2,1)S(1)}, bf16[512,128]{1,0:T(8,128)(2,1)S(1)}, u32[]{:S(2)}, u32[]{:S(2)}) collective-permute-start(bf16[512,128]{1,0:T(8,128)(2,1)S(1)} %pad_maximum_fusion.line_ref), channel_id=1, source_target_pairs={{0,2},{2,0},{4,6},{6,4},{8,10},{10,8},{12,14},{14,12},{16,18},{18,... | collective-permute-start | bytes 393224 | tf_op jit(solution)/shard_map/ppermute | solution.py:355
  14.3 5.5 %collective-permute-start.5 = (bf16[512,128]{1,0:T(8,128)(2,1)S(1)}, bf16[512,128]{1,0:T(8,128)(2,1)S(1)}, u32[]{:S(2)}, u32[]{:S(2)}) collective-permute-start(bf16[512,128]{1,0:T(8,128)(2,1)S(1)} %get-tuple-element.26.refs_0_), channel_id=1, source_target_pairs={{0,1},{1,0},{2,3},{3,2},{4,5},{5,4},{6,7},{7,6},{8,9},{9,8},{10,11... | collective-permute-start | bytes 393224 | tf_op jit(solution)/shard_map/ppermute | solution.py:355
  16.7 3.1 %collective-permute-start.8 = (bf16[512,128]{1,0:T(8,128)(2,1)S(1)}, bf16[512,128]{1,0:T(8,128)(2,1)S(1)}, u32[]{:S(2)}, u32[]{:S(2)}) collective-permute-start(bf16[512,128]{1,0:T(8,128)(2,1)S(1)} %collective-permute-done.4.refs_3_), channel_id=1, source_target_pairs={{0,1},{1,0},{2,3},{3,2},{4,5},{5,4},{6,7},{7,6},{8,9},{9,8},{10,11... | collective-permute-start | bytes 393224 | tf_op jit(solution)/shard_map/ppermute | solution.py:355
  19.3 1.3 %collective-permute-start.7 = (bf16[512,128]{1,0:T(8,128)(2,1)S(1)}, bf16[512,128]{1,0:T(8,128)(2,1)S(1)}, u32[]{:S(2)}, u32[]{:S(2)}) collective-permute-start(bf16[512,128]{1,0:T(8,128)(2,1)S(1)} %collective-permute-done.3.refs_2_), channel_id=1, source_target_pairs={{0,1},{1,0},{2,3},{3,2},{4,5},{5,4},{6,7},{7,6},{8,9},{9,8},{10,11... | collective-permute-start | bytes 393224 | tf_op jit(solution)/shard_map/ppermute | solution.py:355
  19.4 1.4 %collective-permute-start.6 = (bf16[512,128]{1,0:T(8,128)(2,1)S(1)}, bf16[512,128]{1,0:T(8,128)(2,1)S(1)}, u32[]{:S(2)}, u32[]{:S(2)}) collective-permute-start(bf16[512,128]{1,0:T(8,128)(2,1)S(1)} %collective-permute-done.2.refs_1_), channel_id=1, source_target_pairs={{0,1},{1,0},{2,3},{3,2},{4,5},{5,4},{6,7},{7,6},{8,9},{9,8},{10,11... | collective-permute-start | bytes 393224 | tf_op jit(solution)/shard_map/ppermute | solution.py:355
  23.3 1.4 %collective-permute-start.10 = (bf16[512,128]{1,0:T(8,128)(2,1)S(1)}, bf16[512,128]{1,0:T(8,128)(2,1)S(1)}, u32[]{:S(2)}, u32[]{:S(2)}) collective-permute-start(bf16[512,128]{1,0:T(8,128)(2,1)S(1)} %get-tuple-element.34), channel_id=1, source_target_pairs={{0,1},{1,0},{2,3},{3,2},{4,5},{5,4},{6,7},{7,6},{8,9},{9,8},{10,11... | collective-permute-start | bytes 393224 | tf_op jit(solution)/shard_map/ppermute | solution.py:355
  23.7 6.2 %collective-permute-start.9 = (bf16[512,128]{1,0:T(8,128)(2,1)S(1)}, bf16[512,128]{1,0:T(8,128)(2,1)S(1)}, u32[]{:S(2)}, u32[]{:S(2)}) collective-permute-start(bf16[512,128]{1,0:T(8,128)(2,1)S(1)} %get-tuple-element.30), channel_id=1, source_target_pairs={{0,1},{1,0},{2,3},{3,2},{4,5},{5,4},{6,7},{7,6},{8,9},{9,8},{10,11... | collective-permute-start | bytes 393224 | tf_op jit(solution)/shard_map/ppermute | solution.py:355
  23.8 4.9 %collective-permute-start.12 = (bf16[512,128]{1,0:T(8,128)(2,1)S(1)}, bf16[512,128]{1,0:T(8,128)(2,1)S(1)}, u32[]{:S(2)}, u32[]{:S(2)}) collective-permute-start(bf16[512,128]{1,0:T(8,128)(2,1)S(1)} %get-tuple-element.36), channel_id=1, source_target_pairs={{0,1},{1,0},{2,3},{3,2},{4,5},{5,4},{6,7},{7,6},{8,9},{9,8},{10,11... | collective-permute-start | bytes 393224 | tf_op jit(solution)/shard_map/ppermute | solution.py:355
  24.2 4.7 %collective-permute-start.14 = (bf16[512,128]{1,0:T(8,128)(2,1)S(1)}, bf16[512,128]{1,0:T(8,128)(2,1)S(1)}, u32[]{:S(2)}, u32[]{:S(2)}) collective-permute-start(bf16[512,128]{1,0:T(8,128)(2,1)S(1)} %get-tuple-element.38), channel_id=1, source_target_pairs={{0,1},{1,0},{2,3},{3,2},{4,5},{5,4},{6,7},{7,6},{8,9},{9,8},{10,11... | collective-permute-start | bytes 393224 | tf_op jit(solution)/shard_map/ppermute | solution.py:355
  24.7 8.1 %collective-permute-start.11 = (bf16[512,128]{1,0:T(8,128)(2,1)S(1)}, bf16[512,128]{1,0:T(8,128)(2,1)S(1)}, u32[]{:S(2)}, u32[]{:S(2)}) collective-permute-start(bf16[512,128]{1,0:T(8,128)(2,1)S(1)} %add_convert_fusion.3), channel_id=1, source_target_pairs={{0,6},{2,4},{4,2},{6,0},{8,14},{10,12},{12,10},{14,8},{16,22},{18,... | collective-permute-start | bytes 393224 | tf_op jit(solution)/shard_map/ppermute | solution.py:355
  28.7 6.8 %collective-permute-start.13 = (bf16[512,128]{1,0:T(8,128)(2,1)S(1)}, bf16[512,128]{1,0:T(8,128)(2,1)S(1)}, u32[]{:S(2)}, u32[]{:S(2)}) collective-permute-start(bf16[512,128]{1,0:T(8,128)(2,1)S(1)} %add_convert_fusion.2), channel_id=1, source_target_pairs={{0,4},{2,6},{4,0},{6,2},{8,12},{10,14},{12,8},{14,10},{16,20},{18,... | collective-permute-start | bytes 393224 | tf_op jit(solution)/shard_map/ppermute | solution.py:355
  28.9 6.6 %collective-permute-start.15 = (bf16[512,128]{1,0:T(8,128)(2,1)S(1)}, bf16[512,128]{1,0:T(8,128)(2,1)S(1)}, u32[]{:S(2)}, u32[]{:S(2)}) collective-permute-start(bf16[512,128]{1,0:T(8,128)(2,1)S(1)} %add_convert_fusion.1), channel_id=1, source_target_pairs={{0,2},{2,0},{4,6},{6,4},{8,10},{10,8},{12,14},{14,12},{16,18},{18,... | collective-permute-start | bytes 393224 | tf_op jit(solution)/shard_map/ppermute | solution.py:355
  35.6 6.0 %collective-permute-start.16 = (bf16[128,128]{1,0:T(8,128)(2,1)S(1)}, bf16[128,128]{1,0:T(8,128)(2,1)S(1)}, u32[]{:S(2)}, u32[]{:S(2)}) collective-permute-start(bf16[128,128]{1,0:T(8,128)(2,1)S(1)} %get-tuple-element.39), channel_id=1, source_target_pairs={{0,24},{2,26},{4,28},{6,30},{8,16},{10,18},{12,20},{14,22},{16,8},... | collective-permute-start | bytes 98312 | tf_op jit(solution)/shard_map/ppermute | solution.py:355
  36.7 5.4 %collective-permute-start.18 = (bf16[128,128]{1,0:T(8,128)(2,1)S(1)}, bf16[128,128]{1,0:T(8,128)(2,1)S(1)}, u32[]{:S(2)}, u32[]{:S(2)}) collective-permute-start(bf16[128,128]{1,0:T(8,128)(2,1)S(1)} %get-tuple-element.40), channel_id=1, source_target_pairs={{0,16},{2,18},{4,20},{6,22},{8,24},{10,26},{12,28},{14,30},{16,0},... | collective-permute-start | bytes 98312 | tf_op jit(solution)/shard_map/ppermute | solution.py:355
  37.6 4.5 %collective-permute-start.17 = (bf16[128,128]{1,0:T(8,128)(2,1)S(1)}, bf16[128,128]{1,0:T(8,128)(2,1)S(1)}, u32[]{:S(2)}, u32[]{:S(2)}) collective-permute-start(bf16[128,128]{1,0:T(8,128)(2,1)S(1)} %get-tuple-element.41), channel_id=1, source_target_pairs={{0,8},{2,10},{4,12},{6,14},{8,0},{10,2},{12,4},{14,6},{16,24},{18,... | collective-permute-start | bytes 98312 | tf_op jit(solution)/shard_map/ppermute | solution.py:355

commit v9 on v5

--- a/solution.py
+++ b/solution.py
@@ -145,7 +145,7 @@
         key_rows, value_rows, ordered = rows_of(*place)
         keys_ref[ordered, :] = kv_refs[piece][key_rows, :]
         values_ref[ordered, :] = kv_refs[piece][value_rows, :]
-    group = min(256, cols)
+    group = min(512, cols)
     groups = [slice(start, start + group) for start in range(0, cols, group)]
 
     for half in range(2):

time: 44.9 us -> 44.2 us (0.984); the launches traced: 44 us -> 44.2 us
  Pallas kernels: 5.48 us -> 4.63 us
  starting transfers between devices: 19.4 us -> 20.1 us
    ppermute x18, starting transfers between devices: 16.3 us -> 17 us  [swap(): return lax.ppermute(value, axis, pairs)]
    pallas_call x1, Pallas kernels: 2.51 us -> 1.87 us  [attend(): pl.pallas_call(functools.partial(attend_kernel, ctx_count, dp_count, inne...]
  transfers between devices with their start and end apart: 19 -> 19, of which waited for: 10 -> 11; matrix products, arithmetic and copies ran while one was open for 0% -> 0% of each run, Pallas kernels for 7% -> 6%
where the time goes in v9:
time: 44.2 us
  starting transfers between devices  20.1 us (45%)
  waiting for transfers between devices  17.1 us (39%)
  Pallas kernels  4.63 us (10%)
  other arithmetic  1.04 us (2%)
  between operations  0.71 us (2%)
  local copies, waits for them, and re-layouts  0.63 us (1%)
    ppermute x18, waiting for transfers between devices, swap(): return lax.ppermute(value, axis, pairs)  17.1 us
    ppermute x18, starting transfers between devices, swap(): return lax.ppermute(value, axis, pairs)  17 us
    ppermute x1, starting transfers between devices, paired_line(): whole = lax.ppermute(own, ('ctx', 'dp'), pairs)  3.08 us
    pallas_call x1, Pallas kernels, attend(): pl.pallas_call(functools.partial(attend_kernel, ctx_count, dp_count, inne...  1.87 us
    pallas_call x1, Pallas kernels, query_side(): pl.pallas_call(functools.partial(query_kernel, ctx_count, tile), out_shap...  1.5 us
    pallas_call x1, Pallas kernels, prepare(): pl.pallas_call(functools.partial(prepare_kernel, ctx_count, tile), out_sh...  1.25 us
  transfers between devices with their start and end apart: 19, of which 11 were waited for; matrix products, arithmetic and copies ran while one was open for 0% of the time, Pallas kernels for 6%

profile of v9, /device:TPU:0, one launch (start us, length us, event | category | flops | bytes accessed | tf_op | source)
XLA Modules:
  0.0 44.2 jit_solution(3052507541565298105)
XLA Ops:
  0.6 0.8 %pad_maximum_fusion.1 = bf16[2,2,64,128]{3,2,1,0:T(8,128)(2,1)S(1)} fusion(bf16[2,1,64,128]{3,2,1,0:T(8,128)(2,1)} %bitcast.9, bf16[2,1,64,128]{3,2,1,0:T(8,128)(2,1)} %bitcast.10), kind=kLoop, calls=%fused_computation.7 | loop fusion | flops 32768 | bytes 131072 | tf_op jit(solution)/shard_map/max | solution.py:381
  1.4 3.1 %collective-permute-start.1 = (bf16[256,128]{1,0:T(8,128)(2,1)S(1)}, bf16[256,128]{1,0:T(8,128)(2,1)S(1)}, u32[]{:S(2)}, u32[]{:S(2)}) collective-permute-start(bf16[256,128]{1,0:T(8,128)(2,1)S(1)} %bitcast.7), channel_id=1, source_target_pairs={{0,8},{1,25},{2,10},{3,27},{4,12},{5,29},{6,14},{7,31},{8,0},{9,17... | collective-permute-start | bytes 196616 | tf_op jit(solution)/shard_map/ppermute | solution.py:392
  4.5 2.6 %collective-permute-start = (bf16[128,128]{1,0:T(8,128)(2,1)S(1)}, bf16[128,128]{1,0:T(8,128)(2,1)S(1)}, u32[]{:S(2)}, u32[]{:S(2)}) collective-permute-start(bf16[128,128]{1,0:T(8,128)(2,1)S(1)} %constant_dynamic-slice_fusion), channel_id=1, source_target_pairs={{0,16},{2,18},{4,20},{6,22},{8,24},{10,26},{12,28},{14,30},{16,0},... | collective-permute-start | bytes 98312 | tf_op jit(solution)/shard_map/ppermute | solution.py:354
  7.1 2.4 %collective-permute-done = bf16[128,128]{1,0:T(8,128)(2,1)S(1)} collective-permute-done((bf16[128,128]{1,0:T(8,128)(2,1)S(1)}, bf16[128,128]{1,0:T(8,128)(2,1)S(1)}, u32[]{:S(2)}, u32[]{:S(2)}) %collective-permute-start) | collective-permute-done | bytes 32800 | tf_op jit(solution)/shard_map/ppermute | solution.py:354
  9.5 2.5 %collective-permute-start.4 = (bf16[512,128]{1,0:T(8,128)(2,1)S(1)}, bf16[512,128]{1,0:T(8,128)(2,1)S(1)}, u32[]{:S(2)}, u32[]{:S(2)}) collective-permute-start(bf16[512,128]{1,0:T(8,128)(2,1)S(1)} %pad_maximum_fusion.line_ref), channel_id=1, source_target_pairs={{0,6},{2,4},{4,2},{6,0},{8,14},{10,12},{12,10},{14,8},{16,22},{18,... | collective-permute-start | bytes 393224 | tf_op jit(solution)/shard_map/ppermute | solution.py:354
  12.0 0.5 %collective-permute-start.3 = (bf16[512,128]{1,0:T(8,128)(2,1)S(1)}, bf16[512,128]{1,0:T(8,128)(2,1)S(1)}, u32[]{:S(2)}, u32[]{:S(2)}) collective-permute-start(bf16[512,128]{1,0:T(8,128)(2,1)S(1)} %pad_maximum_fusion.line_ref), channel_id=1, source_target_pairs={{0,4},{2,6},{4,0},{6,2},{8,12},{10,14},{12,8},{14,10},{16,20},{18,... | collective-permute-start | bytes 393224 | tf_op jit(solution)/shard_map/ppermute | solution.py:354
  12.5 0.5 %collective-permute-start.2 = (bf16[512,128]{1,0:T(8,128)(2,1)S(1)}, bf16[512,128]{1,0:T(8,128)(2,1)S(1)}, u32[]{:S(2)}, u32[]{:S(2)}) collective-permute-start(bf16[512,128]{1,0:T(8,128)(2,1)S(1)} %pad_maximum_fusion.line_ref), channel_id=1, source_target_pairs={{0,2},{2,0},{4,6},{6,4},{8,10},{10,8},{12,14},{14,12},{16,18},{18,... | collective-permute-start | bytes 393224 | tf_op jit(solution)/shard_map/ppermute | solution.py:354
  13.0 1.3 %shard_map.76 = (bf16[2,2,512,128]{3,2,1,0:T(8,128)(2,1)S(1)}, bf16[2,2,128,512]{3,2,1,0:T(8,128)(2,1)S(1)}, s32[2,1,512]{2,1,0:T(1,128)S(1)}, f32[2,8,128]{2,1,...) custom-call(s32[8]{0:T(128)} %lengths_hbm.1, bf16[128,1024]{1,0:T(8,128)(2,1)} %q_hbm.1, ...), custom_call_target="tpu_custom_call" | custom-call | tf_op jit(solution)/shard_map/pallas_call | solution.py:283
  14.4 2.3 %collective-permute-done.4.refs_3_ = bf16[512,128]{1,0:T(8,128)(2,1)S(1)} collective-permute-done((bf16[512,128]{1,0:T(8,128)(2,1)S(1)}, bf16[512,128]{1,0:T(8,128)(2,1)S(1)}, u32[]{:S(2)}, u32[]{:S(2)}) %collective-permute-start.4) | collective-permute-done | bytes 131104 | tf_op jit(solution)/shard_map/ppermute | solution.py:354
  16.7 2.6 %collective-permute-done.3.refs_2_ = bf16[512,128]{1,0:T(8,128)(2,1)S(1)} collective-permute-done((bf16[512,128]{1,0:T(8,128)(2,1)S(1)}, bf16[512,128]{1,0:T(8,128)(2,1)S(1)}, u32[]{:S(2)}, u32[]{:S(2)}) %collective-permute-start.3) | collective-permute-done | bytes 131104 | tf_op jit(solution)/shard_map/ppermute | solution.py:354
  19.4 0.4 collective-permute-start.6
  19.8 0.8 %collective-permute-done.7.refs_6_ = bf16[512,128]{1,0:T(8,128)(2,1)S(1)} collective-permute-done((bf16[512,128]{1,0:T(8,128)(2,1)S(1)}, bf16[512,128]{1,0:T(8,128)(2,1)S(1)}, u32[]{:S(2)}, u32[]{:S(2)}) %collective-permute-start.7) | collective-permute-done | bytes 131104 | tf_op jit(solution)/shard_map/ppermute | solution.py:354
  20.8 1.9 %shard_map.77 = (bf16[2304,128]{1,0:T(8,128)(2,1)S(1)}, bf16[2,4,2048,128]{3,2,1,0:T(8,128)(2,1)S(1)}, f32[2,2304,128]{2,1,0:T(8,128)S(1)}, bf16[512,128]{1,0:T(...) custom-call(f32[2,8,128]{2,1,0:T(8,128)S(1)} %get-tuple-element.21.t, ...), custom_call_target="tpu_custom_call", output_to_operand_aliasing={{2}: (4, {})} | custom-call | tf_op jit(solution)/shard_map/pallas_call | solution.py:308
  24.2 1.8 %collective-permute-start.11 = (bf16[512,128]{1,0:T(8,128)(2,1)S(1)}, bf16[512,128]{1,0:T(8,128)(2,1)S(1)}, u32[]{:S(2)}, u32[]{:S(2)}) collective-permute-start(bf16[512,128]{1,0:T(8,128)(2,1)S(1)} %add_convert_fusion.3), channel_id=1, source_target_pairs={{0,6},{2,4},{4,2},{6,0},{8,14},{10,12},{12,10},{14,8},{16,22},{18,... | collective-permute-start | bytes 393224 | tf_op jit(solution)/shard_map/ppermute | solution.py:354
  26.0 1.3 %collective-permute-start.13 = (bf16[512,128]{1,0:T(8,128)(2,1)S(1)}, bf16[512,128]{1,0:T(8,128)(2,1)S(1)}, u32[]{:S(2)}, u32[]{:S(2)}) collective-permute-start(bf16[512,128]{1,0:T(8,128)(2,1)S(1)} %add_convert_fusion.2), channel_id=1, source_target_pairs={{0,4},{2,6},{4,0},{6,2},{8,12},{10,14},{12,8},{14,10},{16,20},{18,... | collective-permute-start | bytes 393224 | tf_op jit(solution)/shard_map/ppermute | solution.py:354
  27.3 0.6 %collective-permute-start.15 = (bf16[512,128]{1,0:T(8,128)(2,1)S(1)}, bf16[512,128]{1,0:T(8,128)(2,1)S(1)}, u32[]{:S(2)}, u32[]{:S(2)}) collective-permute-start(bf16[512,128]{1,0:T(8,128)(2,1)S(1)} %add_convert_fusion.1), channel_id=1, source_target_pairs={{0,2},{2,0},{4,6},{6,4},{8,10},{10,8},{12,14},{14,12},{16,18},{18,... | collective-permute-start | bytes 393224 | tf_op jit(solution)/shard_map/ppermute | solution.py:354
  28.0 1.5 %shard_map.78 = (bf16[128,1024]{1,0:T(8,128)(2,1)}, bf16[512,128]{1,0:T(8,128)(2,1)S(1)}) custom-call(f32[2,8,128]{2,1,0:T(8,128)S(1)} %get-tuple-element.21.tiles_ref, bf16[2304,128]{1,0:T(8,128)(2,1)S(1)} %get-tuple-element.27.keys_ref, bf16[2,4,2048,128]{3,2,1,0:T(8,128)(2,1)S(1)} %get-tuple-element.28.dlogits_ref, ...), custom_call_target="tpu_custom_call" | custom-call | tf_op jit(solution)/shard_map/pallas_call | solution.py:335
  29.5 2.0 %collective-permute-done.11 = bf16[512,128]{1,0:T(8,128)(2,1)S(1)} collective-permute-done((bf16[512,128]{1,0:T(8,128)(2,1)S(1)}, bf16[512,128]{1,0:T(8,128)(2,1)S(1)}, u32[]{:S(2)}, u32[]{:S(2)}) %collective-permute-start.11) | collective-permute-done | bytes 131104 | tf_op jit(solution)/shard_map/ppermute | solution.py:354
  31.4 2.2 %collective-permute-done.13 = bf16[512,128]{1,0:T(8,128)(2,1)S(1)} collective-permute-done((bf16[512,128]{1,0:T(8,128)(2,1)S(1)}, bf16[512,128]{1,0:T(8,128)(2,1)S(1)}, u32[]{:S(2)}, u32[]{:S(2)}) %collective-permute-start.13) | collective-permute-done | bytes 131104 | tf_op jit(solution)/shard_map/ppermute | solution.py:354
  33.8 4.9 %collective-permute-start.16 = (bf16[128,128]{1,0:T(8,128)(2,1)S(1)}, bf16[128,128]{1,0:T(8,128)(2,1)S(1)}, u32[]{:S(2)}, u32[]{:S(2)}) collective-permute-start(bf16[128,128]{1,0:T(8,128)(2,1)S(1)} %get-tuple-element.39), channel_id=1, source_target_pairs={{0,24},{2,26},{4,28},{6,30},{8,16},{10,18},{12,20},{14,22},{16,8},... | collective-permute-start | bytes 98312 | tf_op jit(solution)/shard_map/ppermute | solution.py:354
  38.8 0.6 %collective-permute-start.17 = (bf16[128,128]{1,0:T(8,128)(2,1)S(1)}, bf16[128,128]{1,0:T(8,128)(2,1)S(1)}, u32[]{:S(2)}, u32[]{:S(2)}) collective-permute-start(bf16[128,128]{1,0:T(8,128)(2,1)S(1)} %get-tuple-element.41), channel_id=1, source_target_pairs={{0,8},{2,10},{4,12},{6,14},{8,0},{10,2},{12,4},{14,6},{16,24},{18,... | collective-permute-start | bytes 98312 | tf_op jit(solution)/shard_map/ppermute | solution.py:354
  39.4 1.3 %collective-permute-done.16 = bf16[128,128]{1,0:T(8,128)(2,1)S(1)} collective-permute-done((bf16[128,128]{1,0:T(8,128)(2,1)S(1)}, bf16[128,128]{1,0:T(8,128)(2,1)S(1)}, u32[]{:S(2)}, u32[]{:S(2)}) %collective-permute-start.16) | collective-permute-done | bytes 32800 | tf_op jit(solution)/shard_map/ppermute | solution.py:354
  40.7 2.9 %collective-permute-done.18 = bf16[128,128]{1,0:T(8,128)(2,1)S(1)} collective-permute-done((bf16[128,128]{1,0:T(8,128)(2,1)S(1)}, bf16[128,128]{1,0:T(8,128)(2,1)S(1)}, u32[]{:S(2)}, u32[]{:S(2)}) %collective-permute-start.18) | collective-permute-done | bytes 32800 | tf_op jit(solution)/shard_map/ppermute | solution.py:354
  43.6 0.6 %fusion.1 = (bf16[64,128]{1,0:T(8,128)(2,1)}, bf16[64,128]{1,0:T(8,128)(2,1)}) fusion(bf16[128,128]{1,0:T(8,128)(2,1)S(1)} %add_convert_fusion.5), kind=kLoop, calls=%fused_computation.10 | loop fusion | bytes 65536 | tf_op jit(solution)/shard_map/slice | solution.py:437
  (28 shorter events, 2.2 us)
Async XLA Ops:
  1.4 8.1 %collective-permute-start.1 = (bf16[256,128]{1,0:T(8,128)(2,1)S(1)}, bf16[256,128]{1,0:T(8,128)(2,1)S(1)}, u32[]{:S(2)}, u32[]{:S(2)}) collective-permute-start(bf16[256,128]{1,0:T(8,128)(2,1)S(1)} %bitcast.7), channel_id=1, source_target_pairs={{0,8},{1,25},{2,10},{3,27},{4,12},{5,29},{6,14},{7,31},{8,0},{9,17... | collective-permute-start | bytes 196616 | tf_op jit(solution)/shard_map/ppermute | solution.py:392
  4.5 5.0 %collective-permute-start = (bf16[128,128]{1,0:T(8,128)(2,1)S(1)}, bf16[128,128]{1,0:T(8,128)(2,1)S(1)}, u32[]{:S(2)}, u32[]{:S(2)}) collective-permute-start(bf16[128,128]{1,0:T(8,128)(2,1)S(1)} %constant_dynamic-slice_fusion), channel_id=1, source_target_pairs={{0,16},{2,18},{4,20},{6,22},{8,24},{10,26},{12,28},{14,30},{16,0},... | collective-permute-start | bytes 98312 | tf_op jit(solution)/shard_map/ppermute | solution.py:354
  9.5 7.2 %collective-permute-start.4 = (bf16[512,128]{1,0:T(8,128)(2,1)S(1)}, bf16[512,128]{1,0:T(8,128)(2,1)S(1)}, u32[]{:S(2)}, u32[]{:S(2)}) collective-permute-start(bf16[512,128]{1,0:T(8,128)(2,1)S(1)} %pad_maximum_fusion.line_ref), channel_id=1, source_target_pairs={{0,6},{2,4},{4,2},{6,0},{8,14},{10,12},{12,10},{14,8},{16,22},{18,... | collective-permute-start | bytes 393224 | tf_op jit(solution)/shard_map/ppermute | solution.py:354
  12.0 7.3 %collective-permute-start.3 = (bf16[512,128]{1,0:T(8,128)(2,1)S(1)}, bf16[512,128]{1,0:T(8,128)(2,1)S(1)}, u32[]{:S(2)}, u32[]{:S(2)}) collective-permute-start(bf16[512,128]{1,0:T(8,128)(2,1)S(1)} %pad_maximum_fusion.line_ref), channel_id=1, source_target_pairs={{0,4},{2,6},{4,0},{6,2},{8,12},{10,14},{12,8},{14,10},{16,20},{18,... | collective-permute-start | bytes 393224 | tf_op jit(solution)/shard_map/ppermute | solution.py:354
  12.5 6.9 %collective-permute-start.2 = (bf16[512,128]{1,0:T(8,128)(2,1)S(1)}, bf16[512,128]{1,0:T(8,128)(2,1)S(1)}, u32[]{:S(2)}, u32[]{:S(2)}) collective-permute-start(bf16[512,128]{1,0:T(8,128)(2,1)S(1)} %pad_maximum_fusion.line_ref), channel_id=1, source_target_pairs={{0,2},{2,0},{4,6},{6,4},{8,10},{10,8},{12,14},{14,12},{16,18},{18,... | collective-permute-start | bytes 393224 | tf_op jit(solution)/shard_map/ppermute | solution.py:354
  14.3 5.5 %collective-permute-start.5 = (bf16[512,128]{1,0:T(8,128)(2,1)S(1)}, bf16[512,128]{1,0:T(8,128)(2,1)S(1)}, u32[]{:S(2)}, u32[]{:S(2)}) collective-permute-start(bf16[512,128]{1,0:T(8,128)(2,1)S(1)} %get-tuple-element.26.refs_0_), channel_id=1, source_target_pairs={{0,1},{1,0},{2,3},{3,2},{4,5},{5,4},{6,7},{7,6},{8,9},{9,8},{10,11... | collective-permute-start | bytes 393224 | tf_op jit(solution)/shard_map/ppermute | solution.py:354
  16.7 3.1 %collective-permute-start.8 = (bf16[512,128]{1,0:T(8,128)(2,1)S(1)}, bf16[512,128]{1,0:T(8,128)(2,1)S(1)}, u32[]{:S(2)}, u32[]{:S(2)}) collective-permute-start(bf16[512,128]{1,0:T(8,128)(2,1)S(1)} %collective-permute-done.4.refs_3_), channel_id=1, source_target_pairs={{0,1},{1,0},{2,3},{3,2},{4,5},{5,4},{6,7},{7,6},{8,9},{9,8},{10,11... | collective-permute-start | bytes 393224 | tf_op jit(solution)/shard_map/ppermute | solution.py:354
  19.3 1.3 %collective-permute-start.7 = (bf16[512,128]{1,0:T(8,128)(2,1)S(1)}, bf16[512,128]{1,0:T(8,128)(2,1)S(1)}, u32[]{:S(2)}, u32[]{:S(2)}) collective-permute-start(bf16[512,128]{1,0:T(8,128)(2,1)S(1)} %collective-permute-done.3.refs_2_), channel_id=1, source_target_pairs={{0,1},{1,0},{2,3},{3,2},{4,5},{5,4},{6,7},{7,6},{8,9},{9,8},{10,11... | collective-permute-start | bytes 393224 | tf_op jit(solution)/shard_map/ppermute | solution.py:354
  19.4 1.4 %collective-permute-start.6 = (bf16[512,128]{1,0:T(8,128)(2,1)S(1)}, bf16[512,128]{1,0:T(8,128)(2,1)S(1)}, u32[]{:S(2)}, u32[]{:S(2)}) collective-permute-start(bf16[512,128]{1,0:T(8,128)(2,1)S(1)} %collective-permute-done.2.refs_1_), channel_id=1, source_target_pairs={{0,1},{1,0},{2,3},{3,2},{4,5},{5,4},{6,7},{7,6},{8,9},{9,8},{10,11... | collective-permute-start | bytes 393224 | tf_op jit(solution)/shard_map/ppermute | solution.py:354
  22.7 1.4 %collective-permute-start.10 = (bf16[512,128]{1,0:T(8,128)(2,1)S(1)}, bf16[512,128]{1,0:T(8,128)(2,1)S(1)}, u32[]{:S(2)}, u32[]{:S(2)}) collective-permute-start(bf16[512,128]{1,0:T(8,128)(2,1)S(1)} %get-tuple-element.34), channel_id=1, source_target_pairs={{0,1},{1,0},{2,3},{3,2},{4,5},{5,4},{6,7},{7,6},{8,9},{9,8},{10,11... | collective-permute-start | bytes 393224 | tf_op jit(solution)/shard_map/ppermute | solution.py:354
  23.1 4.8 %collective-permute-start.9 = (bf16[512,128]{1,0:T(8,128)(2,1)S(1)}, bf16[512,128]{1,0:T(8,128)(2,1)S(1)}, u32[]{:S(2)}, u32[]{:S(2)}) collective-permute-start(bf16[512,128]{1,0:T(8,128)(2,1)S(1)} %get-tuple-element.30), channel_id=1, source_target_pairs={{0,1},{1,0},{2,3},{3,2},{4,5},{5,4},{6,7},{7,6},{8,9},{9,8},{10,11... | collective-permute-start | bytes 393224 | tf_op jit(solution)/shard_map/ppermute | solution.py:354
  23.3 2.7 %collective-permute-start.12 = (bf16[512,128]{1,0:T(8,128)(2,1)S(1)}, bf16[512,128]{1,0:T(8,128)(2,1)S(1)}, u32[]{:S(2)}, u32[]{:S(2)}) collective-permute-start(bf16[512,128]{1,0:T(8,128)(2,1)S(1)} %get-tuple-element.36), channel_id=1, source_target_pairs={{0,1},{1,0},{2,3},{3,2},{4,5},{5,4},{6,7},{7,6},{8,9},{9,8},{10,11... | collective-permute-start | bytes 393224 | tf_op jit(solution)/shard_map/ppermute | solution.py:354
  23.6 3.7 %collective-permute-start.14 = (bf16[512,128]{1,0:T(8,128)(2,1)S(1)}, bf16[512,128]{1,0:T(8,128)(2,1)S(1)}, u32[]{:S(2)}, u32[]{:S(2)}) collective-permute-start(bf16[512,128]{1,0:T(8,128)(2,1)S(1)} %get-tuple-element.38), channel_id=1, source_target_pairs={{0,1},{1,0},{2,3},{3,2},{4,5},{5,4},{6,7},{7,6},{8,9},{9,8},{10,11... | collective-permute-start | bytes 393224 | tf_op jit(solution)/shard_map/ppermute | solution.py:354
  24.2 7.3 %collective-permute-start.11 = (bf16[512,128]{1,0:T(8,128)(2,1)S(1)}, bf16[512,128]{1,0:T(8,128)(2,1)S(1)}, u32[]{:S(2)}, u32[]{:S(2)}) collective-permute-start(bf16[512,128]{1,0:T(8,128)(2,1)S(1)} %add_convert_fusion.3), channel_id=1, source_target_pairs={{0,6},{2,4},{4,2},{6,0},{8,14},{10,12},{12,10},{14,8},{16,22},{18,... | collective-permute-start | bytes 393224 | tf_op jit(solution)/shard_map/ppermute | solution.py:354
  26.0 7.6 %collective-permute-start.13 = (bf16[512,128]{1,0:T(8,128)(2,1)S(1)}, bf16[512,128]{1,0:T(8,128)(2,1)S(1)}, u32[]{:S(2)}, u32[]{:S(2)}) collective-permute-start(bf16[512,128]{1,0:T(8,128)(2,1)S(1)} %add_convert_fusion.2), channel_id=1, source_target_pairs={{0,4},{2,6},{4,0},{6,2},{8,12},{10,14},{12,8},{14,10},{16,20},{18,... | collective-permute-start | bytes 393224 | tf_op jit(solution)/shard_map/ppermute | solution.py:354
  27.3 6.4 %collective-permute-start.15 = (bf16[512,128]{1,0:T(8,128)(2,1)S(1)}, bf16[512,128]{1,0:T(8,128)(2,1)S(1)}, u32[]{:S(2)}, u32[]{:S(2)}) collective-permute-start(bf16[512,128]{1,0:T(8,128)(2,1)S(1)} %add_convert_fusion.1), channel_id=1, source_target_pairs={{0,2},{2,0},{4,6},{6,4},{8,10},{10,8},{12,14},{14,12},{16,18},{18,... | collective-permute-start | bytes 393224 | tf_op jit(solution)/shard_map/ppermute | solution.py:354
  33.8 6.8 %collective-permute-start.16 = (bf16[128,128]{1,0:T(8,128)(2,1)S(1)}, bf16[128,128]{1,0:T(8,128)(2,1)S(1)}, u32[]{:S(2)}, u32[]{:S(2)}) collective-permute-start(bf16[128,128]{1,0:T(8,128)(2,1)S(1)} %get-tuple-element.39), channel_id=1, source_target_pairs={{0,24},{2,26},{4,28},{6,30},{8,16},{10,18},{12,20},{14,22},{16,8},... | collective-permute-start | bytes 98312 | tf_op jit(solution)/shard_map/ppermute | solution.py:354
  38.8 4.8 %collective-permute-start.18 = (bf16[128,128]{1,0:T(8,128)(2,1)S(1)}, bf16[128,128]{1,0:T(8,128)(2,1)S(1)}, u32[]{:S(2)}, u32[]{:S(2)}) collective-permute-start(bf16[128,128]{1,0:T(8,128)(2,1)S(1)} %get-tuple-element.40), channel_id=1, source_target_pairs={{0,16},{2,18},{4,20},{6,22},{8,24},{10,26},{12,28},{14,30},{16,0},... | collective-permute-start | bytes 98312 | tf_op jit(solution)/shard_map/ppermute | solution.py:354
  38.8 4.8 %collective-permute-start.17 = (bf16[128,128]{1,0:T(8,128)(2,1)S(1)}, bf16[128,128]{1,0:T(8,128)(2,1)S(1)}, u32[]{:S(2)}, u32[]{:S(2)}) collective-permute-start(bf16[128,128]{1,0:T(8,128)(2,1)S(1)} %get-tuple-element.41), channel_id=1, source_target_pairs={{0,8},{2,10},{4,12},{6,14},{8,0},{10,2},{12,4},{14,6},{16,24},{18,... | collective-permute-start | bytes 98312 | tf_op jit(solution)/shard_map/ppermute | solution.py:354

commit v10 on v9

--- a/solution.py
+++ b/solution.py
@@ -145,7 +145,7 @@
         key_rows, value_rows, ordered = rows_of(*place)
         keys_ref[ordered, :] = kv_refs[piece][key_rows, :]
         values_ref[ordered, :] = kv_refs[piece][value_rows, :]
-    group = min(512, cols)
+    group = min(128, cols)
     groups = [slice(start, start + group) for start in range(0, cols, group)]
 
     for half in range(2):
@@ -187,7 +187,6 @@
                 terms = jnp.exp2(logits - new_top)
                 terms_ref[slot, lanes] = terms
                 dweights_ref[slot, lanes] = dweights
-                tops_ref[pl.ds(index, 1), lanes] = new_top
                 decay = jnp.exp2(top - new_top)
                 following.append(
                     (
@@ -196,6 +195,7 @@
                         mixed * decay + jnp.sum(terms * dweights, axis=0, keepdims=True),
                     )
                 )
+            tops_ref[pl.ds(index, 1), :] = jnp.concatenate([top for top, _, _ in following], axis=1)
             return tuple(following)
 
         zero = jnp.zeros((1, group), jnp.float32)

time: 44.2 us -> 43.6 us (0.986); the launches traced: 44.2 us -> 44.1 us
  no operation moved by 1% of the time
where the time goes in v10:
time: 43.6 us; the launch traced here: 44.1 us
  starting transfers between devices  20 us (46%)
  waiting for transfers between devices  17.1 us (39%)
  Pallas kernels  4.59 us (11%)
  other arithmetic  1.04 us (2%)
  between operations  0.71 us (2%)
  local copies, waits for them, and re-layouts  0.63 us (1%)
    ppermute x18, waiting for transfers between devices, swap(): return lax.ppermute(value, axis, pairs)  17.1 us
    ppermute x18, starting transfers between devices, swap(): return lax.ppermute(value, axis, pairs)  17 us
    ppermute x1, starting transfers between devices, paired_line(): whole = lax.ppermute(own, ('ctx', 'dp'), pairs)  3.08 us
    pallas_call x1, Pallas kernels, attend(): pl.pallas_call(functools.partial(attend_kernel, ctx_count, dp_count, inne...  1.83 us
    pallas_call x1, Pallas kernels, query_side(): pl.pallas_call(functools.partial(query_kernel, ctx_count, tile), out_shap...  1.5 us
    pallas_call x1, Pallas kernels, prepare(): pl.pallas_call(functools.partial(prepare_kernel, ctx_count, tile), out_sh...  1.25 us
  transfers between devices with their start and end apart: 19, of which 11 were waited for; matrix products, arithmetic and copies ran while one was open for 0% of the time, Pallas kernels for 6%

profile of v10, /device:TPU:0, one launch (start us, length us, event | category | flops | bytes accessed | tf_op | source)
XLA Modules:
  0.0 44.1 jit_solution(12439099966022775559)
XLA Ops:
  0.6 0.8 %pad_maximum_fusion.1 = bf16[2,2,64,128]{3,2,1,0:T(8,128)(2,1)S(1)} fusion(bf16[2,1,64,128]{3,2,1,0:T(8,128)(2,1)} %bitcast.9, bf16[2,1,64,128]{3,2,1,0:T(8,128)(2,1)} %bitcast.10), kind=kLoop, calls=%fused_computation.7 | loop fusion | flops 32768 | bytes 131072 | tf_op jit(solution)/shard_map/max | solution.py:381
  1.4 3.1 %collective-permute-start.1 = (bf16[256,128]{1,0:T(8,128)(2,1)S(1)}, bf16[256,128]{1,0:T(8,128)(2,1)S(1)}, u32[]{:S(2)}, u32[]{:S(2)}) collective-permute-start(bf16[256,128]{1,0:T(8,128)(2,1)S(1)} %bitcast.7), channel_id=1, source_target_pairs={{0,8},{1,25},{2,10},{3,27},{4,12},{5,29},{6,14},{7,31},{8,0},{9,17... | collective-permute-start | bytes 196616 | tf_op jit(solution)/shard_map/ppermute | solution.py:392
  4.5 2.6 %collective-permute-start = (bf16[128,128]{1,0:T(8,128)(2,1)S(1)}, bf16[128,128]{1,0:T(8,128)(2,1)S(1)}, u32[]{:S(2)}, u32[]{:S(2)}) collective-permute-start(bf16[128,128]{1,0:T(8,128)(2,1)S(1)} %constant_dynamic-slice_fusion), channel_id=1, source_target_pairs={{0,16},{2,18},{4,20},{6,22},{8,24},{10,26},{12,28},{14,30},{16,0},... | collective-permute-start | bytes 98312 | tf_op jit(solution)/shard_map/ppermute | solution.py:354
  7.1 2.4 %collective-permute-done = bf16[128,128]{1,0:T(8,128)(2,1)S(1)} collective-permute-done((bf16[128,128]{1,0:T(8,128)(2,1)S(1)}, bf16[128,128]{1,0:T(8,128)(2,1)S(1)}, u32[]{:S(2)}, u32[]{:S(2)}) %collective-permute-start) | collective-permute-done | bytes 32800 | tf_op jit(solution)/shard_map/ppermute | solution.py:354
  9.5 2.5 %collective-permute-start.4 = (bf16[512,128]{1,0:T(8,128)(2,1)S(1)}, bf16[512,128]{1,0:T(8,128)(2,1)S(1)}, u32[]{:S(2)}, u32[]{:S(2)}) collective-permute-start(bf16[512,128]{1,0:T(8,128)(2,1)S(1)} %pad_maximum_fusion.line_ref), channel_id=1, source_target_pairs={{0,6},{2,4},{4,2},{6,0},{8,14},{10,12},{12,10},{14,8},{16,22},{18,... | collective-permute-start | bytes 393224 | tf_op jit(solution)/shard_map/ppermute | solution.py:354
  12.0 0.5 %collective-permute-start.3 = (bf16[512,128]{1,0:T(8,128)(2,1)S(1)}, bf16[512,128]{1,0:T(8,128)(2,1)S(1)}, u32[]{:S(2)}, u32[]{:S(2)}) collective-permute-start(bf16[512,128]{1,0:T(8,128)(2,1)S(1)} %pad_maximum_fusion.line_ref), channel_id=1, source_target_pairs={{0,4},{2,6},{4,0},{6,2},{8,12},{10,14},{12,8},{14,10},{16,20},{18,... | collective-permute-start | bytes 393224 | tf_op jit(solution)/shard_map/ppermute | solution.py:354
  12.5 0.5 %collective-permute-start.2 = (bf16[512,128]{1,0:T(8,128)(2,1)S(1)}, bf16[512,128]{1,0:T(8,128)(2,1)S(1)}, u32[]{:S(2)}, u32[]{:S(2)}) collective-permute-start(bf16[512,128]{1,0:T(8,128)(2,1)S(1)} %pad_maximum_fusion.line_ref), channel_id=1, source_target_pairs={{0,2},{2,0},{4,6},{6,4},{8,10},{10,8},{12,14},{14,12},{16,18},{18,... | collective-permute-start | bytes 393224 | tf_op jit(solution)/shard_map/ppermute | solution.py:354
  13.0 1.3 %shard_map.76 = (bf16[2,2,512,128]{3,2,1,0:T(8,128)(2,1)S(1)}, bf16[2,2,128,512]{3,2,1,0:T(8,128)(2,1)S(1)}, s32[2,1,512]{2,1,0:T(1,128)S(1)}, f32[2,8,128]{2,1,...) custom-call(s32[8]{0:T(128)} %lengths_hbm.1, bf16[128,1024]{1,0:T(8,128)(2,1)} %q_hbm.1, ...), custom_call_target="tpu_custom_call" | custom-call | tf_op jit(solution)/shard_map/pallas_call | solution.py:283
  14.4 2.3 %collective-permute-done.4.refs_3_ = bf16[512,128]{1,0:T(8,128)(2,1)S(1)} collective-permute-done((bf16[512,128]{1,0:T(8,128)(2,1)S(1)}, bf16[512,128]{1,0:T(8,128)(2,1)S(1)}, u32[]{:S(2)}, u32[]{:S(2)}) %collective-permute-start.4) | collective-permute-done | bytes 131104 | tf_op jit(solution)/shard_map/ppermute | solution.py:354
  16.7 2.6 %collective-permute-done.3.refs_2_ = bf16[512,128]{1,0:T(8,128)(2,1)S(1)} collective-permute-done((bf16[512,128]{1,0:T(8,128)(2,1)S(1)}, bf16[512,128]{1,0:T(8,128)(2,1)S(1)}, u32[]{:S(2)}, u32[]{:S(2)}) %collective-permute-start.3) | collective-permute-done | bytes 131104 | tf_op jit(solution)/shard_map/ppermute | solution.py:354
  19.4 0.4 collective-permute-start.6
  19.8 0.8 %collective-permute-done.7.refs_6_ = bf16[512,128]{1,0:T(8,128)(2,1)S(1)} collective-permute-done((bf16[512,128]{1,0:T(8,128)(2,1)S(1)}, bf16[512,128]{1,0:T(8,128)(2,1)S(1)}, u32[]{:S(2)}, u32[]{:S(2)}) %collective-permute-start.7) | collective-permute-done | bytes 131104 | tf_op jit(solution)/shard_map/ppermute | solution.py:354
  20.8 1.8 %shard_map.77 = (bf16[2304,128]{1,0:T(8,128)(2,1)S(1)}, bf16[2,4,2048,128]{3,2,1,0:T(8,128)(2,1)S(1)}, f32[2,2304,128]{2,1,0:T(8,128)S(1)}, bf16[512,128]{1,0:T(...) custom-call(f32[2,8,128]{2,1,0:T(8,128)S(1)} %get-tuple-element.21.t, ...), custom_call_target="tpu_custom_call", output_to_operand_aliasing={{2}: (4, {})} | custom-call | tf_op jit(solution)/shard_map/pallas_call | solution.py:308
  24.1 1.8 %collective-permute-start.11 = (bf16[512,128]{1,0:T(8,128)(2,1)S(1)}, bf16[512,128]{1,0:T(8,128)(2,1)S(1)}, u32[]{:S(2)}, u32[]{:S(2)}) collective-permute-start(bf16[512,128]{1,0:T(8,128)(2,1)S(1)} %add_convert_fusion.3), channel_id=1, source_target_pairs={{0,6},{2,4},{4,2},{6,0},{8,14},{10,12},{12,10},{14,8},{16,22},{18,... | collective-permute-start | bytes 393224 | tf_op jit(solution)/shard_map/ppermute | solution.py:354
  26.0 1.3 %collective-permute-start.13 = (bf16[512,128]{1,0:T(8,128)(2,1)S(1)}, bf16[512,128]{1,0:T(8,128)(2,1)S(1)}, u32[]{:S(2)}, u32[]{:S(2)}) collective-permute-start(bf16[512,128]{1,0:T(8,128)(2,1)S(1)} %add_convert_fusion.2), channel_id=1, source_target_pairs={{0,4},{2,6},{4,0},{6,2},{8,12},{10,14},{12,8},{14,10},{16,20},{18,... | collective-permute-start | bytes 393224 | tf_op jit(solution)/shard_map/ppermute | solution.py:354
  27.3 0.6 %collective-permute-start.15 = (bf16[512,128]{1,0:T(8,128)(2,1)S(1)}, bf16[512,128]{1,0:T(8,128)(2,1)S(1)}, u32[]{:S(2)}, u32[]{:S(2)}) collective-permute-start(bf16[512,128]{1,0:T(8,128)(2,1)S(1)} %add_convert_fusion.1), channel_id=1, source_target_pairs={{0,2},{2,0},{4,6},{6,4},{8,10},{10,8},{12,14},{14,12},{16,18},{18,... | collective-permute-start | bytes 393224 | tf_op jit(solution)/shard_map/ppermute | solution.py:354
  27.9 1.5 %shard_map.78 = (bf16[128,1024]{1,0:T(8,128)(2,1)}, bf16[512,128]{1,0:T(8,128)(2,1)S(1)}) custom-call(f32[2,8,128]{2,1,0:T(8,128)S(1)} %get-tuple-element.21.tiles_ref, bf16[2304,128]{1,0:T(8,128)(2,1)S(1)} %get-tuple-element.27.keys_ref, bf16[2,4,2048,128]{3,2,1,0:T(8,128)(2,1)S(1)} %get-tuple-element.28.dlogits_ref, ...), custom_call_target="tpu_custom_call" | custom-call | tf_op jit(solution)/shard_map/pallas_call | solution.py:335
  29.4 2.0 %collective-permute-done.11 = bf16[512,128]{1,0:T(8,128)(2,1)S(1)} collective-permute-done((bf16[512,128]{1,0:T(8,128)(2,1)S(1)}, bf16[512,128]{1,0:T(8,128)(2,1)S(1)}, u32[]{:S(2)}, u32[]{:S(2)}) %collective-permute-start.11) | collective-permute-done | bytes 131104 | tf_op jit(solution)/shard_map/ppermute | solution.py:354
  31.4 2.2 %collective-permute-done.13 = bf16[512,128]{1,0:T(8,128)(2,1)S(1)} collective-permute-done((bf16[512,128]{1,0:T(8,128)(2,1)S(1)}, bf16[512,128]{1,0:T(8,128)(2,1)S(1)}, u32[]{:S(2)}, u32[]{:S(2)}) %collective-permute-start.13) | collective-permute-done | bytes 131104 | tf_op jit(solution)/shard_map/ppermute | solution.py:354
  33.8 4.9 %collective-permute-start.16 = (bf16[128,128]{1,0:T(8,128)(2,1)S(1)}, bf16[128,128]{1,0:T(8,128)(2,1)S(1)}, u32[]{:S(2)}, u32[]{:S(2)}) collective-permute-start(bf16[128,128]{1,0:T(8,128)(2,1)S(1)} %get-tuple-element.39), channel_id=1, source_target_pairs={{0,24},{2,26},{4,28},{6,30},{8,16},{10,18},{12,20},{14,22},{16,8},... | collective-permute-start | bytes 98312 | tf_op jit(solution)/shard_map/ppermute | solution.py:354
  38.7 0.6 %collective-permute-start.17 = (bf16[128,128]{1,0:T(8,128)(2,1)S(1)}, bf16[128,128]{1,0:T(8,128)(2,1)S(1)}, u32[]{:S(2)}, u32[]{:S(2)}) collective-permute-start(bf16[128,128]{1,0:T(8,128)(2,1)S(1)} %get-tuple-element.41), channel_id=1, source_target_pairs={{0,8},{2,10},{4,12},{6,14},{8,0},{10,2},{12,4},{14,6},{16,24},{18,... | collective-permute-start | bytes 98312 | tf_op jit(solution)/shard_map/ppermute | solution.py:354
  39.3 1.3 %collective-permute-done.16 = bf16[128,128]{1,0:T(8,128)(2,1)S(1)} collective-permute-done((bf16[128,128]{1,0:T(8,128)(2,1)S(1)}, bf16[128,128]{1,0:T(8,128)(2,1)S(1)}, u32[]{:S(2)}, u32[]{:S(2)}) %collective-permute-start.16) | collective-permute-done | bytes 32800 | tf_op jit(solution)/shard_map/ppermute | solution.py:354
  40.6 2.9 %collective-permute-done.18 = bf16[128,128]{1,0:T(8,128)(2,1)S(1)} collective-permute-done((bf16[128,128]{1,0:T(8,128)(2,1)S(1)}, bf16[128,128]{1,0:T(8,128)(2,1)S(1)}, u32[]{:S(2)}, u32[]{:S(2)}) %collective-permute-start.18) | collective-permute-done | bytes 32800 | tf_op jit(solution)/shard_map/ppermute | solution.py:354
  43.5 0.6 %fusion.1 = (bf16[64,128]{1,0:T(8,128)(2,1)}, bf16[64,128]{1,0:T(8,128)(2,1)}) fusion(bf16[128,128]{1,0:T(8,128)(2,1)S(1)} %add_convert_fusion.5), kind=kLoop, calls=%fused_computation.10 | loop fusion | bytes 65536 | tf_op jit(solution)/shard_map/slice | solution.py:437
  (28 shorter events, 2.2 us)
Async XLA Ops:
  1.4 8.1 %collective-permute-start.1 = (bf16[256,128]{1,0:T(8,128)(2,1)S(1)}, bf16[256,128]{1,0:T(8,128)(2,1)S(1)}, u32[]{:S(2)}, u32[]{:S(2)}) collective-permute-start(bf16[256,128]{1,0:T(8,128)(2,1)S(1)} %bitcast.7), channel_id=1, source_target_pairs={{0,8},{1,25},{2,10},{3,27},{4,12},{5,29},{6,14},{7,31},{8,0},{9,17... | collective-permute-start | bytes 196616 | tf_op jit(solution)/shard_map/ppermute | solution.py:392
  4.5 5.0 %collective-permute-start = (bf16[128,128]{1,0:T(8,128)(2,1)S(1)}, bf16[128,128]{1,0:T(8,128)(2,1)S(1)}, u32[]{:S(2)}, u32[]{:S(2)}) collective-permute-start(bf16[128,128]{1,0:T(8,128)(2,1)S(1)} %constant_dynamic-slice_fusion), channel_id=1, source_target_pairs={{0,16},{2,18},{4,20},{6,22},{8,24},{10,26},{12,28},{14,30},{16,0},... | collective-permute-start | bytes 98312 | tf_op jit(solution)/shard_map/ppermute | solution.py:354
  9.5 7.2 %collective-permute-start.4 = (bf16[512,128]{1,0:T(8,128)(2,1)S(1)}, bf16[512,128]{1,0:T(8,128)(2,1)S(1)}, u32[]{:S(2)}, u32[]{:S(2)}) collective-permute-start(bf16[512,128]{1,0:T(8,128)(2,1)S(1)} %pad_maximum_fusion.line_ref), channel_id=1, source_target_pairs={{0,6},{2,4},{4,2},{6,0},{8,14},{10,12},{12,10},{14,8},{16,22},{18,... | collective-permute-start | bytes 393224 | tf_op jit(solution)/shard_map/ppermute | solution.py:354
  12.0 7.3 %collective-permute-start.3 = (bf16[512,128]{1,0:T(8,128)(2,1)S(1)}, bf16[512,128]{1,0:T(8,128)(2,1)S(1)}, u32[]{:S(2)}, u32[]{:S(2)}) collective-permute-start(bf16[512,128]{1,0:T(8,128)(2,1)S(1)} %pad_maximum_fusion.line_ref), channel_id=1, source_target_pairs={{0,4},{2,6},{4,0},{6,2},{8,12},{10,14},{12,8},{14,10},{16,20},{18,... | collective-permute-start | bytes 393224 | tf_op jit(solution)/shard_map/ppermute | solution.py:354
  12.5 6.9 %collective-permute-start.2 = (bf16[512,128]{1,0:T(8,128)(2,1)S(1)}, bf16[512,128]{1,0:T(8,128)(2,1)S(1)}, u32[]{:S(2)}, u32[]{:S(2)}) collective-permute-start(bf16[512,128]{1,0:T(8,128)(2,1)S(1)} %pad_maximum_fusion.line_ref), channel_id=1, source_target_pairs={{0,2},{2,0},{4,6},{6,4},{8,10},{10,8},{12,14},{14,12},{16,18},{18,... | collective-permute-start | bytes 393224 | tf_op jit(solution)/shard_map/ppermute | solution.py:354
  14.3 5.5 %collective-permute-start.5 = (bf16[512,128]{1,0:T(8,128)(2,1)S(1)}, bf16[512,128]{1,0:T(8,128)(2,1)S(1)}, u32[]{:S(2)}, u32[]{:S(2)}) collective-permute-start(bf16[512,128]{1,0:T(8,128)(2,1)S(1)} %get-tuple-element.26.refs_0_), channel_id=1, source_target_pairs={{0,1},{1,0},{2,3},{3,2},{4,5},{5,4},{6,7},{7,6},{8,9},{9,8},{10,11... | collective-permute-start | bytes 393224 | tf_op jit(solution)/shard_map/ppermute | solution.py:354
  16.7 3.1 %collective-permute-start.8 = (bf16[512,128]{1,0:T(8,128)(2,1)S(1)}, bf16[512,128]{1,0:T(8,128)(2,1)S(1)}, u32[]{:S(2)}, u32[]{:S(2)}) collective-permute-start(bf16[512,128]{1,0:T(8,128)(2,1)S(1)} %collective-permute-done.4.refs_3_), channel_id=1, source_target_pairs={{0,1},{1,0},{2,3},{3,2},{4,5},{5,4},{6,7},{7,6},{8,9},{9,8},{10,11... | collective-permute-start | bytes 393224 | tf_op jit(solution)/shard_map/ppermute | solution.py:354
  19.3 1.3 %collective-permute-start.7 = (bf16[512,128]{1,0:T(8,128)(2,1)S(1)}, bf16[512,128]{1,0:T(8,128)(2,1)S(1)}, u32[]{:S(2)}, u32[]{:S(2)}) collective-permute-start(bf16[512,128]{1,0:T(8,128)(2,1)S(1)} %collective-permute-done.3.refs_2_), channel_id=1, source_target_pairs={{0,1},{1,0},{2,3},{3,2},{4,5},{5,4},{6,7},{7,6},{8,9},{9,8},{10,11... | collective-permute-start | bytes 393224 | tf_op jit(solution)/shard_map/ppermute | solution.py:354
  19.4 1.4 %collective-permute-start.6 = (bf16[512,128]{1,0:T(8,128)(2,1)S(1)}, bf16[512,128]{1,0:T(8,128)(2,1)S(1)}, u32[]{:S(2)}, u32[]{:S(2)}) collective-permute-start(bf16[512,128]{1,0:T(8,128)(2,1)S(1)} %collective-permute-done.2.refs_1_), channel_id=1, source_target_pairs={{0,1},{1,0},{2,3},{3,2},{4,5},{5,4},{6,7},{7,6},{8,9},{9,8},{10,11... | collective-permute-start | bytes 393224 | tf_op jit(solution)/shard_map/ppermute | solution.py:354
  22.7 1.4 %collective-permute-start.10 = (bf16[512,128]{1,0:T(8,128)(2,1)S(1)}, bf16[512,128]{1,0:T(8,128)(2,1)S(1)}, u32[]{:S(2)}, u32[]{:S(2)}) collective-permute-start(bf16[512,128]{1,0:T(8,128)(2,1)S(1)} %get-tuple-element.34), channel_id=1, source_target_pairs={{0,1},{1,0},{2,3},{3,2},{4,5},{5,4},{6,7},{7,6},{8,9},{9,8},{10,11... | collective-permute-start | bytes 393224 | tf_op jit(solution)/shard_map/ppermute | solution.py:354
  23.1 4.8 %collective-permute-start.9 = (bf16[512,128]{1,0:T(8,128)(2,1)S(1)}, bf16[512,128]{1,0:T(8,128)(2,1)S(1)}, u32[]{:S(2)}, u32[]{:S(2)}) collective-permute-start(bf16[512,128]{1,0:T(8,128)(2,1)S(1)} %get-tuple-element.30), channel_id=1, source_target_pairs={{0,1},{1,0},{2,3},{3,2},{4,5},{5,4},{6,7},{7,6},{8,9},{9,8},{10,11... | collective-permute-start | bytes 393224 | tf_op jit(solution)/shard_map/ppermute | solution.py:354
  23.2 2.7 %collective-permute-start.12 = (bf16[512,128]{1,0:T(8,128)(2,1)S(1)}, bf16[512,128]{1,0:T(8,128)(2,1)S(1)}, u32[]{:S(2)}, u32[]{:S(2)}) collective-permute-start(bf16[512,128]{1,0:T(8,128)(2,1)S(1)} %get-tuple-element.36), channel_id=1, source_target_pairs={{0,1},{1,0},{2,3},{3,2},{4,5},{5,4},{6,7},{7,6},{8,9},{9,8},{10,11... | collective-permute-start | bytes 393224 | tf_op jit(solution)/shard_map/ppermute | solution.py:354
  23.6 3.7 %collective-permute-start.14 = (bf16[512,128]{1,0:T(8,128)(2,1)S(1)}, bf16[512,128]{1,0:T(8,128)(2,1)S(1)}, u32[]{:S(2)}, u32[]{:S(2)}) collective-permute-start(bf16[512,128]{1,0:T(8,128)(2,1)S(1)} %get-tuple-element.38), channel_id=1, source_target_pairs={{0,1},{1,0},{2,3},{3,2},{4,5},{5,4},{6,7},{7,6},{8,9},{9,8},{10,11... | collective-permute-start | bytes 393224 | tf_op jit(solution)/shard_map/ppermute | solution.py:354
  24.1 7.3 %collective-permute-start.11 = (bf16[512,128]{1,0:T(8,128)(2,1)S(1)}, bf16[512,128]{1,0:T(8,128)(2,1)S(1)}, u32[]{:S(2)}, u32[]{:S(2)}) collective-permute-start(bf16[512,128]{1,0:T(8,128)(2,1)S(1)} %add_convert_fusion.3), channel_id=1, source_target_pairs={{0,6},{2,4},{4,2},{6,0},{8,14},{10,12},{12,10},{14,8},{16,22},{18,... | collective-permute-start | bytes 393224 | tf_op jit(solution)/shard_map/ppermute | solution.py:354
  26.0 7.6 %collective-permute-start.13 = (bf16[512,128]{1,0:T(8,128)(2,1)S(1)}, bf16[512,128]{1,0:T(8,128)(2,1)S(1)}, u32[]{:S(2)}, u32[]{:S(2)}) collective-permute-start(bf16[512,128]{1,0:T(8,128)(2,1)S(1)} %add_convert_fusion.2), channel_id=1, source_target_pairs={{0,4},{2,6},{4,0},{6,2},{8,12},{10,14},{12,8},{14,10},{16,20},{18,... | collective-permute-start | bytes 393224 | tf_op jit(solution)/shard_map/ppermute | solution.py:354
  27.3 6.4 %collective-permute-start.15 = (bf16[512,128]{1,0:T(8,128)(2,1)S(1)}, bf16[512,128]{1,0:T(8,128)(2,1)S(1)}, u32[]{:S(2)}, u32[]{:S(2)}) collective-permute-start(bf16[512,128]{1,0:T(8,128)(2,1)S(1)} %add_convert_fusion.1), channel_id=1, source_target_pairs={{0,2},{2,0},{4,6},{6,4},{8,10},{10,8},{12,14},{14,12},{16,18},{18,... | collective-permute-start | bytes 393224 | tf_op jit(solution)/shard_map/ppermute | solution.py:354
  33.8 6.8 %collective-permute-start.16 = (bf16[128,128]{1,0:T(8,128)(2,1)S(1)}, bf16[128,128]{1,0:T(8,128)(2,1)S(1)}, u32[]{:S(2)}, u32[]{:S(2)}) collective-permute-start(bf16[128,128]{1,0:T(8,128)(2,1)S(1)} %get-tuple-element.39), channel_id=1, source_target_pairs={{0,24},{2,26},{4,28},{6,30},{8,16},{10,18},{12,20},{14,22},{16,8},... | collective-permute-start | bytes 98312 | tf_op jit(solution)/shard_map/ppermute | solution.py:354
  38.7 4.8 %collective-permute-start.18 = (bf16[128,128]{1,0:T(8,128)(2,1)S(1)}, bf16[128,128]{1,0:T(8,128)(2,1)S(1)}, u32[]{:S(2)}, u32[]{:S(2)}) collective-permute-start(bf16[128,128]{1,0:T(8,128)(2,1)S(1)} %get-tuple-element.40), channel_id=1, source_target_pairs={{0,16},{2,18},{4,20},{6,22},{8,24},{10,26},{12,28},{14,30},{16,0},... | collective-permute-start | bytes 98312 | tf_op jit(solution)/shard_map/ppermute | solution.py:354
  38.7 4.8 %collective-permute-start.17 = (bf16[128,128]{1,0:T(8,128)(2,1)S(1)}, bf16[128,128]{1,0:T(8,128)(2,1)S(1)}, u32[]{:S(2)}, u32[]{:S(2)}) collective-permute-start(bf16[128,128]{1,0:T(8,128)(2,1)S(1)} %get-tuple-element.41), channel_id=1, source_target_pairs={{0,8},{2,10},{4,12},{6,14},{8,0},{10,2},{12,4},{14,6},{16,24},{18,... | collective-permute-start | bytes 98312 | tf_op jit(solution)/shard_map/ppermute | solution.py:354
